TPU v7x, 128 devices: a whole 4x4x4 slice. The times are simulated.
128 devices in a mesh: gx: 8 (over x, y_lo), gy: 16 (over y_hi, z, core).
Axes of the slice: x: 4, y: 4 (y_hi: 2, y_lo: 2; y = y_hi * 2 + y_lo), z: 4, core: 2. Of those that a mesh axis runs over, the one named last changes fastest.
Arguments:
- fields: float32 [4, 128, 128, 2048], P(None, None, 'gx', 'gy'), may hold values from -6 to 6
- courant: float32 [2, 128, 128, 2048], P(None, None, 'gx', 'gy'), may hold values from -0.3 to 0.3
- sun_columns: int32 [8, 16, 2048], P('gx', 'gy'), may hold values from -1 to 2047, as said below
- rad_w1: bfloat16 [512, 1024], replicated, may hold values from -0.25 to 0.25
- rad_b1: float32 [1024], replicated, may hold values from -3 to 3
- rad_w2: bfloat16 [1024, 1024], replicated, may hold values from -0.1875 to 0.1875
- rad_b2: float32 [1024], replicated, may hold values from -3 to 3
- rad_w3: bfloat16 [1024, 512], replicated, may hold values from -0.1875 to 0.1875
- segment_route: int32 [2, 8, 16, 1024], P(None, 'gx', 'gy'), may hold values from 0 to 1023, as said below
- regrid_weights: bfloat16 [8, 16, 16, 128, 128], P('gx', 'gy'), may hold values from 0 to 1, as said below
- chem_w1: bfloat16 [256, 1024], replicated, may hold values from -0.375 to 0.375
- chem_b1: float32 [1024], replicated, may hold values from -3 to 3
- chem_w2: bfloat16 [1024, 256], replicated, may hold values from -0.1875 to 0.1875
Outputs:
- fields_out: float32 [4, 128, 128, 2048], P(None, None, 'gx', 'gy')
- chem_tendency: bfloat16 [8, 16, 2048, 256], P('gx', 'gy')
Inputs may be any that keep to these rules, and one draw needn't show every extreme that they name: `sun_columns`: in each tile the live entries come first and are distinct columns of the tile; the rest are -1. Counting a tile's sunlit blocks as its live entries divided by 128, rounded up, a tile and the tile with the same first index and second index 8 further (modulo 16) have exactly 16 sunlit blocks together. `segment_route`: entry 0 is the receiving tile, entry 1 the slot there. Every tile receives exactly 1024 segments, one in each slot; no tile receives more than 16 segments from one tile, and some tile receives exactly 16 from one tile. `regrid_weights`: entries are nonnegative and each row sums to one up to rounding.
All inputs are finite; a program needn't handle non-finite values.
Results may differ from a plain program's by a relative error of at most 0.0075.
Values may be sent and summed in bfloat16 or wider, within the bound.
No kernel may reach another device: no remote copies, remote signals or barrier semaphores. Data moves between devices by JAX's collectives and lax.ppermute only.
A program may use at most 128 MiB of HBM per device.

v0:
```python
import jax
import jax.numpy as jnp
from jax import lax
from jax.experimental import pallas as pl
from jax.experimental.pallas import tpu as pltpu
from jax.sharding import PartitionSpec as P

F32 = jnp.float32
BF16 = jnp.bfloat16
LANES = 128
FIELDS = 4
ROWS = 16
COLS = 128
FEAT = FIELDS * LANES
CELLS = ROWS * COLS
SEGS = CELLS // 2
EDGE = 8
INNER = COLS - 2 * EDGE
GROUP = 2
RIM = 2 * COLS + (ROWS - 2) * 2 * EDGE
VMEM_LIMIT = 20 * 1024 * 1024

VMEM = pl.BlockSpec(memory_space=pltpu.VMEM)
SMEM = pl.BlockSpec(memory_space=pltpu.SMEM)
ANY = pl.BlockSpec(memory_space=pl.ANY)


def vmem_out(shape, dtype):
    return pltpu.VMEM(shape, dtype)


def params():
    return pltpu.CompilerParams(vmem_limit_bytes=VMEM_LIMIT)


def cost(flops, bytes_accessed=0):
    return pl.CostEstimate(flops=flops, bytes_accessed=bytes_accessed, transcendentals=0)


def dot(a, b):
    return jnp.dot(a, b, preferred_element_type=F32)


def dot_nt(a, b):
    return lax.dot_general(a, b, (((1,), (1,)), ((), ())), preferred_element_type=F32)


def silu(u):
    half = 0.5 * u
    return half + half * jnp.tanh(half)


def iota(shape, dim):
    return lax.broadcasted_iota(jnp.int32, shape, dim)


def turn_kernel(f_ref, c_ref, t_ref, cc_ref, row_lo_ref, row_hi_ref, col_lo_ref, col_hi_ref):
    step = pl.program_id(0)

    @pl.when(step < FIELDS)
    def _():
        for r in range(ROWS):
            block = f_ref[pl.ds(r, LANES, stride=ROWS), :].T
            t_ref[0, r] = block
            if r == 0:
                row_lo_ref[...] = block.astype(BF16)
            if r == ROWS - 1:
                row_hi_ref[...] = block.astype(BF16)
        col_lo_ref[...] = t_ref[0, :, 0, :].astype(BF16)
        col_hi_ref[...] = t_ref[0, :, COLS - 1, :].astype(BF16)

    @pl.when(step >= FIELDS)
    def _():
        for r in range(ROWS):
            cc_ref[0, r] = c_ref[pl.ds(r, LANES, stride=ROWS), :].T

    @pl.when(step == FIELDS)
    def _():
        row_lo_ref[...] = cc_ref[0, 0].astype(BF16)
        row_hi_ref[...] = cc_ref[0, ROWS - 1].astype(BF16)

    @pl.when(step == FIELDS + 1)
    def _():
        col_lo_ref[...] = cc_ref[0, :, 0, :].astype(BF16)
        col_hi_ref[...] = cc_ref[0, :, COLS - 1, :].astype(BF16)


def turn(fields, courant):
    flat_f = fields.reshape(FIELDS * LANES * ROWS, COLS)
    flat_c = courant.reshape(2 * LANES * ROWS, COLS)
    field_at = lambda i: jnp.minimum(i, FIELDS - 1)
    speed_at = lambda i: jnp.maximum(i - FIELDS, 0)
    halo_at = lambda i: jnp.minimum(i, FIELDS)
    return pl.pallas_call(
        turn_kernel,
        grid=(FIELDS + 2,),
        in_specs=[
            pl.BlockSpec((LANES * ROWS, COLS), lambda i: (field_at(i), 0)),
            pl.BlockSpec((LANES * ROWS, COLS), lambda i: (speed_at(i), 0)),
        ],
        out_specs=[
            pl.BlockSpec((1, ROWS, COLS, LANES), lambda i: (field_at(i), 0, 0, 0)),
            pl.BlockSpec((1, ROWS, COLS, LANES), lambda i: (speed_at(i), 0, 0, 0)),
            pl.BlockSpec((COLS, LANES), lambda i: (0, halo_at(i))),
            pl.BlockSpec((COLS, LANES), lambda i: (0, halo_at(i))),
            pl.BlockSpec((ROWS, LANES), lambda i: (0, halo_at(i))),
            pl.BlockSpec((ROWS, LANES), lambda i: (0, halo_at(i))),
        ],
        out_shape=[
            jax.ShapeDtypeStruct((FIELDS, ROWS, COLS, LANES), F32),
            jax.ShapeDtypeStruct((2, ROWS, COLS, LANES), F32),
            jax.ShapeDtypeStruct((COLS, FEAT + LANES), BF16),
            jax.ShapeDtypeStruct((COLS, FEAT + LANES), BF16),
            jax.ShapeDtypeStruct((ROWS, FEAT + LANES), BF16),
            jax.ShapeDtypeStruct((ROWS, FEAT + LANES), BF16),
        ],
        compiler_params=params(),
        cost_estimate=cost(20_000_000, 12 << 20),
        name="turn",
    )(flat_f, flat_c)


def plan_kernel(sun_ref, route_ref, regrid_ref, mask_ref, place_ref, tags_ref, mix_ref):
    slots = sun_ref[...]
    low = (iota((COLS, CELLS), 0) == (slots & (COLS - 1))).astype(F32).astype(BF16)
    high = (iota((LANES, CELLS), 0) == (slots >> 7)).astype(F32).astype(BF16)
    lit = dot_nt(low, high)
    for r in range(ROWS):
        mask_ref[r] = jnp.broadcast_to(lit[:, r : r + 1], (COLS, LANES))

    target = route_ref[0:1, :]
    arrival = route_ref[1:2, :] + 1
    before = (iota((LANES, LANES), 0) < iota((LANES, LANES), 1)).astype(F32).astype(BF16)
    ones = jnp.ones((LANES, LANES), BF16)
    carry = jnp.zeros((LANES, LANES), F32)
    ranks = []
    for b in range(SEGS // LANES):
        goes = (iota((LANES, LANES), 0) == target[:, b * LANES : (b + 1) * LANES]).astype(F32)
        goes16 = goes.astype(BF16)
        ranks.append(jnp.sum(goes * (dot(goes16, before) + carry), axis=0, keepdims=True))
        carry = carry + dot(goes16, ones)
    rank = jnp.concatenate(ranks, axis=1).astype(jnp.int32)
    row = target * 16 + rank
    index = iota((LANES, SEGS), 0)
    coarse = (arrival >> 5).astype(F32)
    fine = (arrival & 31).astype(F32)
    tag_rows = [
        jnp.where(index == 2 * q, coarse, jnp.where(index == 2 * q + 1, fine, 0.0)).astype(BF16)
        for q in range(2)
    ]
    for b in range(SEGS // LANES):
        tags = jnp.zeros((LANES, LANES), F32)
        for q in range(2):
            want = 2 * (iota((LANES, SEGS), 0) + b * LANES) + q
            chosen = (row == want).astype(F32).astype(BF16)
            place_ref[q, b * LANES : (b + 1) * LANES, :] = chosen
            tags = tags + dot_nt(chosen, tag_rows[q])
        tags_ref[b * LANES : (b + 1) * LANES, :] = tags.astype(BF16)

    from_cell = iota((LANES, LANES), 0)
    to_lane = iota((LANES, LANES), 1)
    source_cell = jnp.where(to_lane < 64, 2 * to_lane, 2 * (to_lane - 64) + 1)
    split = (from_cell == source_cell).astype(F32).astype(BF16)
    mix_ref[...] = dot(regrid_ref[...], split).astype(BF16)


def plan(sun_columns, segment_route, regrid_weights):
    return pl.pallas_call(
        plan_kernel,
        in_specs=[VMEM] * 3,
        out_specs=[VMEM] * 4,
        out_shape=[
            vmem_out((ROWS, COLS, LANES), F32),
            vmem_out((2, SEGS, SEGS), BF16),
            vmem_out((SEGS, LANES), BF16),
            vmem_out((CELLS, LANES), BF16),
        ],
        compiler_params=params(),
        cost_estimate=cost(3_000_000_000, 1 << 20),
        name="plan",
    )(
        sun_columns.reshape(1, CELLS),
        segment_route.reshape(2, SEGS),
        regrid_weights.reshape(CELLS, LANES),
    )


def weights_of(lo0, mid0, hi0, left1, mid1, right1, valid_lo=None, valid_hi=None):
    f_lo = 0.5 * (lo0 + mid0)
    f_hi = 0.5 * (mid0 + hi0)
    if valid_lo is not None:
        f_lo = f_lo * valid_lo
    if valid_hi is not None:
        f_hi = f_hi * valid_hi
    g_lo = 0.5 * (left1 + mid1)
    g_hi = 0.5 * (mid1 + right1)
    keep = (
        1.0
        - jnp.maximum(f_hi, 0.0)
        + jnp.minimum(f_lo, 0.0)
        - jnp.maximum(g_hi, 0.0)
        + jnp.minimum(g_lo, 0.0)
    )
    return (
        keep,
        jnp.maximum(f_lo, 0.0),
        -jnp.minimum(f_hi, 0.0),
        jnp.maximum(g_lo, 0.0),
        -jnp.minimum(g_hi, 0.0),
    )


def combine(k, mid, lo, hi, left, right):
    return k[0] * mid + k[1] * lo + k[2] * hi + k[3] * left + k[4] * right


def net(x_ref, h1_ref, h2_ref, w1_ref, b1_ref, w2_ref, b2_ref, w3_ref, emit):
    hidden = w2_ref.shape[0]
    wide = 256
    x = x_ref[...]
    for n in range(0, hidden, wide):
        u = dot(x, w1_ref[:, n : n + wide]) + b1_ref[:, n : n + wide]
        h1_ref[:, n : n + wide] = silu(u).astype(BF16)
    h1 = h1_ref[...]
    for n in range(0, hidden, wide):
        u = dot(h1, w2_ref[:, n : n + wide]) + b2_ref[:, n : n + wide]
        h2_ref[:, n : n + wide] = silu(u).astype(BF16)
    h2 = h2_ref[...]
    for n in range(0, FEAT, wide):
        emit(n, dot(h2, w3_ref[:, n : n + wide]))


def inner_kernel(
    t_ref, c_ref, mask_ref, w1_ref, b1_ref, w2_ref, b2_ref, w3_ref,
    out_ref, x_ref, adv_ref, h1_ref, h2_ref,
):
    mid = slice(EDGE, EDGE + INNER)
    left = slice(EDGE - 1, EDGE + INNER - 1)
    right = slice(EDGE + 1, EDGE + INNER + 1)

    def body(i, carry):
        first = 1 + i * GROUP
        for j in range(GROUP):
            r = first + j
            k = weights_of(
                c_ref[0, r - 1, mid, :], c_ref[0, r, mid, :], c_ref[0, r + 1, mid, :],
                c_ref[1, r, left, :], c_ref[1, r, mid, :], c_ref[1, r, right, :],
            )
            for f in range(FIELDS):
                at = slice(f * LANES, (f + 1) * LANES)
                moved = combine(
                    k, t_ref[f, r, mid, :], t_ref[f, r - 1, mid, :], t_ref[f, r + 1, mid, :],
                    t_ref[f, r, left, :], t_ref[f, r, right, :],
                )
                adv_ref[j * INNER : (j + 1) * INNER, at] = moved
                x_ref[j * INNER : (j + 1) * INNER, at] = moved.astype(BF16)

        def emit(n, heat):
            for j in range(GROUP):
                for m in range(0, heat.shape[1], LANES):
                    at = slice(n + m, n + m + LANES)
                    here = slice(j * INNER, (j + 1) * INNER)
                    out_ref[(n + m) // LANES, first + j, mid, :] = (
                        adv_ref[here, at] + mask_ref[first + j, mid, :] * heat[here, m : m + LANES]
                    )

        net(x_ref, h1_ref, h2_ref, w1_ref, b1_ref, w2_ref, b2_ref, w3_ref, emit)
        return carry

    lax.fori_loop(0, (ROWS - 2) // GROUP, body, 0)


def inner(state, speeds, mask, weights):
    many = GROUP * INNER
    hidden = weights[2].shape[0]
    return pl.pallas_call(
        inner_kernel,
        in_specs=[VMEM] * 8,
        out_specs=VMEM,
        out_shape=vmem_out((FIELDS, ROWS, COLS, LANES), F32),
        scratch_shapes=[
            pltpu.VMEM((many, FEAT), BF16),
            pltpu.VMEM((many, FEAT), F32),
            pltpu.VMEM((many, hidden), BF16),
            pltpu.VMEM((many, hidden), BF16),
        ],
        compiler_params=params(),
        cost_estimate=cost(7_500_000_000, 4 << 20),
        name="inner",
    )(state, speeds, mask, *weights)


def rim_kernel(
    last,
    valid_ref, t_ref, c_ref, mask_ref,
    row_lo_ref, row_hi_ref, col_lo_ref, col_hi_ref,
    crow_lo_ref, crow_hi_ref, ccol_lo_ref, ccol_hi_ref,
    w1_ref, b1_ref, w2_ref, b2_ref, w3_ref, *rest,
):
    if last:
        (place_ref, tags_ref, _, out_ref, pack_ref,
         x_ref, adv_ref, h1_ref, h2_ref, cols_ref, ccols_ref) = rest
    else:
        (_, out_ref, srow_lo_ref, srow_hi_ref, scol_lo_ref, scol_hi_ref,
         x_ref, adv_ref, h1_ref, h2_ref, cols_ref, ccols_ref) = rest
    lat = slice(0, LANES)
    speed_at = slice(FEAT, FEAT + LANES)
    for side, col, ccol in ((0, col_lo_ref, ccol_lo_ref), (1, col_hi_ref, ccol_hi_ref)):
        col = col[:, :FEAT].astype(F32)
        ccol = ccol[:, speed_at].astype(F32)
        for r in range(ROWS):
            cols_ref[side, r] = jnp.broadcast_to(col[r : r + 1, :], (EDGE, FEAT))
            ccols_ref[side, r] = jnp.broadcast_to(ccol[r : r + 1, :], (EDGE, LANES))

    def from_left(whole, edge):
        return jnp.where(iota(whole.shape, 0) == 0, edge, pltpu.roll(whole, 1, 0))

    def from_right(whole, edge):
        count = whole.shape[0]
        return jnp.where(iota(whole.shape, 0) == count - 1, edge, pltpu.roll(whole, count - 1, 0))

    for at_row, side in ((0, 0), (ROWS - 1, 1)):
        low_row = lambda ref, f, halo, at: halo[:, at].astype(F32) if side == 0 else ref[f, at_row - 1]
        high_row = lambda ref, f, halo, at: ref[f, at_row + 1] if side == 0 else halo[:, at].astype(F32)
        crow = crow_lo_ref if side == 0 else crow_hi_ref
        vrow = row_lo_ref if side == 0 else row_hi_ref
        mid1 = c_ref[1, at_row]
        k = weights_of(
            low_row(c_ref, 0, crow, speed_at), c_ref[0, at_row], high_row(c_ref, 0, crow, speed_at),
            from_left(mid1, ccols_ref[0, at_row, 0:1, :]), mid1,
            from_right(mid1, ccols_ref[1, at_row, 0:1, :]),
            valid_ref[0] if side == 0 else None,
            valid_ref[1] if side == 1 else None,
        )
        for f in range(FIELDS):
            at = slice(f * LANES, (f + 1) * LANES)
            v = t_ref[f, at_row]
            moved = combine(
                k, v, low_row(t_ref, f, vrow, at), high_row(t_ref, f, vrow, at),
                from_left(v, cols_ref[0, at_row, 0:1, at]),
                from_right(v, cols_ref[1, at_row, 0:1, at]),
            )
            adv_ref[side * COLS : (side + 1) * COLS, at] = moved
            x_ref[side * COLS : (side + 1) * COLS, at] = moved.astype(BF16)

    def edges(ref, f, r, cols, at):
        lo = ref[f, r, 0:EDGE, :]
        hi = ref[f, r, COLS - EDGE : COLS, :]
        left = jnp.concatenate(
            [from_left(lo, cols[0, r, :, at]), ref[f, r, COLS - EDGE - 1 : COLS - 1, :]], axis=0
        )
        right = jnp.concatenate(
            [ref[f, r, 1 : EDGE + 1, :], from_right(hi, cols[1, r, :, at])], axis=0
        )
        return jnp.concatenate([lo, hi], axis=0), left, right

    def both(ref, f, r):
        return jnp.concatenate([ref[f, r, 0:EDGE, :], ref[f, r, COLS - EDGE : COLS, :]], axis=0)

    def edge_row(i, carry):
        r = i + 1
        spot = pl.multiple_of(2 * COLS + i * 2 * EDGE, 2 * EDGE)
        mid1, left1, right1 = edges(c_ref, 1, r, ccols_ref, lat)
        k = weights_of(
            both(c_ref, 0, r - 1), both(c_ref, 0, r), both(c_ref, 0, r + 1), left1, mid1, right1
        )
        for f in range(FIELDS):
            at = slice(f * LANES, (f + 1) * LANES)
            v, left, right = edges(t_ref, f, r, cols_ref, at)
            moved = combine(k, v, both(t_ref, f, r - 1), both(t_ref, f, r + 1), left, right)
            adv_ref[pl.ds(spot, 2 * EDGE), at] = moved
            x_ref[pl.ds(spot, 2 * EDGE), at] = moved.astype(BF16)
        return carry

    lax.fori_loop(0, ROWS - 2, edge_row, 0)

    def emit(n, heat):
        for m in range(0, heat.shape[1], LANES):
            at = slice(n + m, n + m + LANES)
            part = heat[:, m : m + LANES]
            f = (n + m) // LANES
            for side, at_row in ((0, 0), (1, ROWS - 1)):
                here = slice(side * COLS, (side + 1) * COLS)
                out_ref[f, at_row] = adv_ref[here, at] + mask_ref[at_row] * part[here]
            for r in range(1, ROWS - 1):
                spot = 2 * COLS + (r - 1) * 2 * EDGE
                lo = slice(spot, spot + EDGE)
                hi = slice(spot + EDGE, spot + 2 * EDGE)
                out_ref[f, r, 0:EDGE, :] = adv_ref[lo, at] + mask_ref[r, 0:EDGE, :] * part[lo]
                out_ref[f, r, COLS - EDGE : COLS, :] = (
                    adv_ref[hi, at] + mask_ref[r, COLS - EDGE : COLS, :] * part[hi]
                )

    net(x_ref, h1_ref, h2_ref, w1_ref, b1_ref, w2_ref, b2_ref, w3_ref, emit)

    if not last:
        for f in range(FIELDS):
            at = slice(f * LANES, (f + 1) * LANES)
            srow_lo_ref[:, at] = out_ref[f, 0].astype(BF16)
            srow_hi_ref[:, at] = out_ref[f, ROWS - 1].astype(BF16)
            scol_lo_ref[:, at] = out_ref[f, :, 0].astype(BF16)
            scol_hi_ref[:, at] = out_ref[f, :, COLS - 1].astype(BF16)
        return
    flat = out_ref.reshape(FIELDS * CELLS, LANES)
    half = FEAT // 2
    for c in range(2):
        columns = jnp.concatenate(
            [
                flat[pl.ds(f * CELLS + c, SEGS, stride=2), :]
                for f in (2, 3)
            ],
            axis=1,
        ).astype(BF16)
        for q in range(2):
            for b in range(0, SEGS, 256):
                pack_ref[b : b + 256, q * FEAT + c * half : q * FEAT + (c + 1) * half] = dot(
                    place_ref[q, b : b + 256, :], columns
                ).astype(BF16)
    pack_ref[:, 2 * FEAT :] = tags_ref[...]


def rim(last, valid, state, speeds, mask, halo, speed_halo, weights, extra, partial):
    hidden = weights[2].shape[0]
    operands = (valid, state, speeds, mask, *halo, *speed_halo, *weights, *extra, partial)
    outs = [vmem_out((FIELDS, ROWS, COLS, LANES), F32)]
    if last:
        outs += [vmem_out((SEGS, 2 * FEAT + LANES), BF16)]
    else:
        outs += [vmem_out((COLS, FEAT), BF16)] * 2 + [vmem_out((ROWS, FEAT), BF16)] * 2
    return pl.pallas_call(
        lambda *refs: rim_kernel(last, *refs),
        in_specs=[SMEM] + [VMEM] * (len(operands) - 1),
        out_specs=[VMEM] * len(outs),
        out_shape=outs,
        input_output_aliases={len(operands) - 1: 0},
        scratch_shapes=[
            pltpu.VMEM((RIM, FEAT), BF16),
            pltpu.VMEM((RIM, FEAT), F32),
            pltpu.VMEM((RIM, hidden), BF16),
            pltpu.VMEM((RIM, hidden), BF16),
            pltpu.VMEM((2, ROWS, EDGE, FEAT), F32),
            pltpu.VMEM((2, ROWS, EDGE, LANES), F32),
        ],
        compiler_params=params(),
        cost_estimate=cost(4_000_000_000, 4 << 20),
        name="rim_last" if last else "rim",
    )(*operands)


def unturn_kernel(t_ref, out_ref, stage_ref, sems):
    size = LANES * ROWS
    for f in range(FIELDS):
        for r in range(ROWS):
            stage_ref[f, pl.ds(r, LANES, stride=ROWS), :] = t_ref[f, r].T
        pltpu.make_async_copy(
            stage_ref.at[f], out_ref.at[pl.ds(f * size, size)], sems.at[f]
        ).start()
    for f in range(FIELDS):
        pltpu.make_async_copy(
            stage_ref.at[f], out_ref.at[pl.ds(f * size, size)], sems.at[f]
        ).wait()


def unturn(state):
    return pl.pallas_call(
        unturn_kernel,
        in_specs=[VMEM],
        out_specs=ANY,
        out_shape=jax.ShapeDtypeStruct((FIELDS * LANES * ROWS, COLS), F32),
        scratch_shapes=[
            pltpu.VMEM((FIELDS, LANES * ROWS, COLS), F32),
            pltpu.SemaphoreType.DMA((FIELDS,)),
        ],
        compiler_params=params(),
        cost_estimate=cost(1_000_000_000, 8 << 20),
        name="unturn",
    )(state)


def chem_kernel(arr_ref, mix_ref, w1_ref, b1_ref, w2_ref, out_ref, want_ref, x_ref, h_ref):
    lane = iota((8, LANES), 1)
    which = iota((8, LANES), 0)
    pick = jnp.where(
        lane == 2 * which, 32.0, jnp.where(lane == 2 * which + 1, 1.0, 0.0)
    )
    pick = jnp.where(which < 2, pick, 0.0).astype(BF16)
    want_ref[...] = dot_nt(pick, arr_ref[:, 2 * FEAT :]).astype(jnp.int32) - 1
    span = 256
    half = FEAT // 2

    def body(i, carry):
        start = i * span
        placed = jnp.zeros((span, FEAT), F32)
        for q in range(2):
            chosen = (iota((span, SEGS), 0) + start == want_ref[q : q + 1, :]).astype(F32).astype(BF16)
            placed = placed + dot(chosen, arr_ref[:, q * FEAT : (q + 1) * FEAT])
        placed = placed.astype(BF16)
        for b in range(span // 64):
            cells = jnp.concatenate(
                [placed[b * 64 : (b + 1) * 64, :half], placed[b * 64 : (b + 1) * 64, half:]], axis=0
            )
            spot = pl.multiple_of(2 * start + b * LANES, LANES)
            x_ref[b * LANES : (b + 1) * LANES, :] = dot(mix_ref[pl.ds(spot, LANES), :], cells).astype(BF16)
        x = x_ref[...]
        for n in range(0, w1_ref.shape[1], 256):
            u = dot(x, w1_ref[:, n : n + 256]) + b1_ref[:, n : n + 256]
            h_ref[:, n : n + 256] = silu(u).astype(BF16)
        out_ref[pl.ds(pl.multiple_of(2 * start, 2 * span), 2 * span), :] = dot(h_ref[...], w2_ref[...]).astype(BF16)
        return carry

    lax.fori_loop(0, SEGS // span, body, 0)


def chem(arrived, mix, w1, b1, w2):
    return pl.pallas_call(
        chem_kernel,
        in_specs=[VMEM] * 5,
        out_specs=VMEM,
        out_shape=jax.ShapeDtypeStruct((CELLS, w2.shape[1]), BF16),
        scratch_shapes=[
            pltpu.VMEM((8, SEGS), jnp.int32),
            pltpu.VMEM((512, FEAT // 2), BF16),
            pltpu.VMEM((512, w1.shape[1]), BF16),
        ],
        compiler_params=params(),
        cost_estimate=cost(4_400_000_000, 4 << 20),
        name="chem",
    )(arrived, mix, w1, b1, w2)


def swap(low, high):
    rows, columns = lax.axis_size("gx"), lax.axis_size("gy")
    up = [(i, i + 1) for i in range(rows - 1)]
    down = [(i + 1, i) for i in range(rows - 1)]
    right = [(i, (i + 1) % columns) for i in range(columns)]
    left = [((i + 1) % columns, i) for i in range(columns)]
    row_lo, col_lo = low
    row_hi, col_hi = high
    return (
        lax.ppermute(row_hi, "gx", up),
        lax.ppermute(row_lo, "gx", down),
        lax.ppermute(col_hi, "gy", right),
        lax.ppermute(col_lo, "gy", left),
    )


def local(
    fields, courant, sun_columns, rad_w1, rad_b1, rad_w2, rad_b2, rad_w3,
    segment_route, regrid_weights, chem_w1, chem_b1, chem_w2,
):
    place_at = lax.axis_index("gx")
    valid = jnp.stack([place_at > 0, place_at < lax.axis_size("gx") - 1]).astype(F32)
    weights = (rad_w1, rad_b1.reshape(1, -1), rad_w2, rad_b2.reshape(1, -1), rad_w3)
    weights = tuple(pltpu.with_memory_space_constraint(w, pltpu.VMEM) for w in weights)

    state, speeds, row_lo, row_hi, col_lo, col_hi = turn(fields, courant)
    state = pltpu.with_memory_space_constraint(state, pltpu.VMEM)
    speeds = pltpu.with_memory_space_constraint(speeds, pltpu.VMEM)
    speed_halo = swap((row_lo, col_lo), (row_hi, col_hi))
    mask, place, tags, mix = plan(sun_columns, segment_route, regrid_weights)
    partial = inner(state, speeds, mask, weights)
    state, row_lo, row_hi, col_lo, col_hi = rim(
        False, valid, state, speeds, mask, speed_halo, speed_halo, weights, (), partial
    )
    halo = swap((row_lo, col_lo), (row_hi, col_hi))
    partial = inner(state, speeds, mask, weights)
    state, packed = rim(
        True, valid, state, speeds, mask, halo, speed_halo, weights, (place, tags), partial
    )
    tiles = lax.axis_size("gx") * lax.axis_size("gy")
    packed = packed.reshape(tiles, SEGS // tiles, packed.shape[1])
    arrived = lax.all_to_all(packed, ("gx", "gy"), split_axis=0, concat_axis=0, tiled=True)
    fields_out = unturn(state).reshape(fields.shape)
    output = chem(
        arrived.reshape(SEGS, arrived.shape[2]), mix, chem_w1, chem_b1.reshape(1, -1), chem_w2
    )
    return fields_out, output.reshape(1, 1, CELLS, -1)


def solution(mesh):
    return jax.shard_map(
        local,
        mesh=mesh,
        in_specs=(
            P(None, None, "gx", "gy"),
            P(None, None, "gx", "gy"),
            P("gx", "gy", None),
            P(),
            P(),
            P(),
            P(),
            P(),
            P(None, "gx", "gy", None),
            P("gx", "gy", None, None, None),
            P(),
            P(),
            P(),
        ),
        out_specs=(P(None, None, "gx", "gy"), P("gx", "gy", None, None)),
        check_vma=False,
    )
```

profile of v0, /device:TPU:1, one launch (start us, length us, event | category | flops | bytes accessed | tf_op | source)
XLA Modules:
  0.0 134.4 jit_solution(1840415737838545648)
XLA Ops:
  0.6 0.0 copy-start.12
  0.6 2.2 %copy-done.12 = f32[4,128,16,128]{3,2,1,0:T(8,128)S(1)} copy-done((f32[4,128,16,128]{3,2,1,0:T(8,128)S(1)}, f32[4,128,16,128]{3,2,1,0:T(8,128)}, u32[]{:S(2)}) %copy-start.12) | copy-done | bytes 4194328
  2.8 1.6 %copy-done.23 = f32[2,128,16,128]{3,2,1,0:T(8,128)S(1)} copy-done((f32[2,128,16,128]{3,2,1,0:T(8,128)S(1)}, f32[2,128,16,128]{3,2,1,0:T(8,128)}, u32[]{:S(2)}) %copy-start.23) | copy-done | bytes 2097176
  4.4 3.6 %turn.1 = (f32[4,16,128,128]{3,2,1,0:T(8,128)S(1)}, f32[2,16,128,128]{3,2,1,0:T(8,128)S(1)}, bf16[128,640]{1,0:T(8,128)(2,1)}, bf16[128,640]{1,0:T(8,128)(2,1)},...) custom-call(f32[8192,128]{1,0:T(8,128)S(1)} %bitcast.16, f32[4096,128]{1,0:T(8,128)S(1)} %bitcast.19), custom_call_target="tpu_custom_call" | custom-call | flops 20000000 | bytes 12582912 | tf_op jit(solution)/shard_map/turn/pallas_call | solution.py:94
  8.0 3.1 %collective-permute-start.2 = (bf16[16,640]{1,0:T(8,128)(2,1)}, bf16[16,640]{1,0:T(8,128)(2,1)S(1)}, u32[]{:S(2)}, u32[]{:S(2)}) collective-permute-start(bf16[16,640]{1,0:T(8,128)(2,1)} %get-tuple-element.24), channel_id=1, source_target_pairs={{0,1},{1,2},{2,3},{3,4},{4,5},{5,6},{6,7},{7,8},{8,9},{9,10},{10,1... | collective-permute-start | bytes 61448 | tf_op jit(solution)/shard_map/ppermute | solution.py:542
  11.1 0.0 collective-permute-start.3
  11.1 3.2 %collective-permute-start = (bf16[128,640]{1,0:T(8,128)(2,1)}, bf16[128,640]{1,0:T(8,128)(2,1)S(1)}, u32[]{:S(2)}, u32[]{:S(2)}) collective-permute-start(bf16[128,640]{1,0:T(8,128)(2,1)} %get-tuple-element.22), channel_id=1, source_target_pairs={{0,16},{16,32},{32,48},{48,64},{64,80},{80,96},{96,112},{1,17},{17... | collective-permute-start | bytes 491528 | tf_op jit(solution)/shard_map/ppermute | solution.py:540
  14.3 1.3 collective-permute-start.1
  15.6 0.0 copy-done.35
  15.6 0.0 copy-done.28
  15.7 0.0 copy-start.6
  15.7 0.0 copy-start.15
  15.7 0.0 copy-start.16
  15.7 0.0 copy-start.26
  15.7 0.0 copy-start.27
  15.7 2.5 %plan.1 = (f32[16,128,128]{2,1,0:T(8,128)S(1)}, bf16[2,1024,1024]{2,1,0:T(8,128)(2,1)S(1)}, bf16[1024,128]{1,0:T(8,128)(2,1)S(1)}, bf16[2048,128]{1,0:T(8,128)(2,1)S(1)}) custom-call(s32[1,2048]{1,0:T(1,128)S(1)} %bitcast.30, s32[2,1024]{1,0:T(2,128)S(1)} %bitcast.28, bf16[2048,128]{1,0:T(8,128)(2,1)S(1)} %bitcast.29), custom_call_target="tpu_custom_call" | custom-call | flops 3000000000 | bytes 1048576 | tf_op jit(solution)/shard_map/plan/pallas_call | solution.py:168
  18.2 1.9 %copy-done.10 = bf16[2,1024,1024]{2,1,0:T(8,128)(2,1)} copy-done((bf16[2,1024,1024]{2,1,0:T(8,128)(2,1)}, bf16[2,1024,1024]{2,1,0:T(8,128)(2,1)S(1)}, u32[]{:S(2)}) %copy-start.10) | copy-done | bytes 4194328
  20.2 0.0 copy-done.13
  20.2 0.0 copy-done.6
  20.2 0.0 copy-done.15
  20.2 0.0 copy-done.16
  20.2 0.0 copy-done.26
  20.2 0.0 copy-done.27
  20.2 10.8 %inner.2.refs_17_ = f32[4,16,128,128]{3,2,1,0:T(8,128)S(1)} custom-call(f32[4,16,128,128]{3,2,1,0:T(8,128)S(1)} %get-tuple-element.19.t_ref.refs_1_, f32[2,16,128,128]{3,2,1,0:T(8,128)S(1)} %get-tuple-element.20.c_ref.refs_2_, f32[16,128,128]{2,1,0:T(8,128)S(1)} %get-tuple-element.21.mask_ref.refs_3_, bf16[512,1024]{1,0:T(8,128)(2,1)S(1)} %copy-done.15, ...), custom_call_target="tpu_custom_call" | custom-call | flops 7500000256 | bytes 4194304 | tf_op jit(solution)/shard_map/inner/pallas_call | solution.py:276
  31.1 2.0 %copy-done.2 = f32[4,16,128,128]{3,2,1,0:T(8,128)} copy-done((f32[4,16,128,128]{3,2,1,0:T(8,128)}, f32[4,16,128,128]{3,2,1,0:T(8,128)S(1)}, u32[]{:S(2)}) %copy-start.2) | copy-done | bytes 4194328
  33.1 0.1 add_convert_fusion.refs_0_
  33.2 0.0 collective-permute-done.2.refs_6_.refs_10_
  33.2 0.0 collective-permute-done.3.refs_7_.refs_11_
  33.2 0.0 collective-permute-done.refs_4_.refs_8_
  33.2 0.0 collective-permute-done.1.refs_5_.refs_9_
  33.2 2.2 %copy-done.3 = f32[4,16,128,128]{3,2,1,0:T(8,128)S(1)} copy-done((f32[4,16,128,128]{3,2,1,0:T(8,128)S(1)}, f32[4,16,128,128]{3,2,1,0:T(8,128)}, u32[]{:S(2)}) %copy-start.3) | copy-done | bytes 4194328
  35.4 1.6 %copy-done.8 = f32[2,16,128,128]{3,2,1,0:T(8,128)S(1)} copy-done((f32[2,16,128,128]{3,2,1,0:T(8,128)S(1)}, f32[2,16,128,128]{3,2,1,0:T(8,128)}, u32[]{:S(2)}) %copy-start.8) | copy-done | bytes 2097176
  37.0 2.2 %copy-done.14 = f32[4,16,128,128]{3,2,1,0:T(8,128)S(1)} copy-done((f32[4,16,128,128]{3,2,1,0:T(8,128)S(1)}, f32[4,16,128,128]{3,2,1,0:T(8,128)}, u32[]{:S(2)}) %copy-start.14) | copy-done | bytes 4194328
  39.2 1.2 copy-done.17
  40.4 1.2 copy-done.20
  41.6 3.9 %rim.1 = (f32[4,16,128,128]{3,2,1,0:T(8,128)S(1)}, bf16[128,512]{1,0:T(8,128)(2,1)S(1)}, bf16[128,512]{1,0:T(8,128)(2,1)S(1)}, bf16[16,512]{1,0:T(8,128)(2,1)S(1)}, bf16[16,512]{1,0:T(8,128)(2,1)S(1)}) custom-call(f32[2]{0:T(128)S(1)} %add_convert_fusion.refs_0_, f32[4,16,128,128]{3,2,1,0:T(8,128)S(1)} %copy-done.14, ...), custom_call_target="tpu_custom_call", output_to_operand_aliasing={{0}: (17, {})} | custom-call | flops 4000000000 | bytes 4194304 | tf_op jit(solution)/shard_map/rim/pallas_call | solution.py:430
  45.5 0.0 copy-start.4
  45.6 2.1 %collective-permute-start.6 = (bf16[16,512]{1,0:T(8,128)(2,1)S(1)}, bf16[16,512]{1,0:T(8,128)(2,1)S(1)}, u32[]{:S(2)}, u32[]{:S(2)}) collective-permute-start(bf16[16,512]{1,0:T(8,128)(2,1)S(1)} %get-tuple-element.29), channel_id=1, source_target_pairs={{0,1},{1,2},{2,3},{3,4},{4,5},{5,6},{6,7},{7,8},{8,9},{9,10},{10,1... | collective-permute-start | bytes 49160 | tf_op jit(solution)/shard_map/ppermute | solution.py:542
  47.7 2.2 %collective-permute-start.7 = (bf16[16,512]{1,0:T(8,128)(2,1)S(1)}, bf16[16,512]{1,0:T(8,128)(2,1)S(1)}, u32[]{:S(2)}, u32[]{:S(2)}) collective-permute-start(bf16[16,512]{1,0:T(8,128)(2,1)S(1)} %get-tuple-element.30), channel_id=1, source_target_pairs={{1,0},{2,1},{3,2},{4,3},{5,4},{6,5},{7,6},{8,7},{9,8},{10,9},{11,1... | collective-permute-start | bytes 49160 | tf_op jit(solution)/shard_map/ppermute | solution.py:543
  49.8 4.5 %collective-permute-start.4 = (bf16[128,512]{1,0:T(8,128)(2,1)S(1)}, bf16[128,512]{1,0:T(8,128)(2,1)S(1)}, u32[]{:S(2)}, u32[]{:S(2)}) collective-permute-start(bf16[128,512]{1,0:T(8,128)(2,1)S(1)} %get-tuple-element.27), channel_id=1, source_target_pairs={{0,16},{16,32},{32,48},{48,64},{64,80},{80,96},{96,112},{1,17},{17... | collective-permute-start | bytes 393224 | tf_op jit(solution)/shard_map/ppermute | solution.py:540
  54.3 1.5 %collective-permute-start.5 = (bf16[128,512]{1,0:T(8,128)(2,1)S(1)}, bf16[128,512]{1,0:T(8,128)(2,1)S(1)}, u32[]{:S(2)}, u32[]{:S(2)}) collective-permute-start(bf16[128,512]{1,0:T(8,128)(2,1)S(1)} %get-tuple-element.28), channel_id=1, source_target_pairs={{16,0},{32,16},{48,32},{64,48},{80,64},{96,80},{112,96},{17,1},{33... | collective-permute-start | bytes 393224 | tf_op jit(solution)/shard_map/ppermute | solution.py:541
  55.8 0.0 copy-done.9
  55.8 0.0 copy-done.21
  55.8 0.0 copy-start.11
  55.8 0.0 copy-start.18
  55.8 10.8 %inner.3.refs_19_ = f32[4,16,128,128]{3,2,1,0:T(8,128)S(1)} custom-call(f32[4,16,128,128]{3,2,1,0:T(8,128)S(1)} %get-tuple-element.26.t_ref.refs_1_, f32[2,16,128,128]{3,2,1,0:T(8,128)S(1)} %copy-done.9, f32[16,128,128]{2,1,0:T(8,128)S(1)} %copy-done.21, bf16[512,1024]{1,0:T(8,128)(2,1)S(1)} %copy-done.15, f32[1,1024]{1,0:T(1,128)S(1)} %bitcast.22, ...), custom_call_target="tpu_custom_call" | custom-call | flops 7500000256 | bytes 4194304 | tf_op jit(solution)/shard_map/inner/pallas_call | solution.py:276
  66.7 0.0 collective-permute-done.6.refs_6_
  66.7 0.0 collective-permute-done.7.refs_7_
  66.7 0.0 collective-permute-done.4.refs_4_
  66.7 0.0 collective-permute-done.5.refs_5_
  66.7 0.0 copy-start.5
  66.8 2.2 %copy-done.5 = f32[4,16,128,128]{3,2,1,0:T(8,128)S(1)} copy-done((f32[4,16,128,128]{3,2,1,0:T(8,128)S(1)}, f32[4,16,128,128]{3,2,1,0:T(8,128)}, u32[]{:S(2)}) %copy-start.5) | copy-done | bytes 4194328
  68.9 6.2 %rim_last.1 = (f32[4,16,128,128]{3,2,1,0:T(8,128)S(1)}, bf16[1024,1152]{1,0:T(8,128)(2,1)S(1)}) custom-call(f32[2]{0:T(128)S(1)} %add_convert_fusion.refs_0_, f32[4,16,128,128]{3,2,1,0:T(8,128)S(1)} %copy-done.5, f32[2,16,128,128]{3,2,1,0:T(8,128)S(1)} %copy-done.9, f32[16,128,128]{2,1,0:T(8,128)S(1)} %copy-done.21, ...), custom_call_target="tpu_custom_call", output_to_operand_aliasing={{0}: (19, {})} | custom-call | flops 4000000000 | bytes 4194304 | tf_op jit(solution)/shard_map/rim_last/pallas_call | solution.py:430
  75.1 0.0 copy-start
  75.1 2.0 %copy-done = f32[4,16,128,128]{3,2,1,0:T(8,128)} copy-done((f32[4,16,128,128]{3,2,1,0:T(8,128)}, f32[4,16,128,128]{3,2,1,0:T(8,128)S(1)}, u32[]{:S(2)}) %copy-start) | copy-done | bytes 4194328
  77.1 1.4 %copy-done.22 = bf16[1024,1152]{1,0:T(8,128)(2,1)} copy-done((bf16[1024,1152]{1,0:T(8,128)(2,1)}, bf16[1024,1152]{1,0:T(8,128)(2,1)S(1)}, u32[]{:S(2)}) %copy-start.22) | copy-done | bytes 2359320
  78.6 14.7 %all-to-all-start = ((bf16[128,8,1152]{2,1,0:T(8,128)(2,1)}), bf16[128,8,1152]{2,1,0:T(8,128)(2,1)S(1)}, u32[]{:S(2)}, u32[]{:S(2)}) async-start(bf16[128,8,1152]{2,1,0:T(8,128)(2,1)} %bitcast.17), calls=%async_computation | async-start | bytes 4718592 | tf_op jit(solution)/shard_map/all_to_all | solution.py:572
  93.3 0.0 copy-start.1
  93.3 2.2 %copy-done.1 = f32[4,16,128,128]{3,2,1,0:T(8,128)S(1)} copy-done((f32[4,16,128,128]{3,2,1,0:T(8,128)S(1)}, f32[4,16,128,128]{3,2,1,0:T(8,128)}, u32[]{:S(2)}) %copy-start.1) | copy-done | bytes 4194328
  95.5 2.5 %unturn.1 = f32[8192,128]{1,0:T(8,128)} custom-call(f32[4,16,128,128]{3,2,1,0:T(8,128)S(1)} %copy-done.1), custom_call_target="tpu_custom_call" | custom-call | flops 1000000000 | bytes 8388608 | tf_op jit(solution)/shard_map/unturn/pallas_call | solution.py:465
  97.9 27.9 %all-to-all-done = bf16[128,8,1152]{2,1,0:T(8,128)(2,1)S(1)} async-done(((bf16[128,8,1152]{2,1,0:T(8,128)(2,1)}), bf16[128,8,1152]{2,1,0:T(8,128)(2,1)S(1)}, u32[]{:S(2)}, u32[]{:S(2)}) %all-to-all-start) | async-done | bytes 2359328 | tf_op jit(solution)/shard_map/all_to_all | solution.py:572
  125.8 0.0 copy-done.29
  125.8 1.0 copy-done.34
  126.9 7.5 %chem.1 = bf16[2048,256]{1,0:T(8,128)(2,1)} custom-call(bf16[1024,1152]{1,0:T(8,128)(2,1)S(1)} %bitcast.18, bf16[2048,128]{1,0:T(8,128)(2,1)S(1)} %copy-done.34, bf16[256,1024]{1,0:T(8,128)(2,1)S(1)} %copy-done.29, f32[1,1024]{1,0:T(1,128)S(1)} %bitcast.31, bf16[1024,256]{1,0:T(8,128)(2,1)S(1)} %copy-done.30), custom_call_target="tpu_custom_call" | custom-call | flops 4400000000 | bytes 4194304 | tf_op jit(solution)/shard_map/chem/pallas_call | solution.py:515
  (36 shorter events, 0.1 us)
Async XLA Ops:
  0.6 2.2 %copy-start.12 = (f32[4,128,16,128]{3,2,1,0:T(8,128)S(1)}, f32[4,128,16,128]{3,2,1,0:T(8,128)}, u32[]{:S(2)}) copy-start(f32[4,128,16,128]{3,2,1,0:T(8,128)} %param.13) | copy-start | bytes 12582916
  2.8 1.6 %copy-start.23 = (f32[2,128,16,128]{3,2,1,0:T(8,128)S(1)}, f32[2,128,16,128]{3,2,1,0:T(8,128)}, u32[]{:S(2)}) copy-start(f32[2,128,16,128]{3,2,1,0:T(8,128)} %param.14) | copy-start | bytes 6291460
  4.4 11.2 %copy-start.35 = (s32[2,1,1,1024]{3,2,1,0:T(1,128)S(1)}, s32[2,1,1,1024]{3,2,1,0:T(1,128)}, u32[]{:S(2)}) copy-start(s32[2,1,1,1024]{3,2,1,0:T(1,128)} %param.21) | copy-start | bytes 24580
  4.4 11.2 %copy-start.28 = (bf16[1,1,16,128,128]{4,3,2,1,0:T(8,128)(2,1)S(1)}, bf16[1,1,16,128,128]{4,3,2,1,0:T(8,128)(2,1)}, u32[]{:S(2)}) copy-start(bf16[1,1,16,128,128]{4,3,2,1,0:T(8,128)(2,1)} %param.22) | copy-start | bytes 1572868
  4.4 11.2 %copy-start.31 = (s32[1,1,2048]{2,1,0:T(1,128)S(1)}, s32[1,1,2048]{2,1,0:T(1,128)}, u32[]{:S(2)}) copy-start(s32[1,1,2048]{2,1,0:T(1,128)} %param.15) | copy-start | bytes 24580
  8.0 12.2 %copy-start.7 = (f32[2,16,128,128]{3,2,1,0:T(8,128)}, f32[2,16,128,128]{3,2,1,0:T(8,128)S(1)}, u32[]{:S(2)}) copy-start(f32[2,16,128,128]{3,2,1,0:T(8,128)S(1)} %get-tuple-element.20.c_ref.refs_2_) | copy-start | bytes 6291460
  8.0 12.2 %copy-start.13 = (f32[4,16,128,128]{3,2,1,0:T(8,128)}, f32[4,16,128,128]{3,2,1,0:T(8,128)S(1)}, u32[]{:S(2)}) copy-start(f32[4,16,128,128]{3,2,1,0:T(8,128)S(1)} %get-tuple-element.19.t_ref.refs_1_) | copy-start | bytes 12582916
  8.0 25.2 %collective-permute-start.2 = (bf16[16,640]{1,0:T(8,128)(2,1)}, bf16[16,640]{1,0:T(8,128)(2,1)S(1)}, u32[]{:S(2)}, u32[]{:S(2)}) collective-permute-start(bf16[16,640]{1,0:T(8,128)(2,1)} %get-tuple-element.24), channel_id=1, source_target_pairs={{0,1},{1,2},{2,3},{3,4},{4,5},{5,6},{6,7},{7,8},{8,9},{9,10},{10,1... | collective-permute-start | bytes 61448 | tf_op jit(solution)/shard_map/ppermute | solution.py:542
  11.1 22.1 %collective-permute-start.3 = (bf16[16,640]{1,0:T(8,128)(2,1)S(1)}, bf16[16,640]{1,0:T(8,128)(2,1)S(1)}, u32[]{:S(2)}, u32[]{:S(2)}) collective-permute-start(bf16[16,640]{1,0:T(8,128)(2,1)S(1)} %get-tuple-element.25), channel_id=1, source_target_pairs={{1,0},{2,1},{3,2},{4,3},{5,4},{6,5},{7,6},{8,7},{9,8},{10,9},{11,1... | collective-permute-start | bytes 61448 | tf_op jit(solution)/shard_map/ppermute | solution.py:543
  11.1 22.1 %collective-permute-start = (bf16[128,640]{1,0:T(8,128)(2,1)}, bf16[128,640]{1,0:T(8,128)(2,1)S(1)}, u32[]{:S(2)}, u32[]{:S(2)}) collective-permute-start(bf16[128,640]{1,0:T(8,128)(2,1)} %get-tuple-element.22), channel_id=1, source_target_pairs={{0,16},{16,32},{32,48},{48,64},{64,80},{80,96},{96,112},{1,17},{17... | collective-permute-start | bytes 491528 | tf_op jit(solution)/shard_map/ppermute | solution.py:540
  14.3 18.9 %collective-permute-start.1 = (bf16[128,640]{1,0:T(8,128)(2,1)}, bf16[128,640]{1,0:T(8,128)(2,1)S(1)}, u32[]{:S(2)}, u32[]{:S(2)}) collective-permute-start(bf16[128,640]{1,0:T(8,128)(2,1)} %get-tuple-element.23), channel_id=1, source_target_pairs={{16,0},{32,16},{48,32},{64,48},{80,64},{96,80},{112,96},{17,1},{33... | collective-permute-start | bytes 491528 | tf_op jit(solution)/shard_map/ppermute | solution.py:541
  15.7 4.5 %copy-start.6 = (bf16[1024,1024]{1,0:T(8,128)(2,1)S(1)}, bf16[1024,1024]{1,0:T(8,128)(2,1)}, u32[]{:S(2)}) copy-start(bf16[1024,1024]{1,0:T(8,128)(2,1)} %refs_14_.3) | copy-start | bytes 6291460
  15.7 4.5 %copy-start.15 = (bf16[512,1024]{1,0:T(8,128)(2,1)S(1)}, bf16[512,1024]{1,0:T(8,128)(2,1)}, u32[]{:S(2)}) copy-start(bf16[512,1024]{1,0:T(8,128)(2,1)} %refs_12_.3) | copy-start | bytes 3145732
  15.7 4.5 %copy-start.16 = (bf16[1024,512]{1,0:T(8,128)(2,1)S(1)}, bf16[1024,512]{1,0:T(8,128)(2,1)}, u32[]{:S(2)}) copy-start(bf16[1024,512]{1,0:T(8,128)(2,1)} %refs_16_.3) | copy-start | bytes 3145732
  15.7 4.5 %copy-start.26 = (f32[1024]{0:T(1024)S(1)}, f32[1024]{0:T(1024)}, u32[]{:S(2)}) copy-start(f32[1024]{0:T(1024)} %param.17) | copy-start | bytes 12292
  15.7 4.5 %copy-start.27 = (f32[1024]{0:T(1024)S(1)}, f32[1024]{0:T(1024)}, u32[]{:S(2)}) copy-start(f32[1024]{0:T(1024)} %param.19) | copy-start | bytes 12292
  18.2 2.0 %copy-start.10 = (bf16[2,1024,1024]{2,1,0:T(8,128)(2,1)}, bf16[2,1024,1024]{2,1,0:T(8,128)(2,1)S(1)}, u32[]{:S(2)}) copy-start(bf16[2,1024,1024]{2,1,0:T(8,128)(2,1)S(1)} %get-tuple-element.31.refs_17_) | copy-start | bytes 12582916
  20.2 10.9 %copy-start.19 = (f32[16,128,128]{2,1,0:T(8,128)}, f32[16,128,128]{2,1,0:T(8,128)S(1)}, u32[]{:S(2)}) copy-start(f32[16,128,128]{2,1,0:T(8,128)S(1)} %get-tuple-element.21.mask_ref.refs_3_) | copy-start | bytes 3145732
  20.2 10.9 %copy-start.24 = (bf16[1024,128]{1,0:T(8,128)(2,1)}, bf16[1024,128]{1,0:T(8,128)(2,1)S(1)}, u32[]{:S(2)}) copy-start(bf16[1024,128]{1,0:T(8,128)(2,1)S(1)} %get-tuple-element.32.refs_18_) | copy-start | bytes 786436
  20.2 10.9 %copy-start.33 = (bf16[2048,128]{1,0:T(8,128)(2,1)}, bf16[2048,128]{1,0:T(8,128)(2,1)S(1)}, u32[]{:S(2)}) copy-start(bf16[2048,128]{1,0:T(8,128)(2,1)S(1)} %get-tuple-element.35.mix_ref) | copy-start | bytes 1572868
  31.1 2.0 %copy-start.2 = (f32[4,16,128,128]{3,2,1,0:T(8,128)}, f32[4,16,128,128]{3,2,1,0:T(8,128)S(1)}, u32[]{:S(2)}) copy-start(f32[4,16,128,128]{3,2,1,0:T(8,128)S(1)} %inner.2.refs_17_) | copy-start | bytes 12582916
  33.2 2.2 %copy-start.3 = (f32[4,16,128,128]{3,2,1,0:T(8,128)S(1)}, f32[4,16,128,128]{3,2,1,0:T(8,128)}, u32[]{:S(2)}) copy-start(f32[4,16,128,128]{3,2,1,0:T(8,128)} %copy-done.2) | copy-start | bytes 12582916
  35.4 1.6 %copy-start.8 = (f32[2,16,128,128]{3,2,1,0:T(8,128)S(1)}, f32[2,16,128,128]{3,2,1,0:T(8,128)}, u32[]{:S(2)}) copy-start(f32[2,16,128,128]{3,2,1,0:T(8,128)} %copy-done.7) | copy-start | bytes 6291460
  37.0 2.2 %copy-start.14 = (f32[4,16,128,128]{3,2,1,0:T(8,128)S(1)}, f32[4,16,128,128]{3,2,1,0:T(8,128)}, u32[]{:S(2)}) copy-start(f32[4,16,128,128]{3,2,1,0:T(8,128)} %copy-done.13) | copy-start | bytes 12582916
  39.2 1.2 copy-start.17
  40.4 1.2 copy-start.20
  41.6 14.2 %copy-start.9 = (f32[2,16,128,128]{3,2,1,0:T(8,128)S(1)}, f32[2,16,128,128]{3,2,1,0:T(8,128)}, u32[]{:S(2)}) copy-start(f32[2,16,128,128]{3,2,1,0:T(8,128)} %copy-done.7) | copy-start | bytes 6291460
  41.6 14.2 %copy-start.21 = (f32[16,128,128]{2,1,0:T(8,128)S(1)}, f32[16,128,128]{2,1,0:T(8,128)}, u32[]{:S(2)}) copy-start(f32[16,128,128]{2,1,0:T(8,128)} %copy-done.19) | copy-start | bytes 3145732
  45.5 21.1 %copy-start.4 = (f32[4,16,128,128]{3,2,1,0:T(8,128)}, f32[4,16,128,128]{3,2,1,0:T(8,128)S(1)}, u32[]{:S(2)}) copy-start(f32[4,16,128,128]{3,2,1,0:T(8,128)S(1)} %get-tuple-element.26.t_ref.refs_1_) | copy-start | bytes 12582916
  45.6 21.1 %collective-permute-start.6 = (bf16[16,512]{1,0:T(8,128)(2,1)S(1)}, bf16[16,512]{1,0:T(8,128)(2,1)S(1)}, u32[]{:S(2)}, u32[]{:S(2)}) collective-permute-start(bf16[16,512]{1,0:T(8,128)(2,1)S(1)} %get-tuple-element.29), channel_id=1, source_target_pairs={{0,1},{1,2},{2,3},{3,4},{4,5},{5,6},{6,7},{7,8},{8,9},{9,10},{10,1... | collective-permute-start | bytes 49160 | tf_op jit(solution)/shard_map/ppermute | solution.py:542
  47.7 19.0 %collective-permute-start.7 = (bf16[16,512]{1,0:T(8,128)(2,1)S(1)}, bf16[16,512]{1,0:T(8,128)(2,1)S(1)}, u32[]{:S(2)}, u32[]{:S(2)}) collective-permute-start(bf16[16,512]{1,0:T(8,128)(2,1)S(1)} %get-tuple-element.30), channel_id=1, source_target_pairs={{1,0},{2,1},{3,2},{4,3},{5,4},{6,5},{7,6},{8,7},{9,8},{10,9},{11,1... | collective-permute-start | bytes 49160 | tf_op jit(solution)/shard_map/ppermute | solution.py:543
  49.8 16.9 %collective-permute-start.4 = (bf16[128,512]{1,0:T(8,128)(2,1)S(1)}, bf16[128,512]{1,0:T(8,128)(2,1)S(1)}, u32[]{:S(2)}, u32[]{:S(2)}) collective-permute-start(bf16[128,512]{1,0:T(8,128)(2,1)S(1)} %get-tuple-element.27), channel_id=1, source_target_pairs={{0,16},{16,32},{32,48},{48,64},{64,80},{80,96},{96,112},{1,17},{17... | collective-permute-start | bytes 393224 | tf_op jit(solution)/shard_map/ppermute | solution.py:540
  54.3 12.4 %collective-permute-start.5 = (bf16[128,512]{1,0:T(8,128)(2,1)S(1)}, bf16[128,512]{1,0:T(8,128)(2,1)S(1)}, u32[]{:S(2)}, u32[]{:S(2)}) collective-permute-start(bf16[128,512]{1,0:T(8,128)(2,1)S(1)} %get-tuple-element.28), channel_id=1, source_target_pairs={{16,0},{32,16},{48,32},{64,48},{80,64},{96,80},{112,96},{17,1},{33... | collective-permute-start | bytes 393224 | tf_op jit(solution)/shard_map/ppermute | solution.py:541
  55.8 10.9 %copy-start.11 = (bf16[2,1024,1024]{2,1,0:T(8,128)(2,1)S(1)}, bf16[2,1024,1024]{2,1,0:T(8,128)(2,1)}, u32[]{:S(2)}) copy-start(bf16[2,1024,1024]{2,1,0:T(8,128)(2,1)} %copy-done.10) | copy-start | bytes 12582916
  55.8 10.9 %copy-start.18 = (bf16[1024,512]{1,0:T(8,128)(2,1)S(1)}, bf16[1024,512]{1,0:T(8,128)(2,1)}, u32[]{:S(2)}) copy-start(bf16[1024,512]{1,0:T(8,128)(2,1)} %refs_16_.3) | copy-start | bytes 3145732
  55.8 10.9 %copy-start.25 = (bf16[1024,128]{1,0:T(8,128)(2,1)S(1)}, bf16[1024,128]{1,0:T(8,128)(2,1)}, u32[]{:S(2)}) copy-start(bf16[1024,128]{1,0:T(8,128)(2,1)} %copy-done.24) | copy-start | bytes 786436
  66.7 2.2 %copy-start.5 = (f32[4,16,128,128]{3,2,1,0:T(8,128)S(1)}, f32[4,16,128,128]{3,2,1,0:T(8,128)}, u32[]{:S(2)}) copy-start(f32[4,16,128,128]{3,2,1,0:T(8,128)} %copy-done.4) | copy-start | bytes 12582916
  75.1 2.0 %copy-start = (f32[4,16,128,128]{3,2,1,0:T(8,128)}, f32[4,16,128,128]{3,2,1,0:T(8,128)S(1)}, u32[]{:S(2)}) copy-start(f32[4,16,128,128]{3,2,1,0:T(8,128)S(1)} %get-tuple-element.33.t_ref) | copy-start | bytes 12582916
  77.1 1.4 %copy-start.22 = (bf16[1024,1152]{1,0:T(8,128)(2,1)}, bf16[1024,1152]{1,0:T(8,128)(2,1)S(1)}, u32[]{:S(2)}) copy-start(bf16[1024,1152]{1,0:T(8,128)(2,1)S(1)} %get-tuple-element.34) | copy-start | bytes 7077892
  78.6 47.2 %all-to-all-start = ((bf16[128,8,1152]{2,1,0:T(8,128)(2,1)}), bf16[128,8,1152]{2,1,0:T(8,128)(2,1)S(1)}, u32[]{:S(2)}, u32[]{:S(2)}) async-start(bf16[128,8,1152]{2,1,0:T(8,128)(2,1)} %bitcast.17), calls=%async_computation | async-start | bytes 4718592 | tf_op jit(solution)/shard_map/all_to_all | solution.py:572
  93.3 2.2 %copy-start.1 = (f32[4,16,128,128]{3,2,1,0:T(8,128)S(1)}, f32[4,16,128,128]{3,2,1,0:T(8,128)}, u32[]{:S(2)}) copy-start(f32[4,16,128,128]{3,2,1,0:T(8,128)} %copy-done) | copy-start | bytes 12582916
  95.5 30.3 %copy-start.29 = (bf16[256,1024]{1,0:T(8,128)(2,1)S(1)}, bf16[256,1024]{1,0:T(8,128)(2,1)}, u32[]{:S(2)}) copy-start(bf16[256,1024]{1,0:T(8,128)(2,1)} %w1_ref.5) | copy-start | bytes 1572868
  95.5 30.3 %copy-start.30 = (bf16[1024,256]{1,0:T(8,128)(2,1)S(1)}, bf16[1024,256]{1,0:T(8,128)(2,1)}, u32[]{:S(2)}) copy-start(bf16[1024,256]{1,0:T(8,128)(2,1)} %w2_ref.5) | copy-start | bytes 1572868
  95.5 30.3 %copy-start.32 = (f32[1024]{0:T(1024)S(1)}, f32[1024]{0:T(1024)}, u32[]{:S(2)}) copy-start(f32[1024]{0:T(1024)} %param.24) | copy-start | bytes 12292
  125.8 1.0 copy-start.34
where the time goes:
time: 135 us; the launch traced here: 134 us
  Pallas kernels  47.8 us (35%)
  starting transfers between devices  32.5 us (24%)
  waiting for transfers between devices  27.9 us (21%)
  local copies, waits for them, and re-layouts  25.1 us (19%)
    all_to_all x1, waiting for transfers between devices, local(): lax.all_to_all(packed, ('gx', 'gy'), split_axis=0, concat_axis=0, tiled=T...  27.9 us
    unnamed x73, local copies, waits for them, and re-layouts  25.1 us
    pallas_call x2, Pallas kernels, inner(): pl.pallas_call(inner_kernel, in_specs=[VMEM] * 8, out_specs=VMEM, out_sha...  21.6 us
    all_to_all x1, starting transfers between devices, local(): lax.all_to_all(packed, ('gx', 'gy'), split_axis=0, concat_axis=0, tiled=T...  14.7 us
    pallas_call x2, Pallas kernels, rim(): pl.pallas_call(lambda *refs: rim_kernel(last, *refs), in_specs=[SMEM] + [...  10.1 us
    ppermute x2, starting transfers between devices, swap(): lax.ppermute(row_hi, 'gx', up)  7.67 us
    pallas_call x1, Pallas kernels, chem(): pl.pallas_call(chem_kernel, in_specs=[VMEM] * 5, out_specs=VMEM, out_shap...  7.53 us
    ppermute x2, starting transfers between devices, swap(): lax.ppermute(col_hi, 'gy', right)  5.19 us
  transfers between devices with their start and end apart: 9, of which 1 were waited for; matrix products, arithmetic and copies ran while one was open for 0% of the time, Pallas kernels for 20%

commit v1 on v0

v1 whole, which is shorter than its diff:
```python
import jax
import jax.numpy as jnp
from jax import lax
from jax.experimental import pallas as pl
from jax.experimental.pallas import tpu as pltpu
from jax.sharding import PartitionSpec as P

F32 = jnp.float32
BF16 = jnp.bfloat16
LANES = 128
FIELDS = 4
ROWS = 16
COLS = 128
FEAT = FIELDS * LANES
CELLS = ROWS * COLS
SEGS = CELLS // 2
EDGE = 8
INNER = COLS - 2 * EDGE
GROUP = 7
RIM = 2 * COLS + (ROWS - 2) * 2 * EDGE
VMEM_LIMIT = 40 * 1024 * 1024

VMEM = pl.BlockSpec(memory_space=pltpu.VMEM)
SMEM = pl.BlockSpec(memory_space=pltpu.SMEM)
ANY = pl.BlockSpec(memory_space=pl.ANY)


HBM = pl.BlockSpec(memory_space=pltpu.HBM)


def hbm_out(shape, dtype):
    return pltpu.HBM(shape, dtype)


def in_vmem(x):
    return pltpu.with_memory_space_constraint(x, pltpu.VMEM)


def in_hbm(x):
    return pltpu.with_memory_space_constraint(x, pltpu.HBM)


def params():
    return pltpu.CompilerParams(vmem_limit_bytes=VMEM_LIMIT)


def cost(flops, bytes_accessed=0):
    return pl.CostEstimate(flops=flops, bytes_accessed=bytes_accessed, transcendentals=0)


def dot(a, b):
    return jnp.dot(a, b, preferred_element_type=F32)


def dot_nt(a, b):
    return lax.dot_general(a, b, (((1,), (1,)), ((), ())), preferred_element_type=F32)


def silu(u):
    half = 0.5 * u
    return half + half * jnp.tanh(half)


def iota(shape, dim):
    return lax.broadcasted_iota(jnp.int32, shape, dim)


def turn_kernel(f_ref, c_ref, t_ref, cc_ref, row_lo_ref, row_hi_ref, col_lo_ref, col_hi_ref):
    step = pl.program_id(0)

    @pl.when(step < FIELDS)
    def _():
        for r in range(ROWS):
            block = f_ref[pl.ds(r, LANES, stride=ROWS), :].T
            t_ref[0, r] = block
            if r == 0:
                row_lo_ref[...] = block.astype(BF16)
            if r == ROWS - 1:
                row_hi_ref[...] = block.astype(BF16)
        col_lo_ref[...] = t_ref[0, :, 0, :].astype(BF16)
        col_hi_ref[...] = t_ref[0, :, COLS - 1, :].astype(BF16)

    @pl.when(step >= FIELDS)
    def _():
        for r in range(ROWS):
            cc_ref[0, r] = c_ref[pl.ds(r, LANES, stride=ROWS), :].T

    @pl.when(step == FIELDS)
    def _():
        row_lo_ref[...] = cc_ref[0, 0].astype(BF16)
        row_hi_ref[...] = cc_ref[0, ROWS - 1].astype(BF16)

    @pl.when(step == FIELDS + 1)
    def _():
        col_lo_ref[...] = cc_ref[0, :, 0, :].astype(BF16)
        col_hi_ref[...] = cc_ref[0, :, COLS - 1, :].astype(BF16)


def turn(fields, courant):
    flat_f = in_hbm(fields.reshape(FIELDS * LANES * ROWS, COLS))
    flat_c = in_hbm(courant.reshape(2 * LANES * ROWS, COLS))
    field_at = lambda i: jnp.minimum(i, FIELDS - 1)
    speed_at = lambda i: jnp.maximum(i - FIELDS, 0)
    halo_at = lambda i: jnp.minimum(i, FIELDS)
    return pl.pallas_call(
        turn_kernel,
        grid=(FIELDS + 2,),
        in_specs=[
            pl.BlockSpec((LANES * ROWS, COLS), lambda i: (field_at(i), 0)),
            pl.BlockSpec((LANES * ROWS, COLS), lambda i: (speed_at(i), 0)),
        ],
        out_specs=[
            pl.BlockSpec((1, ROWS, COLS, LANES), lambda i: (field_at(i), 0, 0, 0)),
            pl.BlockSpec((1, ROWS, COLS, LANES), lambda i: (speed_at(i), 0, 0, 0)),
            pl.BlockSpec((COLS, LANES), lambda i: (0, halo_at(i))),
            pl.BlockSpec((COLS, LANES), lambda i: (0, halo_at(i))),
            pl.BlockSpec((ROWS, LANES), lambda i: (0, halo_at(i))),
            pl.BlockSpec((ROWS, LANES), lambda i: (0, halo_at(i))),
        ],
        out_shape=[
            hbm_out((FIELDS, ROWS, COLS, LANES), F32),
            jax.ShapeDtypeStruct((2, ROWS, COLS, LANES), F32),
            jax.ShapeDtypeStruct((COLS, FEAT + LANES), BF16),
            jax.ShapeDtypeStruct((COLS, FEAT + LANES), BF16),
            jax.ShapeDtypeStruct((ROWS, FEAT + LANES), BF16),
            jax.ShapeDtypeStruct((ROWS, FEAT + LANES), BF16),
        ],
        compiler_params=params(),
        cost_estimate=cost(20_000_000, 12 << 20),
        name="turn",
    )(flat_f, flat_c)


def plan_kernel(sun_ref, route_ref, mask_ref, place_ref, tags_ref, stage_ref, sems):
    slots = sun_ref[...]
    low = (iota((COLS, CELLS), 0) == (slots & (COLS - 1))).astype(F32).astype(BF16)
    high = (iota((LANES, CELLS), 0) == (slots >> 7)).astype(F32).astype(BF16)
    lit = dot_nt(low, high)
    mask_ref[...] = lit

    target = route_ref[0:1, :]
    arrival = route_ref[1:2, :] + 1
    before = (iota((LANES, LANES), 0) < iota((LANES, LANES), 1)).astype(F32).astype(BF16)
    ones = jnp.ones((LANES, LANES), BF16)
    carry = jnp.zeros((LANES, LANES), F32)
    ranks = []
    for b in range(SEGS // LANES):
        goes = (iota((LANES, LANES), 0) == target[:, b * LANES : (b + 1) * LANES]).astype(F32)
        goes16 = goes.astype(BF16)
        ranks.append(jnp.sum(goes * (dot(goes16, before) + carry), axis=0, keepdims=True))
        carry = carry + dot(goes16, ones)
    rank = jnp.concatenate(ranks, axis=1).astype(jnp.int32)
    row = target * 16 + rank
    index = iota((LANES, SEGS), 0)
    coarse = (arrival >> 5).astype(F32)
    fine = (arrival & 31).astype(F32)
    tag_rows = [
        jnp.where(index == 2 * q, coarse, jnp.where(index == 2 * q + 1, fine, 0.0)).astype(BF16)
        for q in range(2)
    ]
    for b in range(SEGS // LANES):
        tags = jnp.zeros((LANES, LANES), F32)
        for q in range(2):
            want = 2 * (iota((LANES, SEGS), 0) + b * LANES) + q
            chosen = (row == want).astype(F32).astype(BF16)
            at = (q, slice(b * LANES, (b + 1) * LANES))
            stage_ref[at] = chosen
            pltpu.make_async_copy(stage_ref.at[at], place_ref.at[at], sems.at[q, b]).start()
            tags = tags + dot_nt(chosen, tag_rows[q])
        tags_ref[b * LANES : (b + 1) * LANES, :] = tags.astype(BF16)
    for b in range(SEGS // LANES):
        for q in range(2):
            at = (q, slice(b * LANES, (b + 1) * LANES))
            pltpu.make_async_copy(stage_ref.at[at], place_ref.at[at], sems.at[q, b]).wait()


def plan(sun_columns, segment_route):
    return pl.pallas_call(
        plan_kernel,
        in_specs=[VMEM] * 2,
        out_specs=[VMEM, HBM, VMEM],
        out_shape=[
            jax.ShapeDtypeStruct((COLS, LANES), F32),
            hbm_out((2, SEGS, SEGS), BF16),
            jax.ShapeDtypeStruct((SEGS, LANES), BF16),
        ],
        scratch_shapes=[
            pltpu.VMEM((2, SEGS, SEGS), BF16),
            pltpu.SemaphoreType.DMA((2, SEGS // LANES)),
        ],
        compiler_params=params(),
        cost_estimate=cost(3_000_000_000, 1 << 20),
        name="plan",
    )(sun_columns.reshape(1, CELLS), segment_route.reshape(2, SEGS))


def weights_of(lo0, mid0, hi0, left1, mid1, right1, valid_lo=None, valid_hi=None):
    f_lo = 0.5 * (lo0 + mid0)
    f_hi = 0.5 * (mid0 + hi0)
    if valid_lo is not None:
        f_lo = f_lo * valid_lo
    if valid_hi is not None:
        f_hi = f_hi * valid_hi
    g_lo = 0.5 * (left1 + mid1)
    g_hi = 0.5 * (mid1 + right1)
    keep = (
        1.0
        - jnp.maximum(f_hi, 0.0)
        + jnp.minimum(f_lo, 0.0)
        - jnp.maximum(g_hi, 0.0)
        + jnp.minimum(g_lo, 0.0)
    )
    return (
        keep,
        jnp.maximum(f_lo, 0.0),
        -jnp.minimum(f_hi, 0.0),
        jnp.maximum(g_lo, 0.0),
        -jnp.minimum(g_hi, 0.0),
    )


def combine(k, mid, lo, hi, left, right):
    return k[0] * mid + k[1] * lo + k[2] * hi + k[3] * left + k[4] * right


def net(x, h1_ref, h2_ref, w1_ref, b1_ref, w2_ref, b2_ref, w3_ref, emit, beside=(), ready=None):
    hidden = w2_ref.shape[0]
    wide = 256
    beside = list(beside)
    for n in range(0, hidden, wide):
        u = dot(x, w1_ref[:, n : n + wide]) + b1_ref[:, n : n + wide]
        h1_ref[:, n : n + wide] = silu(u).astype(BF16)
    if ready is not None:
        ready(1)
    h1 = h1_ref[...]
    for n in range(0, hidden, wide):
        u = dot(h1, w2_ref[:, n : n + wide]) + b2_ref[:, n : n + wide]
        h2_ref[:, n : n + wide] = silu(u).astype(BF16)
        if beside:
            beside.pop(0)()
    if ready is not None:
        ready(2)
    h2 = h2_ref[...]
    for n in range(0, FEAT, wide):
        emit(n, dot(h2, w3_ref[:, n : n + wide]))


def weight_copies(sources, held, sems):
    return [pltpu.make_async_copy(a, b, sems.at[i]) for i, (a, b) in enumerate(zip(sources, held))]


def inner_kernel(
    mask_ref, c_ref, w1_ref, b1_ref, w2_ref, b2_ref, w3_ref, t_hbm, out_hbm,
    t_ref, out_ref, lit_ref, x_ref, adv_ref, h1_ref, h2_ref, t_sems, out_sems,
):
    groups = (ROWS - 2) // GROUP

    def load(g, first, count):
        at = pl.ds(first, count)
        return pltpu.make_async_copy(t_hbm.at[:, at], t_ref.at[:, at], t_sems.at[g])

    def store(g):
        return pltpu.make_async_copy(
            out_ref.at[:, pl.ds(g * GROUP, GROUP)],
            out_hbm.at[:, pl.ds(1 + g * GROUP, GROUP), pl.ds(EDGE, INNER)],
            out_sems.at[g],
        )

    load(0, 0, 2).start()
    for g in range(groups):
        load(g + 1, GROUP * g + 2, GROUP).start()
    for r in range(ROWS):
        lit_ref[r] = jnp.broadcast_to(mask_ref[:, r : r + 1], (COLS, LANES))
    load(0, 0, 2).wait()

    mid = slice(EDGE, EDGE + INNER)
    left = slice(EDGE - 1, EDGE + INNER - 1)
    right = slice(EDGE + 1, EDGE + INNER + 1)

    def body(g, carry):
        load(g + 1, GROUP * g + 2, GROUP).wait()
        for j in range(GROUP):
            r = 1 + g * GROUP + j
            k = weights_of(
                c_ref[0, r - 1, mid, :], c_ref[0, r, mid, :], c_ref[0, r + 1, mid, :],
                c_ref[1, r, left, :], c_ref[1, r, mid, :], c_ref[1, r, right, :],
            )
            for f in range(FIELDS):
                at = slice(f * LANES, (f + 1) * LANES)
                moved = combine(
                    k, t_ref[f, r, mid, :], t_ref[f, r - 1, mid, :], t_ref[f, r + 1, mid, :],
                    t_ref[f, r, left, :], t_ref[f, r, right, :],
                )
                adv_ref[j * INNER : (j + 1) * INNER, at] = moved
                x_ref[j * INNER : (j + 1) * INNER, at] = moved.astype(BF16)

        def emit(n, heat):
            for j in range(GROUP):
                r = 1 + g * GROUP + j
                lit = lit_ref[r, mid, :]
                for m in range(0, heat.shape[1], LANES):
                    here = slice(j * INNER, (j + 1) * INNER)
                    out_ref[(n + m) // LANES, r - 1] = (
                        adv_ref[here, n + m : n + m + LANES] + lit * heat[here, m : m + LANES]
                    )

        net(x_ref[...], h1_ref, h2_ref, w1_ref, b1_ref, w2_ref, b2_ref, w3_ref, emit)
        store(g).start()
        return carry

    lax.fori_loop(0, groups, body, 0)
    for g in range(groups):
        store(g).wait()


def inner(state, speeds, mask, weights):
    many = GROUP * INNER
    hidden = weights[2].shape[0]
    groups = (ROWS - 2) // GROUP
    return pl.pallas_call(
        inner_kernel,
        in_specs=[VMEM] * 7 + [HBM],
        out_specs=HBM,
        out_shape=hbm_out((FIELDS, ROWS, COLS, LANES), F32),
        scratch_shapes=[
            pltpu.VMEM((FIELDS, ROWS, COLS, LANES), F32),
            pltpu.VMEM((FIELDS, ROWS - 2, INNER, LANES), F32),
            pltpu.VMEM((ROWS, COLS, LANES), F32),
            pltpu.VMEM((many, FEAT), BF16),
            pltpu.VMEM((many, FEAT), F32),
            pltpu.VMEM((many, hidden), BF16),
            pltpu.VMEM((many, hidden), BF16),
            pltpu.SemaphoreType.DMA((groups + 1,)),
            pltpu.SemaphoreType.DMA((groups,)),
        ],
        compiler_params=params(),
        cost_estimate=cost(7_500_000_000, 4 << 20),
        name="inner",
    )(
        mask,
        in_vmem(speeds),
        *(in_vmem(w) if w.dtype == BF16 else w for w in weights),
        in_hbm(state),
    )


def rim_kernel(
    last,
    valid_ref, mask_ref,
    row_lo_ref, row_hi_ref, col_lo_ref, col_hi_ref,
    crow_lo_ref, crow_hi_ref, ccol_lo_ref, ccol_hi_ref,
    b1_ref, b2_ref, *rest,
):
    if last:
        tags_ref, rest = rest[0], rest[1:]
        t_hbm, c_hbm, w1_hbm, w2_hbm, w3_hbm, place_hbm, part_hbm, out_hbm, pack_hbm = rest[:9]
        rest = rest[9:]
    else:
        t_hbm, c_hbm, w1_hbm, w2_hbm, w3_hbm, part_hbm, out_hbm = rest[:7]
        srow_lo_ref, srow_hi_ref, scol_lo_ref, scol_hi_ref = rest[7:11]
        rest = rest[11:]
    (
        trow_ref, tlo_ref, thi_ref, crow_ref, clo_ref, chi_ref,
        w1_ref, w2_ref, w3_ref, out_ref, x_ref, adv_ref, h1_ref, h2_ref, cols_ref, ccols_ref,
        t_sems, w_sems, out_sems,
    ) = rest[:19]
    if last:
        place_ref, pack_ref, place_sems, pack_sems = rest[19:]
    loads = []
    for hbm, row, lo, hi in ((t_hbm, trow_ref, tlo_ref, thi_ref), (c_hbm, crow_ref, clo_ref, chi_ref)):
        loads += [
            (hbm.at[:, pl.ds(0, 2)], row.at[:, pl.ds(0, 2)]),
            (hbm.at[:, pl.ds(ROWS - 2, 2)], row.at[:, pl.ds(2, 2)]),
            (hbm.at[:, :, pl.ds(0, 2 * EDGE)], lo),
            (hbm.at[:, :, pl.ds(COLS - 2 * EDGE, 2 * EDGE)], hi),
        ]
    loads = [pltpu.make_async_copy(x, y, t_sems.at[i]) for i, (x, y) in enumerate(loads)]
    weight_loads = weight_copies((w1_hbm, w2_hbm, w3_hbm), (w1_ref, w2_ref, w3_ref), w_sems)
    for copy in loads + weight_loads:
        copy.start()
    if last:
        centre = (pl.ds(1, ROWS - 2), pl.ds(EDGE, INNER))
        centre_load = pltpu.make_async_copy(
            part_hbm.at[pl.ds(2, 2), *centre], out_ref.at[pl.ds(2, 2), *centre], place_sems.at[2]
        )
        centre_load.start()
        place_loads = weight_copies((place_hbm.at[0], place_hbm.at[1]), (place_ref.at[0], place_ref.at[1]), place_sems)
        for copy in place_loads:
            copy.start()
    speed_at = slice(FEAT, FEAT + LANES)
    for side, col, ccol in ((0, col_lo_ref, ccol_lo_ref), (1, col_hi_ref, ccol_hi_ref)):
        col = col[:, :FEAT].astype(F32)
        ccol = ccol[:, speed_at].astype(F32)
        for r in range(ROWS):
            cols_ref[side, r] = jnp.broadcast_to(col[r : r + 1, :], (EDGE, FEAT))
            ccols_ref[side, r] = jnp.broadcast_to(ccol[r : r + 1, :], (EDGE, LANES))

    lat = slice(0, LANES)
    for copy in loads:
        copy.wait()

    def from_left(whole, edge):
        return jnp.where(iota(whole.shape, 0) == 0, edge, pltpu.roll(whole, 1, 0))

    def from_right(whole, edge):
        count = whole.shape[0]
        return jnp.where(iota(whole.shape, 0) == count - 1, edge, pltpu.roll(whole, count - 1, 0))

    for at_row, side in ((0, 0), (ROWS - 1, 1)):
        low_row = lambda ref, f, halo, at: halo[:, at].astype(F32) if side == 0 else ref[f, 2]
        high_row = lambda ref, f, halo, at: ref[f, 1] if side == 0 else halo[:, at].astype(F32)
        crow = crow_lo_ref if side == 0 else crow_hi_ref
        vrow = row_lo_ref if side == 0 else row_hi_ref
        held = 0 if side == 0 else 3
        mid1 = crow_ref[1, held]
        k = weights_of(
            low_row(crow_ref, 0, crow, speed_at), crow_ref[0, held], high_row(crow_ref, 0, crow, speed_at),
            from_left(mid1, ccols_ref[0, at_row, 0:1, :]), mid1,
            from_right(mid1, ccols_ref[1, at_row, 0:1, :]),
            valid_ref[0] if side == 0 else None,
            valid_ref[1] if side == 1 else None,
        )
        for f in range(FIELDS):
            at = slice(f * LANES, (f + 1) * LANES)
            v = trow_ref[f, held]
            moved = combine(
                k, v, low_row(trow_ref, f, vrow, at), high_row(trow_ref, f, vrow, at),
                from_left(v, cols_ref[0, at_row, 0:1, at]),
                from_right(v, cols_ref[1, at_row, 0:1, at]),
            )
            adv_ref[side * COLS : (side + 1) * COLS, at] = moved
            x_ref[side * COLS : (side + 1) * COLS, at] = moved.astype(BF16)

    def edges(lo_ref, hi_ref, f, r, cols, at):
        lo = lo_ref[f, r, 0:EDGE, :]
        hi = hi_ref[f, r, EDGE : 2 * EDGE, :]
        left = jnp.concatenate(
            [from_left(lo, cols[0, r, :, at]), hi_ref[f, r, EDGE - 1 : 2 * EDGE - 1, :]], axis=0
        )
        right = jnp.concatenate(
            [lo_ref[f, r, 1 : EDGE + 1, :], from_right(hi, cols[1, r, :, at])], axis=0
        )
        return jnp.concatenate([lo, hi], axis=0), left, right

    def both(lo_ref, hi_ref, f, r):
        return jnp.concatenate([lo_ref[f, r, 0:EDGE, :], hi_ref[f, r, EDGE : 2 * EDGE, :]], axis=0)

    def edge_row(i, carry):
        r = i + 1
        spot = pl.multiple_of(2 * COLS + i * 2 * EDGE, 2 * EDGE)
        mid1, left1, right1 = edges(clo_ref, chi_ref, 1, r, ccols_ref, lat)
        k = weights_of(
            both(clo_ref, chi_ref, 0, r - 1), both(clo_ref, chi_ref, 0, r), both(clo_ref, chi_ref, 0, r + 1), left1, mid1, right1
        )
        for f in range(FIELDS):
            at = slice(f * LANES, (f + 1) * LANES)
            v, left, right = edges(tlo_ref, thi_ref, f, r, cols_ref, at)
            moved = combine(k, v, both(tlo_ref, thi_ref, f, r - 1), both(tlo_ref, thi_ref, f, r + 1), left, right)
            adv_ref[pl.ds(spot, 2 * EDGE), at] = moved
            x_ref[pl.ds(spot, 2 * EDGE), at] = moved.astype(BF16)
        return carry

    lax.fori_loop(0, ROWS - 2, edge_row, 0)

    def emit(n, heat):
        for m in range(0, heat.shape[1], LANES):
            at = slice(n + m, n + m + LANES)
            part = heat[:, m : m + LANES]
            f = (n + m) // LANES
            for side, at_row in ((0, 0), (1, ROWS - 1)):
                here = slice(side * COLS, (side + 1) * COLS)
                out_ref[f, at_row] = adv_ref[here, at] + mask_ref[:, at_row : at_row + 1] * part[here]
            for r in range(1, ROWS - 1):
                spot = 2 * COLS + (r - 1) * 2 * EDGE
                lo = slice(spot, spot + EDGE)
                hi = slice(spot + EDGE, spot + 2 * EDGE)
                out_ref[f, r, 0:EDGE, :] = adv_ref[lo, at] + mask_ref[0:EDGE, r : r + 1] * part[lo]
                out_ref[f, r, COLS - EDGE : COLS, :] = (
                    adv_ref[hi, at] + mask_ref[COLS - EDGE : COLS, r : r + 1] * part[hi]
                )

    weight_loads[0].wait()
    net(
        x_ref[...], h1_ref, h2_ref, w1_ref, b1_ref, w2_ref, b2_ref, w3_ref, emit, (),
        lambda n: weight_loads[n].wait(),
    )
    stores = []
    for i, at in enumerate((
        (slice(None), 0),
        (slice(None), ROWS - 1),
        (slice(None), pl.ds(1, ROWS - 2), pl.ds(0, EDGE)),
        (slice(None), pl.ds(1, ROWS - 2), pl.ds(COLS - EDGE, EDGE)),
    )):
        stores.append(pltpu.make_async_copy(out_ref.at[at], out_hbm.at[at], out_sems.at[i]))
        stores[-1].start()

    if not last:
        for f in range(FIELDS):
            at = slice(f * LANES, (f + 1) * LANES)
            srow_lo_ref[:, at] = out_ref[f, 0].astype(BF16)
            srow_hi_ref[:, at] = out_ref[f, ROWS - 1].astype(BF16)
            scol_lo_ref[:, at] = out_ref[f, :, 0].astype(BF16)
            scol_hi_ref[:, at] = out_ref[f, :, COLS - 1].astype(BF16)
        for store in stores:
            store.wait()
        return
    centre_load.wait()
    for copy in place_loads:
        copy.wait()
    flat = out_ref.reshape(FIELDS * CELLS, LANES)
    half = FEAT // 2
    columns = [
        jnp.concatenate(
            [flat[pl.ds(f * CELLS + c, SEGS, stride=2), :] for f in (2, 3)], axis=1
        ).astype(BF16)
        for c in range(2)
    ]
    pack_ref[:, 2 * FEAT :] = tags_ref[...]
    for i, b in enumerate(range(0, SEGS, 256)):
        for q in range(2):
            for c in range(2):
                pack_ref[b : b + 256, q * FEAT + c * half : q * FEAT + (c + 1) * half] = dot(
                    place_ref[q, b : b + 256, :], columns[c]
                ).astype(BF16)
        at = pl.ds(b, 256)
        stores.append(pltpu.make_async_copy(pack_ref.at[at], pack_hbm.at[at], pack_sems.at[i]))
        stores[-1].start()
    for store in stores:
        store.wait()


def rim(last, valid, state, speeds, mask, halo, speed_halo, weights, extra, partial):
    w1, b1, w2, b2, w3 = weights
    hidden = w2.shape[0]
    near = (valid, mask, *halo, *speed_halo, b1, b2)
    far = (in_hbm(state), in_hbm(speeds), in_hbm(w1), in_hbm(w2), in_hbm(w3))
    if last:
        place, tags = extra
        near += (tags,)
        far += (in_hbm(place),)
    far += (in_hbm(partial),)
    outs = [hbm_out((FIELDS, ROWS, COLS, LANES), F32)]
    scratch = [
        pltpu.VMEM((FIELDS, 4, COLS, LANES), F32),
        pltpu.VMEM((FIELDS, ROWS, 2 * EDGE, LANES), F32),
        pltpu.VMEM((FIELDS, ROWS, 2 * EDGE, LANES), F32),
        pltpu.VMEM((2, 4, COLS, LANES), F32),
        pltpu.VMEM((2, ROWS, 2 * EDGE, LANES), F32),
        pltpu.VMEM((2, ROWS, 2 * EDGE, LANES), F32),
        pltpu.VMEM(w1.shape, BF16),
        pltpu.VMEM(w2.shape, BF16),
        pltpu.VMEM(w3.shape, BF16),
        pltpu.VMEM((FIELDS, ROWS, COLS, LANES), F32),
        pltpu.VMEM((RIM, FEAT), BF16),
        pltpu.VMEM((RIM, FEAT), F32),
        pltpu.VMEM((RIM, hidden), BF16),
        pltpu.VMEM((RIM, hidden), BF16),
        pltpu.VMEM((2, ROWS, EDGE, FEAT), F32),
        pltpu.VMEM((2, ROWS, EDGE, LANES), F32),
        pltpu.SemaphoreType.DMA((8,)),
        pltpu.SemaphoreType.DMA((3,)),
        pltpu.SemaphoreType.DMA((4,)),
    ]
    if last:
        outs += [hbm_out((SEGS, 2 * FEAT + LANES), BF16)]
        out_specs = [HBM] * 2
        scratch += [
            pltpu.VMEM((2, SEGS, SEGS), BF16),
            pltpu.VMEM((SEGS, 2 * FEAT + LANES), BF16),
            pltpu.SemaphoreType.DMA((3,)),
            pltpu.SemaphoreType.DMA((SEGS // 256,)),
        ]
    else:
        outs += [jax.ShapeDtypeStruct((COLS, FEAT), BF16)] * 2
        outs += [jax.ShapeDtypeStruct((ROWS, FEAT), BF16)] * 2
        out_specs = [HBM] + [VMEM] * 4
    operands = near + far
    return pl.pallas_call(
        lambda *refs: rim_kernel(last, *refs),
        in_specs=[SMEM] + [VMEM] * (len(near) - 1) + [HBM] * len(far),
        out_specs=out_specs,
        out_shape=outs,
        input_output_aliases={len(operands) - 1: 0},
        scratch_shapes=scratch,
        compiler_params=params(),
        cost_estimate=cost(4_000_000_000, 4 << 20),
        name="rim_last" if last else "rim",
    )(*operands)


def unturn_kernel(t_hbm, out_ref, t_ref, stage_ref, in_sems, sems):
    size = LANES * ROWS
    loads = [pltpu.make_async_copy(t_hbm.at[f], t_ref.at[f], in_sems.at[f]) for f in range(FIELDS)]
    stores = [
        pltpu.make_async_copy(stage_ref.at[f], out_ref.at[pl.ds(f * size, size)], sems.at[f])
        for f in range(FIELDS)
    ]
    for load in loads:
        load.start()
    for f in range(FIELDS):
        loads[f].wait()
        for r in range(ROWS):
            stage_ref[f, pl.ds(r, LANES, stride=ROWS), :] = t_ref[f, r].T
        stores[f].start()
    for store in stores:
        store.wait()


def unturn(state):
    return pl.pallas_call(
        unturn_kernel,
        in_specs=[HBM],
        out_specs=HBM,
        out_shape=hbm_out((FIELDS * LANES * ROWS, COLS), F32),
        scratch_shapes=[
            pltpu.VMEM((FIELDS, ROWS, COLS, LANES), F32),
            pltpu.VMEM((FIELDS, LANES * ROWS, COLS), F32),
            pltpu.SemaphoreType.DMA((FIELDS,)),
            pltpu.SemaphoreType.DMA((FIELDS,)),
        ],
        compiler_params=params(),
        cost_estimate=cost(1_000_000_000, 8 << 20),
        name="unturn",
    )(in_hbm(state))


def chem_kernel(
    arr_ref, regrid_ref, w1_ref, b1_ref, w2_ref, out_hbm, want_ref, mix_ref, x_ref, h_ref, out_ref, sems
):
    from_cell = iota((LANES, LANES), 0)
    to_lane = iota((LANES, LANES), 1)
    source_cell = jnp.where(to_lane < 64, 2 * to_lane, 2 * (to_lane - 64) + 1)
    split = (from_cell == source_cell).astype(F32).astype(BF16)
    mix_ref[...] = dot(regrid_ref[...], split).astype(BF16)
    lane = iota((8, LANES), 1)
    which = iota((8, LANES), 0)
    pick = jnp.where(lane == 2 * which, 32.0, jnp.where(lane == 2 * which + 1, 1.0, 0.0))
    pick = jnp.where(which < 2, pick, 0.0).astype(BF16)
    want_ref[...] = dot_nt(pick, arr_ref[:, 2 * FEAT :]).astype(jnp.int32) - 1
    span = 256
    half = FEAT // 2
    stores = []
    for i in range(SEGS // span):
        start = i * span
        placed = []
        for q in range(2):
            chosen = (iota((span, SEGS), 0) + start == want_ref[q : q + 1, :]).astype(F32).astype(BF16)
            placed.append(dot(chosen, arr_ref[:, q * FEAT : (q + 1) * FEAT]))
        placed = (placed[0] + placed[1]).astype(BF16)
        for b in range(span // 64):
            cells = jnp.concatenate(
                [placed[b * 64 : (b + 1) * 64, :half], placed[b * 64 : (b + 1) * 64, half:]], axis=0
            )
            spot = 2 * start + b * LANES
            x_ref[i % 2, b * LANES : (b + 1) * LANES, :] = dot(
                mix_ref[spot : spot + LANES, :], cells
            ).astype(BF16)
        x = x_ref[i % 2]
        for n in range(0, w1_ref.shape[1], 256):
            u = dot(x, w1_ref[:, n : n + 256]) + b1_ref[:, n : n + 256]
            h_ref[i % 2, :, n : n + 256] = silu(u).astype(BF16)
        rows = slice(2 * start, 2 * (start + span))
        out_ref[rows, :] = dot(h_ref[i % 2], w2_ref[...]).astype(BF16)
        at = pl.ds(2 * start, 2 * span)
        stores.append(pltpu.make_async_copy(out_ref.at[at], out_hbm.at[at], sems.at[i]))
        stores[-1].start()
    for store in stores:
        store.wait()


def chem(arrived, regrid_weights, w1, b1, w2):
    return pl.pallas_call(
        chem_kernel,
        in_specs=[VMEM] * 5,
        out_specs=HBM,
        out_shape=hbm_out((CELLS, w2.shape[1]), BF16),
        scratch_shapes=[
            pltpu.VMEM((8, SEGS), jnp.int32),
            pltpu.VMEM((CELLS, LANES), BF16),
            pltpu.VMEM((2, 512, FEAT // 2), BF16),
            pltpu.VMEM((2, 512, w1.shape[1]), BF16),
            pltpu.VMEM((CELLS, w2.shape[1]), BF16),
            pltpu.SemaphoreType.DMA((SEGS // 256,)),
        ],
        compiler_params=params(),
        cost_estimate=cost(4_400_000_000, 4 << 20),
        name="chem",
    )(
        in_vmem(arrived),
        in_vmem(regrid_weights.reshape(CELLS, LANES)),
        in_vmem(w1),
        b1,
        in_vmem(w2),
    )


def swap(low, high):
    rows, columns = lax.axis_size("gx"), lax.axis_size("gy")
    up = [(i, i + 1) for i in range(rows - 1)]
    down = [(i + 1, i) for i in range(rows - 1)]
    right = [(i, (i + 1) % columns) for i in range(columns)]
    left = [((i + 1) % columns, i) for i in range(columns)]
    row_lo, col_lo = low
    row_hi, col_hi = high
    return (
        lax.ppermute(row_hi, "gx", up),
        lax.ppermute(row_lo, "gx", down),
        lax.ppermute(col_hi, "gy", right),
        lax.ppermute(col_lo, "gy", left),
    )


def local(
    fields, courant, sun_columns, rad_w1, rad_b1, rad_w2, rad_b2, rad_w3,
    segment_route, regrid_weights, chem_w1, chem_b1, chem_w2,
):
    place_at = lax.axis_index("gx")
    valid = jnp.stack([place_at > 0, place_at < lax.axis_size("gx") - 1]).astype(F32)
    weights = (rad_w1, rad_b1.reshape(1, -1), rad_w2, rad_b2.reshape(1, -1), rad_w3)

    state, speeds, row_lo, row_hi, col_lo, col_hi = turn(fields, courant)
    speed_halo = swap((row_lo, col_lo), (row_hi, col_hi))
    mask, place, tags = plan(sun_columns, segment_route)
    partial = inner(state, speeds, mask, weights)
    state, row_lo, row_hi, col_lo, col_hi = rim(
        False, valid, state, speeds, mask, speed_halo, speed_halo, weights, (), partial
    )
    halo = swap((row_lo, col_lo), (row_hi, col_hi))
    partial = inner(state, speeds, mask, weights)
    state, packed = rim(
        True, valid, state, speeds, mask, halo, speed_halo, weights, (place, tags), partial
    )
    tiles = lax.axis_size("gx") * lax.axis_size("gy")
    packed = packed.reshape(tiles, SEGS // tiles, packed.shape[1])
    arrived = lax.all_to_all(packed, ("gx", "gy"), split_axis=0, concat_axis=0, tiled=True)
    fields_out = unturn(state).reshape(fields.shape)
    output = chem(
        arrived.reshape(SEGS, arrived.shape[2]), regrid_weights, chem_w1, chem_b1.reshape(1, -1), chem_w2
    )
    return fields_out, output.reshape(1, 1, CELLS, -1)


def solution(mesh):
    return jax.shard_map(
        local,
        mesh=mesh,
        in_specs=(
            P(None, None, "gx", "gy"),
            P(None, None, "gx", "gy"),
            P("gx", "gy", None),
            P(),
            P(),
            P(),
            P(),
            P(),
            P(None, "gx", "gy", None),
            P("gx", "gy", None, None, None),
            P(),
            P(),
            P(),
        ),
        out_specs=(P(None, None, "gx", "gy"), P("gx", "gy", None, None)),
        check_vma=False,
    )
```

time: 135 us -> 131 us (0.970)
  local copies, waits for them, and re-layouts: 25.1 us -> 1.59 us
  Pallas kernels: 47.8 us -> 66.8 us
    unnamed x73 -> x37, local copies, waits for them, and re-layouts: 25.1 us -> 1.59 us
    pallas_call x2, Pallas kernels: 10.1 us -> 19.8 us  [rim(): pl.pallas_call(lambda *refs: rim_kernel(last, *refs), in_specs=[SMEM] + [...]
    pallas_call x5, Pallas kernels: 34.1 us -> 38.9 us  [the longest x2 24.1 us: inner(): pl.pallas_call(inner_kernel, in_specs=[VMEM] * 7 + [HBM], out_specs=HBM,...]
    pallas_call x1, Pallas kernels: 3.58 us -> 8.07 us  [turn(): pl.pallas_call(turn_kernel, grid=(FIELDS + 2,), in_specs=[pl.BlockSpec((L...]
  transfers between devices with their start and end apart: 9 -> 9, of which waited for: 1 -> 1; matrix products, arithmetic and copies ran while one was open for 0% -> 0% of each run, Pallas kernels for 20% -> 24%
where the time goes in v1:
time: 131 us
  Pallas kernels  66.8 us (51%)
  starting transfers between devices  32.5 us (25%)
  waiting for transfers between devices  28.5 us (22%)
  local copies, waits for them, and re-layouts  1.59 us (1%)
    all_to_all x1, waiting for transfers between devices, local(): lax.all_to_all(packed, ('gx', 'gy'), split_axis=0, concat_axis=0, tiled=T...  28.5 us
    pallas_call x2, Pallas kernels, inner(): pl.pallas_call(inner_kernel, in_specs=[VMEM] * 7 + [HBM], out_specs=HBM,...  24.1 us
    pallas_call x2, Pallas kernels, rim(): pl.pallas_call(lambda *refs: rim_kernel(last, *refs), in_specs=[SMEM] + [...  19.8 us
    all_to_all x1, starting transfers between devices, local(): lax.all_to_all(packed, ('gx', 'gy'), split_axis=0, concat_axis=0, tiled=T...  14.7 us
    pallas_call x1, Pallas kernels, turn(): pl.pallas_call(turn_kernel, grid=(FIELDS + 2,), in_specs=[pl.BlockSpec((L...  8.07 us
    pallas_call x1, Pallas kernels, chem(): pl.pallas_call(chem_kernel, in_specs=[VMEM] * 5, out_specs=HBM, out_shape...  7.75 us
    ppermute x2, starting transfers between devices, swap(): lax.ppermute(row_hi, 'gx', up)  7.65 us
    ppermute x2, starting transfers between devices, swap(): lax.ppermute(col_hi, 'gy', right)  5.37 us
  transfers between devices with their start and end apart: 9, of which 1 were waited for; matrix products, arithmetic and copies ran while one was open for 0% of the time, Pallas kernels for 24%

profile of v1, /device:TPU:1, one launch (start us, length us, event | category | flops | bytes accessed | tf_op | source)
XLA Modules:
  0.0 130.7 jit_solution(18100836650608230910)
XLA Ops:
  0.6 0.0 copy-start.17
  0.6 0.0 copy-start.15
  0.7 8.1 %turn.1 = (f32[4,16,128,128]{3,2,1,0:T(8,128)}, f32[2,16,128,128]{3,2,1,0:T(8,128)S(1)}, bf16[128,640]{1,0:T(8,128)(2,1)}, bf16[128,640]{1,0:T(8,128)(2,1)}, bf1...) custom-call(f32[8192,128]{1,0:T(8,128)} %bitcast.29, f32[4096,128]{1,0:T(8,128)} %bitcast.32), custom_call_target="tpu_custom_call" | custom-call | flops 20000000 | bytes 12582912 | tf_op jit(solution)/shard_map/turn/pallas_call | solution.py:105
  8.7 0.0 copy-start.2
  8.7 3.1 %collective-permute-start.2 = (bf16[16,640]{1,0:T(8,128)(2,1)}, bf16[16,640]{1,0:T(8,128)(2,1)}, u32[]{:S(2)}, u32[]{:S(2)}) collective-permute-start(bf16[16,640]{1,0:T(8,128)(2,1)} %get-tuple-element.21), channel_id=1, source_target_pairs={{0,1},{1,2},{2,3},{3,4},{4,5},{5,6},{6,7},{7,8},{8,9},{9,10},{10,1... | collective-permute-start | bytes 61448 | tf_op jit(solution)/shard_map/ppermute | solution.py:708
  11.8 0.0 collective-permute-start.3
  11.8 3.2 %collective-permute-start = (bf16[128,640]{1,0:T(8,128)(2,1)}, bf16[128,640]{1,0:T(8,128)(2,1)S(1)}, u32[]{:S(2)}, u32[]{:S(2)}) collective-permute-start(bf16[128,640]{1,0:T(8,128)(2,1)} %get-tuple-element.19), channel_id=1, source_target_pairs={{0,16},{16,32},{32,48},{48,64},{64,80},{80,96},{96,112},{1,17},{17... | collective-permute-start | bytes 491528 | tf_op jit(solution)/shard_map/ppermute | solution.py:706
  15.0 1.3 collective-permute-start.1
  16.3 0.0 copy-done.17
  16.4 0.0 copy-done.15
  16.4 0.0 copy-start
  16.4 0.0 copy-start.4
  16.4 0.0 copy-start.6
  16.4 0.0 copy-start.10
  16.4 0.0 copy-start.11
  16.4 3.1 %plan.1 = (f32[128,128]{1,0:T(8,128)S(1)}, bf16[2,1024,1024]{2,1,0:T(8,128)(2,1)}, bf16[1024,128]{1,0:T(8,128)(2,1)S(1)}) custom-call(s32[1,2048]{1,0:T(1,128)S(1)} %bitcast.27, s32[2,1024]{1,0:T(2,128)S(1)} %bitcast.25), custom_call_target="tpu_custom_call" | custom-call | flops 3000000000 | bytes 1048576 | tf_op jit(solution)/shard_map/plan/pallas_call | solution.py:178
  19.5 0.0 copy-start.8
  19.6 0.0 copy-done.2
  19.6 0.0 copy-done
  19.6 0.0 copy-done.4
  19.6 0.5 copy-done.6
  20.1 0.0 copy-done.10
  20.1 0.0 copy-done.11
  20.1 12.0 %inner.2.refs_17_ = f32[4,16,128,128]{3,2,1,0:T(8,128)} custom-call(f32[128,128]{1,0:T(8,128)S(1)} %get-tuple-element.18.mask_ref.refs_1_, f32[2,16,128,128]{3,2,1,0:T(8,128)S(1)} %get-tuple-element.24.c_ref.refs_13_.refs_14_, bf16[512,1024]{1,0:T(8,128)(2,1)S(1)} %copy-done.4, f32[1,1024]{1,0:T(1,128)S(1)} %bitcast.17, bf16[1024,1024]{1,0:T(8,128)(2,1)S(1)} %copy-done, ...), custom_call_target="tpu_custom_call" | custom-call | flops 7500000256 | bytes 4194304 | tf_op jit(solution)/shard_map/inner/pallas_call | solution.py:320
  32.1 0.0 copy-done.8
  32.1 0.1 add_convert_fusion.refs_0_
  32.2 0.0 copy-start.1
  32.2 0.0 copy-start.3
  32.2 0.0 copy-start.5
  32.2 0.0 copy-start.7
  32.2 0.0 collective-permute-done.2.refs_4_.refs_8_
  32.2 0.0 collective-permute-done.3.refs_5_.refs_9_
  32.2 0.0 collective-permute-done.refs_2_.refs_6_
  32.2 0.0 collective-permute-done.1.refs_3_.refs_7_
  32.2 9.1 %rim.1 = (f32[4,16,128,128]{3,2,1,0:T(8,128)}, bf16[128,512]{1,0:T(8,128)(2,1)S(1)}, bf16[128,512]{1,0:T(8,128)(2,1)S(1)}, bf16[16,512]{1,0:T(8,128)(2,1)S(1)}, bf16[16,512]{1,0:T(8,128)(2,1)S(1)}) custom-call(f32[2]{0:T(128)S(1)} %add_convert_fusion.refs_0_, f32[128,128]{1,0:T(8,128)S(1)} %get-tuple-element.18.mask_ref.refs_1_, ...), custom_call_target="tpu_custom_call", output_to_operand_aliasing={{0}: (17, {})} | custom-call | flops 4000000000 | bytes 4194304 | tf_op jit(solution)/shard_map/rim/pallas_call | solution.py:578
  41.4 2.3 %collective-permute-start.6 = (bf16[16,512]{1,0:T(8,128)(2,1)S(1)}, bf16[16,512]{1,0:T(8,128)(2,1)S(1)}, u32[]{:S(2)}, u32[]{:S(2)}) collective-permute-start(bf16[16,512]{1,0:T(8,128)(2,1)S(1)} %get-tuple-element.27), channel_id=1, source_target_pairs={{0,1},{1,2},{2,3},{3,4},{4,5},{5,6},{6,7},{7,8},{8,9},{9,10},{10,1... | collective-permute-start | bytes 49160 | tf_op jit(solution)/shard_map/ppermute | solution.py:708
  43.6 2.2 %collective-permute-start.7 = (bf16[16,512]{1,0:T(8,128)(2,1)S(1)}, bf16[16,512]{1,0:T(8,128)(2,1)S(1)}, u32[]{:S(2)}, u32[]{:S(2)}) collective-permute-start(bf16[16,512]{1,0:T(8,128)(2,1)S(1)} %get-tuple-element.28), channel_id=1, source_target_pairs={{1,0},{2,1},{3,2},{4,3},{5,4},{6,5},{7,6},{8,7},{9,8},{10,9},{11,1... | collective-permute-start | bytes 49160 | tf_op jit(solution)/shard_map/ppermute | solution.py:709
  45.8 4.5 %collective-permute-start.4 = (bf16[128,512]{1,0:T(8,128)(2,1)S(1)}, bf16[128,512]{1,0:T(8,128)(2,1)S(1)}, u32[]{:S(2)}, u32[]{:S(2)}) collective-permute-start(bf16[128,512]{1,0:T(8,128)(2,1)S(1)} %get-tuple-element.25), channel_id=1, source_target_pairs={{0,16},{16,32},{32,48},{48,64},{64,80},{80,96},{96,112},{1,17},{17... | collective-permute-start | bytes 393224 | tf_op jit(solution)/shard_map/ppermute | solution.py:706
  50.3 1.3 collective-permute-start.5
  51.6 0.0 copy-done.1
  51.6 0.0 copy-done.3
  51.6 0.0 copy-done.5
  51.6 0.0 copy-done.7
  51.6 0.0 copy-start.9
  51.6 12.1 %inner.3.refs_19_ = f32[4,16,128,128]{3,2,1,0:T(8,128)} custom-call(f32[128,128]{1,0:T(8,128)S(1)} %get-tuple-element.18.mask_ref.refs_1_, f32[2,16,128,128]{3,2,1,0:T(8,128)S(1)} %copy-done.3, bf16[512,1024]{1,0:T(8,128)(2,1)S(1)} %copy-done.5, f32[1,1024]{1,0:T(1,128)S(1)} %bitcast.19, bf16[1024,1024]{1,0:T(8,128)(2,1)S(1)} %copy-done.1, ...), custom_call_target="tpu_custom_call" | custom-call | flops 7500000256 | bytes 4194304 | tf_op jit(solution)/shard_map/inner/pallas_call | solution.py:320
  63.7 0.0 collective-permute-done.6.refs_4_
  63.7 0.0 collective-permute-done.7.refs_5_
  63.8 0.0 collective-permute-done.4.refs_2_
  63.8 0.0 collective-permute-done.5.refs_3_
  63.8 0.0 copy-done.9
  63.8 10.6 %rim_last.1 = (f32[4,16,128,128]{3,2,1,0:T(8,128)}, bf16[1024,1152]{1,0:T(8,128)(2,1)}) custom-call(f32[2]{0:T(128)S(1)} %add_convert_fusion.refs_0_, f32[128,128]{1,0:T(8,128)S(1)} %get-tuple-element.18.mask_ref.refs_1_, bf16[128,512]{1,0:T(8,128)(2,1)S(1)} %collective-permute-done.4.refs_2_, ...), custom_call_target="tpu_custom_call", output_to_operand_aliasing={{0}: (19, {})} | custom-call | flops 4000000000 | bytes 4194304 | tf_op jit(solution)/shard_map/rim_last/pallas_call | solution.py:578
  74.4 14.7 %all-to-all-start = ((bf16[128,8,1152]{2,1,0:T(8,128)(2,1)}), bf16[128,8,1152]{2,1,0:T(8,128)(2,1)S(1)}, u32[]{:S(2)}, u32[]{:S(2)}) async-start(bf16[128,8,1152]{2,1,0:T(8,128)(2,1)} %bitcast.31), calls=%async_computation | async-start | bytes 4718592 | tf_op jit(solution)/shard_map/all_to_all | solution.py:735
  89.2 0.0 copy-start.12
  89.2 0.0 copy-start.13
  89.2 0.0 copy-start.16
  89.2 4.0 %unturn.1 = f32[8192,128]{1,0:T(8,128)} custom-call(f32[4,16,128,128]{3,2,1,0:T(8,128)} %get-tuple-element.32.t_hbm), custom_call_target="tpu_custom_call" | custom-call | flops 1000000000 | bytes 8388608 | tf_op jit(solution)/shard_map/unturn/pallas_call | solution.py:610
  93.2 28.5 %all-to-all-done = bf16[128,8,1152]{2,1,0:T(8,128)(2,1)S(1)} async-done(((bf16[128,8,1152]{2,1,0:T(8,128)(2,1)}), bf16[128,8,1152]{2,1,0:T(8,128)(2,1)S(1)}, u32[]{:S(2)}, u32[]{:S(2)}) %all-to-all-start) | async-done | bytes 2359328 | tf_op jit(solution)/shard_map/all_to_all | solution.py:735
  121.7 0.0 copy-done.12
  121.7 0.0 copy-done.13
  121.7 0.0 copy-done.16
  121.7 0.0 copy-start.14
  121.7 1.0 copy-done.14
  122.8 7.8 %chem.1 = bf16[2048,256]{1,0:T(8,128)(2,1)} custom-call(bf16[1024,1152]{1,0:T(8,128)(2,1)S(1)} %bitcast.16, bf16[2048,128]{1,0:T(8,128)(2,1)S(1)} %bitcast.26, bf16[256,1024]{1,0:T(8,128)(2,1)S(1)} %copy-done.13, f32[1,1024]{1,0:T(1,128)S(1)} %bitcast.28, bf16[1024,256]{1,0:T(8,128)(2,1)S(1)} %copy-done.14), custom_call_target="tpu_custom_call" | custom-call | flops 4400000000 | bytes 4194304 | tf_op jit(solution)/shard_map/chem/pallas_call | solution.py:672
  (1 shorter events, 0.0 us)
Async XLA Ops:
  0.6 15.7 %copy-start.17 = (s32[2,1,1,1024]{3,2,1,0:T(1,128)S(1)}, s32[2,1,1,1024]{3,2,1,0:T(1,128)}, u32[]{:S(2)}) copy-start(s32[2,1,1,1024]{3,2,1,0:T(1,128)} %param.21) | copy-start | bytes 24580
  0.6 15.7 %copy-start.15 = (s32[1,1,2048]{2,1,0:T(1,128)S(1)}, s32[1,1,2048]{2,1,0:T(1,128)}, u32[]{:S(2)}) copy-start(s32[1,1,2048]{2,1,0:T(1,128)} %param.15) | copy-start | bytes 24580
  8.7 10.8 %copy-start.2 = (f32[2,16,128,128]{3,2,1,0:T(8,128)}, f32[2,16,128,128]{3,2,1,0:T(8,128)S(1)}, u32[]{:S(2)}) copy-start(f32[2,16,128,128]{3,2,1,0:T(8,128)S(1)} %get-tuple-element.24.c_ref.refs_13_.refs_14_) | copy-start | bytes 6291460
  8.7 23.5 %collective-permute-start.2 = (bf16[16,640]{1,0:T(8,128)(2,1)}, bf16[16,640]{1,0:T(8,128)(2,1)}, u32[]{:S(2)}, u32[]{:S(2)}) collective-permute-start(bf16[16,640]{1,0:T(8,128)(2,1)} %get-tuple-element.21), channel_id=1, source_target_pairs={{0,1},{1,2},{2,3},{3,4},{4,5},{5,6},{6,7},{7,8},{8,9},{9,10},{10,1... | collective-permute-start | bytes 61448 | tf_op jit(solution)/shard_map/ppermute | solution.py:708
  11.8 20.4 %collective-permute-start.3 = (bf16[16,640]{1,0:T(8,128)(2,1)}, bf16[16,640]{1,0:T(8,128)(2,1)}, u32[]{:S(2)}, u32[]{:S(2)}) collective-permute-start(bf16[16,640]{1,0:T(8,128)(2,1)} %get-tuple-element.22), channel_id=1, source_target_pairs={{1,0},{2,1},{3,2},{4,3},{5,4},{6,5},{7,6},{8,7},{9,8},{10,9},{11,1... | collective-permute-start | bytes 61448 | tf_op jit(solution)/shard_map/ppermute | solution.py:709
  11.8 20.4 %collective-permute-start = (bf16[128,640]{1,0:T(8,128)(2,1)}, bf16[128,640]{1,0:T(8,128)(2,1)S(1)}, u32[]{:S(2)}, u32[]{:S(2)}) collective-permute-start(bf16[128,640]{1,0:T(8,128)(2,1)} %get-tuple-element.19), channel_id=1, source_target_pairs={{0,16},{16,32},{32,48},{48,64},{64,80},{80,96},{96,112},{1,17},{17... | collective-permute-start | bytes 491528 | tf_op jit(solution)/shard_map/ppermute | solution.py:706
  15.0 17.2 %collective-permute-start.1 = (bf16[128,640]{1,0:T(8,128)(2,1)}, bf16[128,640]{1,0:T(8,128)(2,1)S(1)}, u32[]{:S(2)}, u32[]{:S(2)}) collective-permute-start(bf16[128,640]{1,0:T(8,128)(2,1)} %get-tuple-element.20), channel_id=1, source_target_pairs={{16,0},{32,16},{48,32},{64,48},{80,64},{96,80},{112,96},{17,1},{33... | collective-permute-start | bytes 491528 | tf_op jit(solution)/shard_map/ppermute | solution.py:707
  16.4 3.2 %copy-start = (bf16[1024,1024]{1,0:T(8,128)(2,1)S(1)}, bf16[1024,1024]{1,0:T(8,128)(2,1)}, u32[]{:S(2)}) copy-start(bf16[1024,1024]{1,0:T(8,128)(2,1)} %refs_16_.3) | copy-start | bytes 6291460
  16.4 3.2 %copy-start.4 = (bf16[512,1024]{1,0:T(8,128)(2,1)S(1)}, bf16[512,1024]{1,0:T(8,128)(2,1)}, u32[]{:S(2)}) copy-start(bf16[512,1024]{1,0:T(8,128)(2,1)} %refs_15_.3) | copy-start | bytes 3145732
  16.4 3.7 %copy-start.6 = (bf16[1024,512]{1,0:T(8,128)(2,1)S(1)}, bf16[1024,512]{1,0:T(8,128)(2,1)}, u32[]{:S(2)}) copy-start(bf16[1024,512]{1,0:T(8,128)(2,1)} %refs_17_.1) | copy-start | bytes 3145732
  16.4 3.6 %copy-start.10 = (f32[1024]{0:T(1024)S(1)}, f32[1024]{0:T(1024)}, u32[]{:S(2)}) copy-start(f32[1024]{0:T(1024)} %param.17) | copy-start | bytes 12292
  16.4 3.6 %copy-start.11 = (f32[1024]{0:T(1024)S(1)}, f32[1024]{0:T(1024)}, u32[]{:S(2)}) copy-start(f32[1024]{0:T(1024)} %param.19) | copy-start | bytes 12292
  19.5 12.5 %copy-start.8 = (bf16[1024,128]{1,0:T(8,128)(2,1)}, bf16[1024,128]{1,0:T(8,128)(2,1)S(1)}, u32[]{:S(2)}) copy-start(bf16[1024,128]{1,0:T(8,128)(2,1)S(1)} %get-tuple-element.29.refs_12_) | copy-start | bytes 786436
  32.2 19.4 %copy-start.1 = (bf16[1024,1024]{1,0:T(8,128)(2,1)S(1)}, bf16[1024,1024]{1,0:T(8,128)(2,1)}, u32[]{:S(2)}) copy-start(bf16[1024,1024]{1,0:T(8,128)(2,1)} %refs_16_.3) | copy-start | bytes 6291460
  32.2 19.4 %copy-start.3 = (f32[2,16,128,128]{3,2,1,0:T(8,128)S(1)}, f32[2,16,128,128]{3,2,1,0:T(8,128)}, u32[]{:S(2)}) copy-start(f32[2,16,128,128]{3,2,1,0:T(8,128)} %copy-done.2) | copy-start | bytes 6291460
  32.2 19.4 %copy-start.5 = (bf16[512,1024]{1,0:T(8,128)(2,1)S(1)}, bf16[512,1024]{1,0:T(8,128)(2,1)}, u32[]{:S(2)}) copy-start(bf16[512,1024]{1,0:T(8,128)(2,1)} %refs_15_.3) | copy-start | bytes 3145732
  32.2 19.4 %copy-start.7 = (bf16[1024,512]{1,0:T(8,128)(2,1)S(1)}, bf16[1024,512]{1,0:T(8,128)(2,1)}, u32[]{:S(2)}) copy-start(bf16[1024,512]{1,0:T(8,128)(2,1)} %refs_17_.1) | copy-start | bytes 3145732
  41.4 22.4 %collective-permute-start.6 = (bf16[16,512]{1,0:T(8,128)(2,1)S(1)}, bf16[16,512]{1,0:T(8,128)(2,1)S(1)}, u32[]{:S(2)}, u32[]{:S(2)}) collective-permute-start(bf16[16,512]{1,0:T(8,128)(2,1)S(1)} %get-tuple-element.27), channel_id=1, source_target_pairs={{0,1},{1,2},{2,3},{3,4},{4,5},{5,6},{6,7},{7,8},{8,9},{9,10},{10,1... | collective-permute-start | bytes 49160 | tf_op jit(solution)/shard_map/ppermute | solution.py:708
  43.6 20.1 %collective-permute-start.7 = (bf16[16,512]{1,0:T(8,128)(2,1)S(1)}, bf16[16,512]{1,0:T(8,128)(2,1)S(1)}, u32[]{:S(2)}, u32[]{:S(2)}) collective-permute-start(bf16[16,512]{1,0:T(8,128)(2,1)S(1)} %get-tuple-element.28), channel_id=1, source_target_pairs={{1,0},{2,1},{3,2},{4,3},{5,4},{6,5},{7,6},{8,7},{9,8},{10,9},{11,1... | collective-permute-start | bytes 49160 | tf_op jit(solution)/shard_map/ppermute | solution.py:709
  45.8 17.9 %collective-permute-start.4 = (bf16[128,512]{1,0:T(8,128)(2,1)S(1)}, bf16[128,512]{1,0:T(8,128)(2,1)S(1)}, u32[]{:S(2)}, u32[]{:S(2)}) collective-permute-start(bf16[128,512]{1,0:T(8,128)(2,1)S(1)} %get-tuple-element.25), channel_id=1, source_target_pairs={{0,16},{16,32},{32,48},{48,64},{64,80},{80,96},{96,112},{1,17},{17... | collective-permute-start | bytes 393224 | tf_op jit(solution)/shard_map/ppermute | solution.py:706
  50.3 13.5 %collective-permute-start.5 = (bf16[128,512]{1,0:T(8,128)(2,1)S(1)}, bf16[128,512]{1,0:T(8,128)(2,1)S(1)}, u32[]{:S(2)}, u32[]{:S(2)}) collective-permute-start(bf16[128,512]{1,0:T(8,128)(2,1)S(1)} %get-tuple-element.26), channel_id=1, source_target_pairs={{16,0},{32,16},{48,32},{64,48},{80,64},{96,80},{112,96},{17,1},{33... | collective-permute-start | bytes 393224 | tf_op jit(solution)/shard_map/ppermute | solution.py:707
  51.6 12.2 %copy-start.9 = (bf16[1024,128]{1,0:T(8,128)(2,1)S(1)}, bf16[1024,128]{1,0:T(8,128)(2,1)}, u32[]{:S(2)}) copy-start(bf16[1024,128]{1,0:T(8,128)(2,1)} %copy-done.8) | copy-start | bytes 786436
  74.4 47.3 %all-to-all-start = ((bf16[128,8,1152]{2,1,0:T(8,128)(2,1)}), bf16[128,8,1152]{2,1,0:T(8,128)(2,1)S(1)}, u32[]{:S(2)}, u32[]{:S(2)}) async-start(bf16[128,8,1152]{2,1,0:T(8,128)(2,1)} %bitcast.31), calls=%async_computation | async-start | bytes 4718592 | tf_op jit(solution)/shard_map/all_to_all | solution.py:735
  89.2 32.5 %copy-start.12 = (bf16[1,1,16,128,128]{4,3,2,1,0:T(8,128)(2,1)S(1)}, bf16[1,1,16,128,128]{4,3,2,1,0:T(8,128)(2,1)}, u32[]{:S(2)}) copy-start(bf16[1,1,16,128,128]{4,3,2,1,0:T(8,128)(2,1)} %param.22) | copy-start | bytes 1572868
  89.2 32.5 %copy-start.13 = (bf16[256,1024]{1,0:T(8,128)(2,1)S(1)}, bf16[256,1024]{1,0:T(8,128)(2,1)}, u32[]{:S(2)}) copy-start(bf16[256,1024]{1,0:T(8,128)(2,1)} %w1_ref.5) | copy-start | bytes 1572868
  89.2 32.5 %copy-start.16 = (f32[1024]{0:T(1024)S(1)}, f32[1024]{0:T(1024)}, u32[]{:S(2)}) copy-start(f32[1024]{0:T(1024)} %param.24) | copy-start | bytes 12292
  121.7 1.0 copy-start.14

commit v2 on v1

v2 whole, which is shorter than its diff:
```python
import jax
import jax.numpy as jnp
from jax import lax
from jax.experimental import pallas as pl
from jax.experimental.pallas import tpu as pltpu
from jax.sharding import PartitionSpec as P

F32 = jnp.float32
BF16 = jnp.bfloat16
LANES = 128
FIELDS = 4
ROWS = 16
COLS = 128
FEAT = FIELDS * LANES
CELLS = ROWS * COLS
SEGS = CELLS // 2
EDGE = 8
GROUP = 4
MIB = 1024 * 1024

VMEM = pl.BlockSpec(memory_space=pltpu.VMEM)
SMEM = pl.BlockSpec(memory_space=pltpu.SMEM)
ANY = pl.BlockSpec(memory_space=pl.ANY)


HBM = pl.BlockSpec(memory_space=pltpu.HBM)


def hbm_out(shape, dtype):
    return pltpu.HBM(shape, dtype)


def in_vmem(x):
    return pltpu.with_memory_space_constraint(x, pltpu.VMEM)


def in_hbm(x):
    return pltpu.with_memory_space_constraint(x, pltpu.HBM)


def params(mib):
    return pltpu.CompilerParams(vmem_limit_bytes=mib * MIB)


def cost(flops, bytes_accessed=0):
    return pl.CostEstimate(flops=flops, bytes_accessed=bytes_accessed, transcendentals=0)


def dot(a, b):
    return jnp.dot(a, b, preferred_element_type=F32)


def dot_nt(a, b):
    return lax.dot_general(a, b, (((1,), (1,)), ((), ())), preferred_element_type=F32)


def silu(u):
    half = 0.5 * u
    return half + half * jnp.tanh(half)


def iota(shape, dim):
    return lax.broadcasted_iota(jnp.int32, shape, dim)


def turn_kernel(f_ref, c_ref, t_ref, cc_ref, row_lo_ref, row_hi_ref, col_lo_ref, col_hi_ref):
    step = pl.program_id(0)

    @pl.when(step < FIELDS)
    def _():
        for r in range(ROWS):
            block = f_ref[pl.ds(r, LANES, stride=ROWS), :].T
            t_ref[0, r] = block
            if r == 0:
                row_lo_ref[...] = block.astype(BF16)
            if r == ROWS - 1:
                row_hi_ref[...] = block.astype(BF16)
        col_lo_ref[...] = t_ref[0, :, 0, :].astype(BF16)
        col_hi_ref[...] = t_ref[0, :, COLS - 1, :].astype(BF16)

    @pl.when(step >= FIELDS)
    def _():
        for r in range(ROWS):
            cc_ref[0, r] = c_ref[pl.ds(r, LANES, stride=ROWS), :].T

    @pl.when(step == FIELDS)
    def _():
        row_lo_ref[...] = cc_ref[0, 0].astype(BF16)
        row_hi_ref[...] = cc_ref[0, ROWS - 1].astype(BF16)

    @pl.when(step == FIELDS + 1)
    def _():
        col_lo_ref[...] = cc_ref[0, :, 0, :].astype(BF16)
        col_hi_ref[...] = cc_ref[0, :, COLS - 1, :].astype(BF16)


def turn(fields, courant):
    flat_f = in_hbm(fields.reshape(FIELDS * LANES * ROWS, COLS))
    flat_c = in_hbm(courant.reshape(2 * LANES * ROWS, COLS))
    field_at = lambda i: jnp.minimum(i, FIELDS - 1)
    speed_at = lambda i: jnp.maximum(i - FIELDS, 0)
    halo_at = lambda i: jnp.minimum(i, FIELDS)
    return pl.pallas_call(
        turn_kernel,
        grid=(FIELDS + 2,),
        in_specs=[
            pl.BlockSpec((LANES * ROWS, COLS), lambda i: (field_at(i), 0)),
            pl.BlockSpec((LANES * ROWS, COLS), lambda i: (speed_at(i), 0)),
        ],
        out_specs=[
            pl.BlockSpec((1, ROWS, COLS, LANES), lambda i: (field_at(i), 0, 0, 0)),
            pl.BlockSpec((1, ROWS, COLS, LANES), lambda i: (speed_at(i), 0, 0, 0)),
            pl.BlockSpec((COLS, LANES), lambda i: (0, halo_at(i))),
            pl.BlockSpec((COLS, LANES), lambda i: (0, halo_at(i))),
            pl.BlockSpec((ROWS, LANES), lambda i: (0, halo_at(i))),
            pl.BlockSpec((ROWS, LANES), lambda i: (0, halo_at(i))),
        ],
        out_shape=[
            jax.ShapeDtypeStruct((FIELDS, ROWS, COLS, LANES), F32),
            jax.ShapeDtypeStruct((2, ROWS, COLS, LANES), F32),
            jax.ShapeDtypeStruct((COLS, FEAT + LANES), BF16),
            jax.ShapeDtypeStruct((COLS, FEAT + LANES), BF16),
            jax.ShapeDtypeStruct((ROWS, FEAT + LANES), BF16),
            jax.ShapeDtypeStruct((ROWS, FEAT + LANES), BF16),
        ],
        compiler_params=params(14),
        cost_estimate=cost(20_000_000, 12 << 20),
        name="turn",
    )(flat_f, flat_c)


def plan_kernel(sun_ref, route_ref, mask_ref, place_ref, tags_ref, stage_ref, sems):
    slots = sun_ref[...]
    low = (iota((COLS, CELLS), 0) == (slots & (COLS - 1))).astype(F32).astype(BF16)
    high = (iota((LANES, CELLS), 0) == (slots >> 7)).astype(F32).astype(BF16)
    lit = dot_nt(low, high)
    mask_ref[...] = lit

    target = route_ref[0, 0]
    arrival = route_ref[1, 0] + 1
    before = (iota((LANES, LANES), 0) < iota((LANES, LANES), 1)).astype(F32).astype(BF16)
    ones = jnp.ones((LANES, LANES), BF16)
    carry = jnp.zeros((LANES, LANES), F32)
    ranks = []
    for b in range(SEGS // LANES):
        goes = (iota((LANES, LANES), 0) == target[:, b * LANES : (b + 1) * LANES]).astype(F32)
        goes16 = goes.astype(BF16)
        ranks.append(jnp.sum(goes * (dot(goes16, before) + carry), axis=0, keepdims=True))
        carry = carry + dot(goes16, ones)
    rank = jnp.concatenate(ranks, axis=1).astype(jnp.int32)
    row = target * 16 + rank
    index = iota((LANES, SEGS), 0)
    coarse = (arrival >> 5).astype(F32)
    fine = (arrival & 31).astype(F32)
    tag_rows = [
        jnp.where(index == 2 * q, coarse, jnp.where(index == 2 * q + 1, fine, 0.0)).astype(BF16)
        for q in range(2)
    ]
    for b in range(SEGS // LANES):
        tags = jnp.zeros((LANES, LANES), F32)
        for q in range(2):
            want = 2 * (iota((LANES, SEGS), 0) + b * LANES) + q
            chosen = (row == want).astype(F32).astype(BF16)
            at = (q, slice(b * LANES, (b + 1) * LANES))
            stage_ref[at] = chosen
            pltpu.make_async_copy(stage_ref.at[at], place_ref.at[at], sems.at[q, b]).start()
            tags = tags + dot_nt(chosen, tag_rows[q])
        tags_ref[b * LANES : (b + 1) * LANES, :] = tags.astype(BF16)
    for b in range(SEGS // LANES):
        for q in range(2):
            at = (q, slice(b * LANES, (b + 1) * LANES))
            pltpu.make_async_copy(stage_ref.at[at], place_ref.at[at], sems.at[q, b]).wait()


def plan(sun_columns, segment_route):
    return pl.pallas_call(
        plan_kernel,
        in_specs=[VMEM] * 2,
        out_specs=[VMEM, ANY, VMEM],
        out_shape=[
            jax.ShapeDtypeStruct((COLS, LANES), F32),
            jax.ShapeDtypeStruct((2, SEGS, SEGS), BF16),
            jax.ShapeDtypeStruct((SEGS, LANES), BF16),
        ],
        scratch_shapes=[
            pltpu.VMEM((2, SEGS, SEGS), BF16),
            pltpu.SemaphoreType.DMA((2, SEGS // LANES)),
        ],
        compiler_params=params(10),
        cost_estimate=cost(3_000_000_000, 1 << 20),
        name="plan",
    )(sun_columns.reshape(1, CELLS), segment_route)


def weights_of(lo0, mid0, hi0, left1, mid1, right1):
    f_lo = 0.5 * (lo0 + mid0)
    f_hi = 0.5 * (mid0 + hi0)
    g_lo = 0.5 * (left1 + mid1)
    g_hi = 0.5 * (mid1 + right1)
    keep = (
        1.0
        - jnp.maximum(f_hi, 0.0)
        + jnp.minimum(f_lo, 0.0)
        - jnp.maximum(g_hi, 0.0)
        + jnp.minimum(g_lo, 0.0)
    )
    return (
        keep,
        jnp.maximum(f_lo, 0.0),
        -jnp.minimum(f_hi, 0.0),
        jnp.maximum(g_lo, 0.0),
        -jnp.minimum(g_hi, 0.0),
    )


def combine(k, mid, lo, hi, left, right):
    return k[0] * mid + k[1] * lo + k[2] * hi + k[3] * left + k[4] * right


def net(x, h1_ref, h2_ref, w1_ref, b1_ref, w2_ref, b2_ref, w3_ref, emit):
    hidden = w2_ref.shape[0]
    wide = 256
    for n in range(0, hidden, wide):
        u = dot(x, w1_ref[:, n : n + wide]) + b1_ref[:, n : n + wide]
        h1_ref[:, n : n + wide] = silu(u).astype(BF16)
    h1 = h1_ref[...]
    for n in range(0, hidden, wide):
        u = dot(h1, w2_ref[:, n : n + wide]) + b2_ref[:, n : n + wide]
        h2_ref[:, n : n + wide] = silu(u).astype(BF16)
    h2 = h2_ref[...]
    for n in range(0, FEAT, wide):
        emit(n, dot(h2, w3_ref[:, n : n + wide]))


def step_kernel(
    last,
    mask_ref,
    row_lo_ref, row_hi_ref, col_lo_ref, col_hi_ref,
    crow_lo_ref, crow_hi_ref, ccol_lo_ref, ccol_hi_ref,
    w1_ref, b1_ref, w2_ref, b2_ref, w3_ref, *rest,
):
    if last:
        tags_ref, t_any, c_any, place_any, out_any, pack_any = rest[:6]
        rest = rest[6:]
    else:
        t_any, c_any, out_any, srow_lo_ref, srow_hi_ref, scol_lo_ref, scol_hi_ref = rest[:7]
        rest = rest[7:]
    v_ref, c_ref, lit_ref, out_ref, x_ref, adv_ref, h1_ref, h2_ref, t_sems, c_sems, out_sems = rest[:11]
    if last:
        place_ref, pack_ref, place_sem, pack_sems = rest[11:]
    mid = slice(EDGE, EDGE + COLS)
    left = slice(EDGE - 1, EDGE + COLS - 1)
    right = slice(EDGE + 1, EDGE + COLS + 1)
    inside = pl.ds(EDGE, COLS)

    def load(r):
        return (
            pltpu.make_async_copy(t_any.at[:, r], v_ref.at[:, r + 1, inside], t_sems.at[r]),
            pltpu.make_async_copy(c_any.at[:, r], c_ref.at[:, r + 1, inside], c_sems.at[r]),
        )

    def store(g):
        rows = pl.ds(g * GROUP, GROUP)
        return pltpu.make_async_copy(out_ref.at[:, rows], out_any.at[:, rows], out_sems.at[g])

    first, final = 0, ROWS - 1
    order = [first, final] + list(range(1, ROWS - 1))
    for r in order:
        for copy in load(r):
            copy.start()
    if last:
        place_load = pltpu.make_async_copy(place_any, place_ref, place_sem.at[0])
        place_load.start()

    speed_at = slice(FEAT, FEAT + LANES)
    for f in range(FIELDS):
        at = slice(f * LANES, (f + 1) * LANES)
        v_ref[f, 0, mid, :] = row_lo_ref[:, at].astype(F32)
        v_ref[f, ROWS + 1, mid, :] = row_hi_ref[:, at].astype(F32)
        low = col_lo_ref[:, at].astype(F32)
        high = col_hi_ref[:, at].astype(F32)
        for r in range(ROWS):
            v_ref[f, r + 1, EDGE - 1 : EDGE, :] = low[r : r + 1, :]
            v_ref[f, r + 1, EDGE + COLS : EDGE + COLS + 1, :] = high[r : r + 1, :]
    low = ccol_lo_ref[:, speed_at].astype(F32)
    high = ccol_hi_ref[:, speed_at].astype(F32)
    for r in range(ROWS):
        c_ref[1, r + 1, EDGE - 1 : EDGE, :] = low[r : r + 1, :]
        c_ref[1, r + 1, EDGE + COLS : EDGE + COLS + 1, :] = high[r : r + 1, :]
        lit_ref[r] = jnp.broadcast_to(mask_ref[:, r : r + 1], (COLS, LANES))
    for r in (first, final):
        for copy in load(r):
            copy.wait()
    for spot, held, halo_ref, flag in (
        (0, 1, crow_lo_ref, lax.axis_index("gx") > 0),
        (ROWS + 1, ROWS, crow_hi_ref, lax.axis_index("gx") < lax.axis_size("gx") - 1),
    ):
        halo = halo_ref[:, speed_at].astype(F32)
        c_ref[0, spot, mid, :] = jnp.where(flag, halo, -c_ref[0, held, mid, :])

    def body(g, carry):
        for j in range(GROUP):
            r = g * GROUP + 1 + j

            def arrive():
                for copy in load(r):
                    copy.wait()

            if j < GROUP - 2:
                arrive()
            else:
                pl.when(r < final)(arrive)
        for j in range(GROUP):
            r = g * GROUP + j + 1
            k = weights_of(
                c_ref[0, r - 1, mid, :], c_ref[0, r, mid, :], c_ref[0, r + 1, mid, :],
                c_ref[1, r, left, :], c_ref[1, r, mid, :], c_ref[1, r, right, :],
            )
            for f in range(FIELDS):
                at = slice(f * LANES, (f + 1) * LANES)
                moved = combine(
                    k, v_ref[f, r, mid, :], v_ref[f, r - 1, mid, :], v_ref[f, r + 1, mid, :],
                    v_ref[f, r, left, :], v_ref[f, r, right, :],
                )
                adv_ref[j * COLS : (j + 1) * COLS, at] = moved
                x_ref[j * COLS : (j + 1) * COLS, at] = moved.astype(BF16)

        def emit(n, heat):
            for j in range(GROUP):
                r = g * GROUP + j
                for m in range(0, heat.shape[1], LANES):
                    here = slice(j * COLS, (j + 1) * COLS)
                    out_ref[(n + m) // LANES, r] = (
                        adv_ref[here, n + m : n + m + LANES] + lit_ref[r] * heat[here, m : m + LANES]
                    )

        net(x_ref[...], h1_ref, h2_ref, w1_ref, b1_ref, w2_ref, b2_ref, w3_ref, emit)
        store(g).start()
        return carry

    lax.fori_loop(0, ROWS // GROUP, body, 0)
    stores = [store(g) for g in range(ROWS // GROUP)]

    if not last:
        for f in range(FIELDS):
            at = slice(f * LANES, (f + 1) * LANES)
            srow_lo_ref[:, at] = out_ref[f, 0].astype(BF16)
            srow_hi_ref[:, at] = out_ref[f, ROWS - 1].astype(BF16)
            scol_lo_ref[:, at] = out_ref[f, :, 0].astype(BF16)
            scol_hi_ref[:, at] = out_ref[f, :, COLS - 1].astype(BF16)
        for copy in stores:
            copy.wait()
        return
    place_load.wait()
    flat = out_ref.reshape(FIELDS * CELLS, LANES)
    half = FEAT // 2
    columns = [
        jnp.concatenate(
            [flat[pl.ds(f * CELLS + c, SEGS, stride=2), :] for f in (2, 3)], axis=1
        ).astype(BF16)
        for c in range(2)
    ]
    pack_ref[:, 2 * FEAT :] = tags_ref[...]
    for i, b in enumerate(range(0, SEGS, 256)):
        for q in range(2):
            for c in range(2):
                pack_ref[b : b + 256, q * FEAT + c * half : q * FEAT + (c + 1) * half] = dot(
                    place_ref[q, b : b + 256, :], columns[c]
                ).astype(BF16)
        at = pl.ds(b, 256)
        stores.append(pltpu.make_async_copy(pack_ref.at[at], pack_any.at[at], pack_sems.at[i]))
        stores[-1].start()
    for copy in stores:
        copy.wait()


def step(last, state, speeds, mask, halo, speed_halo, weights, extra):
    w1, b1, w2, b2, w3 = weights
    hidden = w2.shape[0]
    many = GROUP * COLS
    near = (mask, *halo, *speed_halo, in_vmem(w1), b1, in_vmem(w2), b2, in_vmem(w3))
    far = (state, speeds)
    outs = [jax.ShapeDtypeStruct((FIELDS, ROWS, COLS, LANES), F32)]
    scratch = [
        pltpu.VMEM((FIELDS, ROWS + 2, COLS + 2 * EDGE, LANES), F32),
        pltpu.VMEM((2, ROWS + 2, COLS + 2 * EDGE, LANES), F32),
        pltpu.VMEM((ROWS, COLS, LANES), F32),
        pltpu.VMEM((FIELDS, ROWS, COLS, LANES), F32),
        pltpu.VMEM((many, FEAT), BF16),
        pltpu.VMEM((many, FEAT), F32),
        pltpu.VMEM((many, hidden), BF16),
        pltpu.VMEM((many, hidden), BF16),
        pltpu.SemaphoreType.DMA((ROWS,)),
        pltpu.SemaphoreType.DMA((ROWS,)),
        pltpu.SemaphoreType.DMA((ROWS // GROUP,)),
    ]
    if last:
        place, tags = extra
        near += (tags,)
        far += (place,)
        outs = [hbm_out((FIELDS, ROWS, COLS, LANES), F32)]
        outs += [jax.ShapeDtypeStruct((SEGS, 2 * FEAT + LANES), BF16)]
        out_specs = [HBM, ANY]
        scratch += [
            pltpu.VMEM((2, SEGS, SEGS), BF16),
            pltpu.VMEM((SEGS, 2 * FEAT + LANES), BF16),
            pltpu.SemaphoreType.DMA((1,)),
            pltpu.SemaphoreType.DMA((SEGS // 256,)),
        ]
    else:
        outs += [jax.ShapeDtypeStruct((COLS, FEAT), BF16)] * 2
        outs += [jax.ShapeDtypeStruct((ROWS, FEAT), BF16)] * 2
        out_specs = [ANY] + [VMEM] * 4
    return pl.pallas_call(
        lambda *refs: step_kernel(last, *refs),
        in_specs=[VMEM] * len(near) + [ANY] * len(far),
        out_specs=out_specs,
        out_shape=outs,
        scratch_shapes=scratch,
        compiler_params=params(30 if last else 22),
        cost_estimate=cost(10_000_000_000, 4 << 20),
        name="step_last" if last else "step",
    )(*near, *far)


def unturn_kernel(t_hbm, out_ref, t_ref, stage_ref, in_sems, sems):
    size = LANES * ROWS
    loads = [pltpu.make_async_copy(t_hbm.at[f], t_ref.at[f], in_sems.at[f]) for f in range(FIELDS)]
    stores = [
        pltpu.make_async_copy(stage_ref.at[f], out_ref.at[pl.ds(f * size, size)], sems.at[f])
        for f in range(FIELDS)
    ]
    for load in loads:
        load.start()
    for f in range(FIELDS):
        loads[f].wait()
        for r in range(ROWS):
            stage_ref[f, pl.ds(r, LANES, stride=ROWS), :] = t_ref[f, r].T
        stores[f].start()
    for store in stores:
        store.wait()


def unturn(state):
    return pl.pallas_call(
        unturn_kernel,
        in_specs=[HBM],
        out_specs=HBM,
        out_shape=hbm_out((FIELDS * LANES * ROWS, COLS), F32),
        scratch_shapes=[
            pltpu.VMEM((FIELDS, ROWS, COLS, LANES), F32),
            pltpu.VMEM((FIELDS, LANES * ROWS, COLS), F32),
            pltpu.SemaphoreType.DMA((FIELDS,)),
            pltpu.SemaphoreType.DMA((FIELDS,)),
        ],
        compiler_params=params(12),
        cost_estimate=cost(1_000_000_000, 8 << 20),
        name="unturn",
    )(in_hbm(state))


def chem_kernel(
    arr_ref, regrid_ref, w1_ref, b1_ref, w2_hbm, out_hbm,
    want_ref, mix_ref, x_ref, h_ref, out_ref, w2_ref, sems, w_sem,
):
    w2_load = pltpu.make_async_copy(w2_hbm, w2_ref, w_sem.at[0])
    w2_load.start()
    from_cell = iota((LANES, LANES), 0)
    to_lane = iota((LANES, LANES), 1)
    source_cell = jnp.where(to_lane < 64, 2 * to_lane, 2 * (to_lane - 64) + 1)
    split = (from_cell == source_cell).astype(F32).astype(BF16)
    mix_ref[...] = dot(regrid_ref[...], split).astype(BF16)
    lane = iota((8, LANES), 1)
    which = iota((8, LANES), 0)
    pick = jnp.where(lane == 2 * which, 32.0, jnp.where(lane == 2 * which + 1, 1.0, 0.0))
    pick = jnp.where(which < 2, pick, 0.0).astype(BF16)
    want_ref[...] = dot_nt(pick, arr_ref[:, 2 * FEAT :]).astype(jnp.int32) - 1
    span = 256
    half = FEAT // 2
    stores = []
    for i in range(SEGS // span):
        start = i * span
        placed = []
        for q in range(2):
            chosen = (iota((span, SEGS), 0) + start == want_ref[q : q + 1, :]).astype(F32).astype(BF16)
            placed.append(dot(chosen, arr_ref[:, q * FEAT : (q + 1) * FEAT]))
        placed = (placed[0] + placed[1]).astype(BF16)
        for b in range(span // 64):
            cells = jnp.concatenate(
                [placed[b * 64 : (b + 1) * 64, :half], placed[b * 64 : (b + 1) * 64, half:]], axis=0
            )
            spot = 2 * start + b * LANES
            x_ref[i % 2, b * LANES : (b + 1) * LANES, :] = dot(
                mix_ref[spot : spot + LANES, :], cells
            ).astype(BF16)
        x = x_ref[i % 2]
        for n in range(0, w1_ref.shape[1], 256):
            u = dot(x, w1_ref[:, n : n + 256]) + b1_ref[:, n : n + 256]
            h_ref[i % 2, :, n : n + 256] = silu(u).astype(BF16)
        if i == 0:
            w2_load.wait()
        rows = slice(2 * start, 2 * (start + span))
        out_ref[rows, :] = dot(h_ref[i % 2], w2_ref[...]).astype(BF16)
        at = pl.ds(2 * start, 2 * span)
        stores.append(pltpu.make_async_copy(out_ref.at[at], out_hbm.at[at], sems.at[i]))
        stores[-1].start()
    for store in stores:
        store.wait()


def chem(arrived, regrid_weights, w1, b1, w2):
    return pl.pallas_call(
        chem_kernel,
        in_specs=[VMEM] * 4 + [HBM],
        out_specs=HBM,
        out_shape=hbm_out((CELLS, w2.shape[1]), BF16),
        scratch_shapes=[
            pltpu.VMEM((8, SEGS), jnp.int32),
            pltpu.VMEM((CELLS, LANES), BF16),
            pltpu.VMEM((2, 512, FEAT // 2), BF16),
            pltpu.VMEM((2, 512, w1.shape[1]), BF16),
            pltpu.VMEM((CELLS, w2.shape[1]), BF16),
            pltpu.VMEM(w2.shape, BF16),
            pltpu.SemaphoreType.DMA((SEGS // 256,)),
            pltpu.SemaphoreType.DMA((1,)),
        ],
        compiler_params=params(14),
        cost_estimate=cost(4_400_000_000, 4 << 20),
        name="chem",
    )(
        in_vmem(arrived),
        in_vmem(regrid_weights.reshape(CELLS, LANES)),
        in_vmem(w1),
        b1,
        in_hbm(w2),
    )


def swap(low, high):
    rows, columns = lax.axis_size("gx"), lax.axis_size("gy")
    up = [(i, i + 1) for i in range(rows - 1)]
    down = [(i + 1, i) for i in range(rows - 1)]
    right = [(i, (i + 1) % columns) for i in range(columns)]
    left = [((i + 1) % columns, i) for i in range(columns)]
    row_lo, col_lo = low
    row_hi, col_hi = high
    return (
        lax.ppermute(row_hi, "gx", up),
        lax.ppermute(row_lo, "gx", down),
        lax.ppermute(col_hi, "gy", right),
        lax.ppermute(col_lo, "gy", left),
    )


def local(
    fields, courant, sun_columns, rad_w1, rad_b1, rad_w2, rad_b2, rad_w3,
    segment_route, regrid_weights, chem_w1, chem_b1, chem_w2,
):
    weights = (rad_w1, rad_b1.reshape(1, -1), rad_w2, rad_b2.reshape(1, -1), rad_w3)

    state, speeds, row_lo, row_hi, col_lo, col_hi = turn(fields, courant)
    speed_halo = swap((row_lo, col_lo), (row_hi, col_hi))
    mask, place, tags = plan(sun_columns, segment_route)
    state, row_lo, row_hi, col_lo, col_hi = step(
        False, state, speeds, mask, speed_halo, speed_halo, weights, ()
    )
    halo = swap((row_lo, col_lo), (row_hi, col_hi))
    state, packed = step(
        True, state, speeds, mask, halo, speed_halo, weights, (place, tags)
    )
    tiles = lax.axis_size("gx") * lax.axis_size("gy")
    packed = packed.reshape(tiles, SEGS // tiles, packed.shape[1])
    arrived = lax.all_to_all(packed, ("gx", "gy"), split_axis=0, concat_axis=0, tiled=True)
    fields_out = unturn(state).reshape(fields.shape)
    output = chem(
        arrived.reshape(SEGS, arrived.shape[2]), regrid_weights, chem_w1, chem_b1.reshape(1, -1), chem_w2
    )
    return fields_out, output.reshape(1, 1, CELLS, -1)


def solution(mesh):
    return jax.shard_map(
        local,
        mesh=mesh,
        in_specs=(
            P(None, None, "gx", "gy"),
            P(None, None, "gx", "gy"),
            P("gx", "gy", None),
            P(),
            P(),
            P(),
            P(),
            P(),
            P(None, "gx", "gy", None),
            P("gx", "gy", None, None, None),
            P(),
            P(),
            P(),
        ),
        out_specs=(P(None, None, "gx", "gy"), P("gx", "gy", None, None)),
        check_vma=False,
    )
```

time: 131 us -> 122 us (0.931)
  Pallas kernels: 66.8 us -> 55.3 us
  starting transfers between devices: 32.5 us -> 35.8 us
  local copies, waits for them, and re-layouts: 1.59 us -> 0.06 us
    pallas_call x6 -> x4, Pallas kernels: 54.7 us -> 45.4 us  [the longest x2 32.6 us: step(): pl.pallas_call(lambda *refs: step_kernel(last, *refs), in_specs=[VMEM] *...]
    pallas_call x1, Pallas kernels: 8.07 us -> 5.88 us  [turn(): pl.pallas_call(turn_kernel, grid=(FIELDS + 2,), in_specs=[pl.BlockSpec((L...]
    ppermute x2, starting transfers between devices: 5.37 us -> 7.31 us  [swap(): lax.ppermute(col_hi, 'gy', right)]
    all_to_all x1, starting transfers between devices: 14.7 us -> 16.3 us  [local(): lax.all_to_all(packed, ('gx', 'gy'), split_axis=0, concat_axis=0, tiled=T...]
    unnamed x37 -> x20, local copies, waits for them, and re-layouts: 1.59 us -> 0.06 us
  transfers between devices with their start and end apart: 9 -> 9, of which waited for: 1 -> 4; matrix products, arithmetic and copies ran while one was open for 0% -> 0% of each run, Pallas kernels for 24% -> 7%
where the time goes in v2:
time: 122 us
  Pallas kernels  55.3 us (45%)
  starting transfers between devices  35.8 us (29%)
  waiting for transfers between devices  29.5 us (24%)
    pallas_call x2, Pallas kernels, step(): pl.pallas_call(lambda *refs: step_kernel(last, *refs), in_specs=[VMEM] *...  32.6 us
    all_to_all x1, waiting for transfers between devices, local(): lax.all_to_all(packed, ('gx', 'gy'), split_axis=0, concat_axis=0, tiled=T...  28.5 us
    all_to_all x1, starting transfers between devices, local(): lax.all_to_all(packed, ('gx', 'gy'), split_axis=0, concat_axis=0, tiled=T...  16.3 us
    pallas_call x1, Pallas kernels, chem(): pl.pallas_call(chem_kernel, in_specs=[VMEM] * 4 + [HBM], out_specs=HBM, o...  8.28 us
    ppermute x2, starting transfers between devices, swap(): lax.ppermute(col_hi, 'gy', right)  7.31 us
    ppermute x2, starting transfers between devices, swap(): lax.ppermute(row_hi, 'gx', up)  7.2 us
    pallas_call x1, Pallas kernels, turn(): pl.pallas_call(turn_kernel, grid=(FIELDS + 2,), in_specs=[pl.BlockSpec((L...  5.88 us
    pallas_call x1, Pallas kernels, plan(): pl.pallas_call(plan_kernel, in_specs=[VMEM] * 2, out_specs=[VMEM, ANY, VM...  4.5 us
  transfers between devices with their start and end apart: 9, of which 4 were waited for; matrix products, arithmetic and copies ran while one was open for 0% of the time, Pallas kernels for 7%

profile of v2, /device:TPU:1, one launch (start us, length us, event | category | flops | bytes accessed | tf_op | source)
XLA Modules:
  0.0 121.7 jit_solution(8513849304019102695)
XLA Ops:
  0.6 0.0 copy-start.6
  0.6 0.0 copy-start.5
  0.7 5.9 %turn.1 = (f32[4,16,128,128]{3,2,1,0:T(8,128)S(1)}, f32[2,16,128,128]{3,2,1,0:T(8,128)S(1)}, bf16[128,640]{1,0:T(8,128)(2,1)S(1)}, bf16[128,640]{1,0:T(8,128)(2,...) custom-call(f32[8192,128]{1,0:T(8,128)} %bitcast.19, f32[4096,128]{1,0:T(8,128)} %bitcast.21), custom_call_target="tpu_custom_call" | custom-call | flops 20000000 | bytes 12582912 | tf_op jit(solution)/shard_map/turn/pallas_call | solution.py:103
  6.5 3.1 %collective-permute-start.2 = (bf16[16,640]{1,0:T(8,128)(2,1)S(1)}, bf16[16,640]{1,0:T(8,128)(2,1)S(1)}, u32[]{:S(2)}, u32[]{:S(2)}) collective-permute-start(bf16[16,640]{1,0:T(8,128)(2,1)S(1)} %get-tuple-element.21), channel_id=1, source_target_pairs={{0,1},{1,2},{2,3},{3,4},{4,5},{5,6},{6,7},{7,8},{8,9},{9,10},{10,1... | collective-permute-start | bytes 61448 | tf_op jit(solution)/shard_map/ppermute | solution.py:550
  9.6 0.0 collective-permute-start.3
  9.6 3.2 %collective-permute-start = (bf16[128,640]{1,0:T(8,128)(2,1)S(1)}, bf16[128,640]{1,0:T(8,128)(2,1)S(1)}, u32[]{:S(2)}, u32[]{:S(2)}) collective-permute-start(bf16[128,640]{1,0:T(8,128)(2,1)S(1)} %get-tuple-element.19), channel_id=1, source_target_pairs={{0,16},{16,32},{32,48},{48,64},{64,80},{80,96},{96,112},{1,17},{17... | collective-permute-start | bytes 491528 | tf_op jit(solution)/shard_map/ppermute | solution.py:548
  12.8 1.3 %collective-permute-start.1 = (bf16[128,640]{1,0:T(8,128)(2,1)S(1)}, bf16[128,640]{1,0:T(8,128)(2,1)S(1)}, u32[]{:S(2)}, u32[]{:S(2)}) collective-permute-start(bf16[128,640]{1,0:T(8,128)(2,1)S(1)} %get-tuple-element.20), channel_id=1, source_target_pairs={{16,0},{32,16},{48,32},{64,48},{80,64},{96,80},{112,96},{17,1},{33... | collective-permute-start | bytes 491528 | tf_op jit(solution)/shard_map/ppermute | solution.py:549
  14.1 0.0 copy-done.6
  14.2 0.0 copy-done.5
  14.2 0.0 copy-start
  14.2 0.0 copy-start.1
  14.2 0.0 copy-start.2
  14.2 0.0 copy-start.7
  14.2 0.0 copy-start.8
  14.2 4.5 %plan.1 = (f32[128,128]{1,0:T(8,128)S(1)}, bf16[2,1024,1024]{2,1,0:T(8,128)(2,1)S(1)}, bf16[1024,128]{1,0:T(8,128)(2,1)S(1)}) custom-call(s32[1,2048]{1,0:T(1,128)S(1)} %bitcast.13, s32[2,1,1,1024]{3,2,1,0:T(1,128)S(1)} %copy-done.6), custom_call_target="tpu_custom_call" | custom-call | flops 3000000000 | bytes 1048576 | tf_op jit(solution)/shard_map/plan/pallas_call | solution.py:176
  18.7 0.0 collective-permute-done.2.refs_3_.refs_7_
  18.7 0.0 collective-permute-done.3.refs_4_.refs_8_
  18.8 0.0 collective-permute-done.refs_1_.refs_5_
  18.8 0.1 collective-permute-done.1.refs_2_.refs_6_
  18.9 0.0 copy-done
  18.9 0.0 copy-done.1
  18.9 0.0 copy-done.2
  18.9 0.0 copy-done.7
  18.9 0.0 copy-done.8
  18.9 14.8 %step.1 = (f32[4,16,128,128]{3,2,1,0:T(8,128)S(1)}, bf16[128,512]{1,0:T(8,128)(2,1)S(1)}, bf16[128,512]{1,0:T(8,128)(2,1)S(1)}, bf16[16,512]{1,0:T(8,128)(2,1)S(1)}, bf16[16,512]{1,0:T(8,128)(2,1)S(1)}) custom-call(f32[128,128]{1,0:T(8,128)S(1)} %get-tuple-element.18.refs_0_, bf16[128,640]{1,0:T(8,128)(2,1)S(1)} %collective-permute-done.refs_1_.refs_5_, ...), custom_call_target="tpu_custom_call" | custom-call | flops 10000000000 | bytes 4194304 | tf_op jit(solution)/shard_map/step/pallas_call | solution.py:414
  33.7 4.0 %collective-permute-start.4 = (bf16[128,512]{1,0:T(8,128)(2,1)S(1)}, bf16[128,512]{1,0:T(8,128)(2,1)S(1)}, u32[]{:S(2)}, u32[]{:S(2)}) collective-permute-start(bf16[128,512]{1,0:T(8,128)(2,1)S(1)} %get-tuple-element.25), channel_id=1, source_target_pairs={{0,16},{16,32},{32,48},{48,64},{64,80},{80,96},{96,112},{1,17},{17... | collective-permute-start | bytes 393224 | tf_op jit(solution)/shard_map/ppermute | solution.py:548
  37.7 1.3 %collective-permute-start.5 = (bf16[128,512]{1,0:T(8,128)(2,1)S(1)}, bf16[128,512]{1,0:T(8,128)(2,1)S(1)}, u32[]{:S(2)}, u32[]{:S(2)}) collective-permute-start(bf16[128,512]{1,0:T(8,128)(2,1)S(1)} %get-tuple-element.26), channel_id=1, source_target_pairs={{16,0},{32,16},{48,32},{64,48},{80,64},{96,80},{112,96},{17,1},{33... | collective-permute-start | bytes 393224 | tf_op jit(solution)/shard_map/ppermute | solution.py:549
  39.0 4.2 %collective-permute-start.6 = (bf16[16,512]{1,0:T(8,128)(2,1)S(1)}, bf16[16,512]{1,0:T(8,128)(2,1)S(1)}, u32[]{:S(2)}, u32[]{:S(2)}) collective-permute-start(bf16[16,512]{1,0:T(8,128)(2,1)S(1)} %get-tuple-element.27), channel_id=1, source_target_pairs={{0,1},{1,2},{2,3},{3,4},{4,5},{5,6},{6,7},{7,8},{8,9},{9,10},{10,1... | collective-permute-start | bytes 49160 | tf_op jit(solution)/shard_map/ppermute | solution.py:550
  43.3 2.4 %collective-permute-start.7 = (bf16[16,512]{1,0:T(8,128)(2,1)S(1)}, bf16[16,512]{1,0:T(8,128)(2,1)S(1)}, u32[]{:S(2)}, u32[]{:S(2)}) collective-permute-start(bf16[16,512]{1,0:T(8,128)(2,1)S(1)} %get-tuple-element.28), channel_id=1, source_target_pairs={{1,0},{2,1},{3,2},{4,3},{5,4},{6,5},{7,6},{8,7},{9,8},{10,9},{11,1... | collective-permute-start | bytes 49160 | tf_op jit(solution)/shard_map/ppermute | solution.py:551
  45.6 0.4 collective-permute-done.6.refs_3_
  46.1 0.4 collective-permute-done.7.refs_4_
  46.5 0.0 collective-permute-done.4.refs_1_
  46.5 0.0 collective-permute-done.5.refs_2_
  46.5 17.8 %step_last.1 = (f32[4,16,128,128]{3,2,1,0:T(8,128)}, bf16[1024,1152]{1,0:T(8,128)(2,1)}) custom-call(f32[128,128]{1,0:T(8,128)S(1)} %get-tuple-element.18.refs_0_, bf16[128,512]{1,0:T(8,128)(2,1)S(1)} %collective-permute-done.4.refs_1_, bf16[128,512]{1,0:T(8,128)(2,1)S(1)} %collective-permute-done.5.refs_2_, ...), custom_call_target="tpu_custom_call" | custom-call | flops 10000000000 | bytes 4194304 | tf_op jit(solution)/shard_map/step_last/pallas_call | solution.py:414
  64.3 16.3 %all-to-all-start = ((bf16[128,8,1152]{2,1,0:T(8,128)(2,1)}), bf16[128,8,1152]{2,1,0:T(8,128)(2,1)S(1)}, u32[]{:S(2)}, u32[]{:S(2)}) async-start(bf16[128,8,1152]{2,1,0:T(8,128)(2,1)} %bitcast.6), calls=%async_computation | async-start | bytes 4718592 | tf_op jit(solution)/shard_map/all_to_all | solution.py:573
  80.7 0.0 copy-start.3
  80.7 0.0 copy-start.4
  80.7 0.0 copy-start.9
  80.7 4.0 %unturn.1 = f32[8192,128]{1,0:T(8,128)} custom-call(f32[4,16,128,128]{3,2,1,0:T(8,128)} %get-tuple-element.32.t_hbm), custom_call_target="tpu_custom_call" | custom-call | flops 1000000000 | bytes 8388608 | tf_op jit(solution)/shard_map/unturn/pallas_call | solution.py:445
  84.7 28.5 %all-to-all-done = bf16[128,8,1152]{2,1,0:T(8,128)(2,1)S(1)} async-done(((bf16[128,8,1152]{2,1,0:T(8,128)(2,1)}), bf16[128,8,1152]{2,1,0:T(8,128)(2,1)S(1)}, u32[]{:S(2)}, u32[]{:S(2)}) %all-to-all-start) | async-done | bytes 2359328 | tf_op jit(solution)/shard_map/all_to_all | solution.py:573
  113.2 0.0 copy-done.3
  113.2 0.0 copy-done.4
  113.2 0.0 copy-done.9
  113.2 8.3 %chem.1 = bf16[2048,256]{1,0:T(8,128)(2,1)} custom-call(bf16[1024,1152]{1,0:T(8,128)(2,1)S(1)} %bitcast.11, bf16[2048,128]{1,0:T(8,128)(2,1)S(1)} %bitcast.12, bf16[256,1024]{1,0:T(8,128)(2,1)S(1)} %copy-done.4, f32[1,1024]{1,0:T(1,128)S(1)} %bitcast.18, bf16[1024,256]{1,0:T(8,128)(2,1)} %w2_hbm.1), custom_call_target="tpu_custom_call" | custom-call | flops 4400000000 | bytes 4194304 | tf_op jit(solution)/shard_map/chem/pallas_call | solution.py:512
Async XLA Ops:
  0.6 13.5 %copy-start.6 = (s32[2,1,1,1024]{3,2,1,0:T(1,128)S(1)}, s32[2,1,1,1024]{3,2,1,0:T(1,128)}, u32[]{:S(2)}) copy-start(s32[2,1,1,1024]{3,2,1,0:T(1,128)} %route_ref.1) | copy-start | bytes 24580
  0.6 13.5 %copy-start.5 = (s32[1,1,2048]{2,1,0:T(1,128)S(1)}, s32[1,1,2048]{2,1,0:T(1,128)}, u32[]{:S(2)}) copy-start(s32[1,1,2048]{2,1,0:T(1,128)} %param.15) | copy-start | bytes 24580
  6.5 12.2 %collective-permute-start.2 = (bf16[16,640]{1,0:T(8,128)(2,1)S(1)}, bf16[16,640]{1,0:T(8,128)(2,1)S(1)}, u32[]{:S(2)}, u32[]{:S(2)}) collective-permute-start(bf16[16,640]{1,0:T(8,128)(2,1)S(1)} %get-tuple-element.21), channel_id=1, source_target_pairs={{0,1},{1,2},{2,3},{3,4},{4,5},{5,6},{6,7},{7,8},{8,9},{9,10},{10,1... | collective-permute-start | bytes 61448 | tf_op jit(solution)/shard_map/ppermute | solution.py:550
  9.6 9.1 %collective-permute-start.3 = (bf16[16,640]{1,0:T(8,128)(2,1)S(1)}, bf16[16,640]{1,0:T(8,128)(2,1)S(1)}, u32[]{:S(2)}, u32[]{:S(2)}) collective-permute-start(bf16[16,640]{1,0:T(8,128)(2,1)S(1)} %get-tuple-element.22), channel_id=1, source_target_pairs={{1,0},{2,1},{3,2},{4,3},{5,4},{6,5},{7,6},{8,7},{9,8},{10,9},{11,1... | collective-permute-start | bytes 61448 | tf_op jit(solution)/shard_map/ppermute | solution.py:551
  9.6 9.1 %collective-permute-start = (bf16[128,640]{1,0:T(8,128)(2,1)S(1)}, bf16[128,640]{1,0:T(8,128)(2,1)S(1)}, u32[]{:S(2)}, u32[]{:S(2)}) collective-permute-start(bf16[128,640]{1,0:T(8,128)(2,1)S(1)} %get-tuple-element.19), channel_id=1, source_target_pairs={{0,16},{16,32},{32,48},{48,64},{64,80},{80,96},{96,112},{1,17},{17... | collective-permute-start | bytes 491528 | tf_op jit(solution)/shard_map/ppermute | solution.py:548
  12.8 6.1 %collective-permute-start.1 = (bf16[128,640]{1,0:T(8,128)(2,1)S(1)}, bf16[128,640]{1,0:T(8,128)(2,1)S(1)}, u32[]{:S(2)}, u32[]{:S(2)}) collective-permute-start(bf16[128,640]{1,0:T(8,128)(2,1)S(1)} %get-tuple-element.20), channel_id=1, source_target_pairs={{16,0},{32,16},{48,32},{64,48},{80,64},{96,80},{112,96},{17,1},{33... | collective-permute-start | bytes 491528 | tf_op jit(solution)/shard_map/ppermute | solution.py:549
  14.2 4.7 %copy-start = (bf16[1024,1024]{1,0:T(8,128)(2,1)S(1)}, bf16[1024,1024]{1,0:T(8,128)(2,1)}, u32[]{:S(2)}) copy-start(bf16[1024,1024]{1,0:T(8,128)(2,1)} %refs_11_.3) | copy-start | bytes 6291460
  14.2 4.7 %copy-start.1 = (bf16[512,1024]{1,0:T(8,128)(2,1)S(1)}, bf16[512,1024]{1,0:T(8,128)(2,1)}, u32[]{:S(2)}) copy-start(bf16[512,1024]{1,0:T(8,128)(2,1)} %refs_9_.3) | copy-start | bytes 3145732
  14.2 4.7 %copy-start.2 = (bf16[1024,512]{1,0:T(8,128)(2,1)S(1)}, bf16[1024,512]{1,0:T(8,128)(2,1)}, u32[]{:S(2)}) copy-start(bf16[1024,512]{1,0:T(8,128)(2,1)} %refs_13_.3) | copy-start | bytes 3145732
  14.2 4.7 %copy-start.7 = (f32[1024]{0:T(1024)S(1)}, f32[1024]{0:T(1024)}, u32[]{:S(2)}) copy-start(f32[1024]{0:T(1024)} %param.17) | copy-start | bytes 12292
  14.2 4.7 %copy-start.8 = (f32[1024]{0:T(1024)S(1)}, f32[1024]{0:T(1024)}, u32[]{:S(2)}) copy-start(f32[1024]{0:T(1024)} %param.19) | copy-start | bytes 12292
  33.7 12.8 %collective-permute-start.4 = (bf16[128,512]{1,0:T(8,128)(2,1)S(1)}, bf16[128,512]{1,0:T(8,128)(2,1)S(1)}, u32[]{:S(2)}, u32[]{:S(2)}) collective-permute-start(bf16[128,512]{1,0:T(8,128)(2,1)S(1)} %get-tuple-element.25), channel_id=1, source_target_pairs={{0,16},{16,32},{32,48},{48,64},{64,80},{80,96},{96,112},{1,17},{17... | collective-permute-start | bytes 393224 | tf_op jit(solution)/shard_map/ppermute | solution.py:548
  37.7 8.7 %collective-permute-start.5 = (bf16[128,512]{1,0:T(8,128)(2,1)S(1)}, bf16[128,512]{1,0:T(8,128)(2,1)S(1)}, u32[]{:S(2)}, u32[]{:S(2)}) collective-permute-start(bf16[128,512]{1,0:T(8,128)(2,1)S(1)} %get-tuple-element.26), channel_id=1, source_target_pairs={{16,0},{32,16},{48,32},{64,48},{80,64},{96,80},{112,96},{17,1},{33... | collective-permute-start | bytes 393224 | tf_op jit(solution)/shard_map/ppermute | solution.py:549
  39.0 7.0 %collective-permute-start.6 = (bf16[16,512]{1,0:T(8,128)(2,1)S(1)}, bf16[16,512]{1,0:T(8,128)(2,1)S(1)}, u32[]{:S(2)}, u32[]{:S(2)}) collective-permute-start(bf16[16,512]{1,0:T(8,128)(2,1)S(1)} %get-tuple-element.27), channel_id=1, source_target_pairs={{0,1},{1,2},{2,3},{3,4},{4,5},{5,6},{6,7},{7,8},{8,9},{9,10},{10,1... | collective-permute-start | bytes 49160 | tf_op jit(solution)/shard_map/ppermute | solution.py:550
  43.3 3.2 %collective-permute-start.7 = (bf16[16,512]{1,0:T(8,128)(2,1)S(1)}, bf16[16,512]{1,0:T(8,128)(2,1)S(1)}, u32[]{:S(2)}, u32[]{:S(2)}) collective-permute-start(bf16[16,512]{1,0:T(8,128)(2,1)S(1)} %get-tuple-element.28), channel_id=1, source_target_pairs={{1,0},{2,1},{3,2},{4,3},{5,4},{6,5},{7,6},{8,7},{9,8},{10,9},{11,1... | collective-permute-start | bytes 49160 | tf_op jit(solution)/shard_map/ppermute | solution.py:551
  64.3 48.9 %all-to-all-start = ((bf16[128,8,1152]{2,1,0:T(8,128)(2,1)}), bf16[128,8,1152]{2,1,0:T(8,128)(2,1)S(1)}, u32[]{:S(2)}, u32[]{:S(2)}) async-start(bf16[128,8,1152]{2,1,0:T(8,128)(2,1)} %bitcast.6), calls=%async_computation | async-start | bytes 4718592 | tf_op jit(solution)/shard_map/all_to_all | solution.py:573
  80.7 32.5 %copy-start.3 = (bf16[1,1,16,128,128]{4,3,2,1,0:T(8,128)(2,1)S(1)}, bf16[1,1,16,128,128]{4,3,2,1,0:T(8,128)(2,1)}, u32[]{:S(2)}) copy-start(bf16[1,1,16,128,128]{4,3,2,1,0:T(8,128)(2,1)} %param.22) | copy-start | bytes 1572868
  80.7 32.5 %copy-start.4 = (bf16[256,1024]{1,0:T(8,128)(2,1)S(1)}, bf16[256,1024]{1,0:T(8,128)(2,1)}, u32[]{:S(2)}) copy-start(bf16[256,1024]{1,0:T(8,128)(2,1)} %w1_ref.1) | copy-start | bytes 1572868
  80.7 32.5 %copy-start.9 = (f32[1024]{0:T(1024)S(1)}, f32[1024]{0:T(1024)}, u32[]{:S(2)}) copy-start(f32[1024]{0:T(1024)} %param.24) | copy-start | bytes 12292

commit v3 on v2

v3 whole, which is shorter than its diff:
```python
import jax
import jax.numpy as jnp
from jax import lax
from jax.experimental import pallas as pl
from jax.experimental.pallas import tpu as pltpu
from jax.sharding import PartitionSpec as P

F32 = jnp.float32
BF16 = jnp.bfloat16
LANES = 128
FIELDS = 4
ROWS = 16
COLS = 128
FEAT = FIELDS * LANES
CELLS = ROWS * COLS
SEGS = CELLS // 2
EDGE = 8
GROUP = 4
PIECES = ((1, 4), (5, 4), (9, 3), (12, 3))
INNER = COLS - 2 * EDGE
RIM = 2 * COLS + (ROWS - 2) * 2 * EDGE
MARGIN = (ROWS + 2, COLS + 2 * EDGE, LANES)
MIB = 1024 * 1024

VMEM = pl.BlockSpec(memory_space=pltpu.VMEM)
SMEM = pl.BlockSpec(memory_space=pltpu.SMEM)
ANY = pl.BlockSpec(memory_space=pl.ANY)


HBM = pl.BlockSpec(memory_space=pltpu.HBM)


def vmem_out(shape, dtype):
    return pltpu.VMEM(shape, dtype)


def hbm_out(shape, dtype):
    return pltpu.HBM(shape, dtype)


def in_vmem(x):
    return pltpu.with_memory_space_constraint(x, pltpu.VMEM)


def in_hbm(x):
    return pltpu.with_memory_space_constraint(x, pltpu.HBM)


def params(mib):
    return pltpu.CompilerParams(vmem_limit_bytes=mib * MIB)


def cost(flops, bytes_accessed=0):
    return pl.CostEstimate(flops=flops, bytes_accessed=bytes_accessed, transcendentals=0)


def dot(a, b):
    return jnp.dot(a, b, preferred_element_type=F32)


def dot_nt(a, b):
    return lax.dot_general(a, b, (((1,), (1,)), ((), ())), preferred_element_type=F32)


def silu(u):
    half = 0.5 * u
    return half + half * jnp.tanh(half)


def iota(shape, dim):
    return lax.broadcasted_iota(jnp.int32, shape, dim)


def turn_kernel(f_hbm, c_hbm, t_ref, cc_ref, row_lo_ref, row_hi_ref, col_lo_ref, col_hi_ref, f_ref, c_ref, sems):
    size = LANES * ROWS
    inside = slice(EDGE, EDGE + COLS)
    loads = [
        pltpu.make_async_copy(f_hbm.at[pl.ds(i * size, size)], f_ref.at[i], sems.at[i])
        for i in range(FIELDS)
    ]
    loads += [
        pltpu.make_async_copy(c_hbm.at[pl.ds(i * size, size)], c_ref.at[i], sems.at[FIELDS + i])
        for i in range(2)
    ]
    for load in loads:
        load.start()

    def plane(source, i, target):
        for r in range(ROWS):
            target[i, r + 1, inside, :] = source[i, pl.ds(r, LANES, stride=ROWS), :].T

    for i in range(FIELDS):
        loads[i].wait()
        plane(f_ref, i, t_ref)
        at = slice(i * LANES, (i + 1) * LANES)
        row_lo_ref[:, at] = t_ref[i, 1, inside, :].astype(BF16)
        row_hi_ref[:, at] = t_ref[i, ROWS, inside, :].astype(BF16)
        col_lo_ref[:, at] = t_ref[i, 1 : ROWS + 1, EDGE].astype(BF16)
        col_hi_ref[:, at] = t_ref[i, 1 : ROWS + 1, EDGE + COLS - 1].astype(BF16)
    at = slice(FEAT, FEAT + LANES)
    for i in range(2):
        loads[FIELDS + i].wait()
        plane(c_ref, i, cc_ref)
    row_lo_ref[:, at] = cc_ref[0, 1, inside, :].astype(BF16)
    row_hi_ref[:, at] = cc_ref[0, ROWS, inside, :].astype(BF16)
    col_lo_ref[:, at] = cc_ref[1, 1 : ROWS + 1, EDGE].astype(BF16)
    col_hi_ref[:, at] = cc_ref[1, 1 : ROWS + 1, EDGE + COLS - 1].astype(BF16)


def turn(fields, courant):
    flat_f = in_hbm(fields.reshape(FIELDS * LANES * ROWS, COLS))
    flat_c = in_hbm(courant.reshape(2 * LANES * ROWS, COLS))
    return pl.pallas_call(
        turn_kernel,
        in_specs=[HBM] * 2,
        out_specs=[VMEM] * 6,
        out_shape=[
            vmem_out((FIELDS, *MARGIN), F32),
            vmem_out((2, *MARGIN), F32),
            jax.ShapeDtypeStruct((COLS, FEAT + LANES), BF16),
            jax.ShapeDtypeStruct((COLS, FEAT + LANES), BF16),
            jax.ShapeDtypeStruct((ROWS, FEAT + LANES), BF16),
            jax.ShapeDtypeStruct((ROWS, FEAT + LANES), BF16),
        ],
        scratch_shapes=[
            pltpu.VMEM((FIELDS, LANES * ROWS, COLS), F32),
            pltpu.VMEM((2, LANES * ROWS, COLS), F32),
            pltpu.SemaphoreType.DMA((FIELDS + 2,)),
        ],
        compiler_params=params(14),
        cost_estimate=cost(4_000_000_000, 12 << 20),
        name="turn",
    )(flat_f, flat_c)


def plan_kernel(sun_ref, route_ref, mask_ref, place_ref, tags_ref):
    slots = sun_ref[...]
    low = (iota((COLS, CELLS), 0) == (slots & (COLS - 1))).astype(F32).astype(BF16)
    high = (iota((LANES, CELLS), 0) == (slots >> 7)).astype(F32).astype(BF16)
    lit = dot_nt(low, high)
    for r in range(ROWS):
        mask_ref[r] = jnp.broadcast_to(lit[:, r : r + 1], (COLS, LANES))

    target = route_ref[0, 0]
    arrival = route_ref[1, 0] + 1
    before = (iota((LANES, LANES), 0) < iota((LANES, LANES), 1)).astype(F32).astype(BF16)
    ones = jnp.ones((LANES, LANES), BF16)
    carry = jnp.zeros((LANES, LANES), F32)
    ranks = []
    for b in range(SEGS // LANES):
        goes = (iota((LANES, LANES), 0) == target[:, b * LANES : (b + 1) * LANES]).astype(F32)
        goes16 = goes.astype(BF16)
        ranks.append(jnp.sum(goes * (dot(goes16, before) + carry), axis=0, keepdims=True))
        carry = carry + dot(goes16, ones)
    rank = jnp.concatenate(ranks, axis=1).astype(jnp.int32)
    row = target * 16 + rank
    index = iota((LANES, SEGS), 0)
    coarse = (arrival >> 5).astype(F32)
    fine = (arrival & 31).astype(F32)
    tag_rows = [
        jnp.where(index == 2 * q, coarse, jnp.where(index == 2 * q + 1, fine, 0.0)).astype(BF16)
        for q in range(2)
    ]
    for b in range(SEGS // LANES):
        tags = jnp.zeros((LANES, LANES), F32)
        for q in range(2):
            want = 2 * (iota((LANES, SEGS), 0) + b * LANES) + q
            chosen = (row == want).astype(F32).astype(BF16)
            place_ref[q, b * LANES : (b + 1) * LANES, :] = chosen
            tags = tags + dot_nt(chosen, tag_rows[q])
        tags_ref[b * LANES : (b + 1) * LANES, :] = tags.astype(BF16)


def plan(sun_columns, segment_route):
    return pl.pallas_call(
        plan_kernel,
        in_specs=[VMEM] * 2,
        out_specs=[VMEM] * 3,
        out_shape=[
            vmem_out((ROWS, COLS, LANES), F32),
            vmem_out((2, SEGS, SEGS), BF16),
            vmem_out((SEGS, LANES), BF16),
        ],
        compiler_params=params(10),
        cost_estimate=cost(3_000_000_000, 1 << 20),
        name="plan",
    )(sun_columns.reshape(1, CELLS), segment_route)


def weights_of(lo0, mid0, hi0, left1, mid1, right1):
    f_lo = 0.5 * (lo0 + mid0)
    f_hi = 0.5 * (mid0 + hi0)
    g_lo = 0.5 * (left1 + mid1)
    g_hi = 0.5 * (mid1 + right1)
    keep = (
        1.0
        - jnp.maximum(f_hi, 0.0)
        + jnp.minimum(f_lo, 0.0)
        - jnp.maximum(g_hi, 0.0)
        + jnp.minimum(g_lo, 0.0)
    )
    return (
        keep,
        jnp.maximum(f_lo, 0.0),
        -jnp.minimum(f_hi, 0.0),
        jnp.maximum(g_lo, 0.0),
        -jnp.minimum(g_hi, 0.0),
    )


def combine(k, mid, lo, hi, left, right):
    return k[0] * mid + k[1] * lo + k[2] * hi + k[3] * left + k[4] * right


def net(x, h1_ref, h2_ref, w1_ref, b1_ref, w2_ref, b2_ref, w3_ref, emit):
    hidden = w2_ref.shape[0]
    wide = 256
    for n in range(0, hidden, wide):
        u = dot(x, w1_ref[:, n : n + wide]) + b1_ref[:, n : n + wide]
        h1_ref[:, n : n + wide] = silu(u).astype(BF16)
    h1 = h1_ref[...]
    for n in range(0, hidden, wide):
        u = dot(h1, w2_ref[:, n : n + wide]) + b2_ref[:, n : n + wide]
        h2_ref[:, n : n + wide] = silu(u).astype(BF16)
    h2 = h2_ref[...]
    for n in range(0, FEAT, wide):
        emit(n, dot(h2, w3_ref[:, n : n + wide]))


def sides(first, count):
    return (
        slice(first, first + count), slice(first - 1, first + count - 1), slice(first + 1, first + count + 1)
    )


def fill_halo(v_ref, row_lo_ref, row_hi_ref, col_lo_ref, col_hi_ref):
    inside = slice(EDGE, EDGE + COLS)
    for f in range(FIELDS):
        at = slice(f * LANES, (f + 1) * LANES)
        v_ref[f, 0, inside, :] = row_lo_ref[:, at].astype(F32)
        v_ref[f, ROWS + 1, inside, :] = row_hi_ref[:, at].astype(F32)
        low = col_lo_ref[:, at].astype(F32)
        high = col_hi_ref[:, at].astype(F32)
        for r in range(ROWS):
            v_ref[f, r + 1, EDGE - 1 : EDGE, :] = low[r : r + 1, :]
            v_ref[f, r + 1, EDGE + COLS : EDGE + COLS + 1, :] = high[r : r + 1, :]


def fill_speed_halo(c_ref, row_lo_ref, row_hi_ref, col_lo_ref, col_hi_ref):
    inside = slice(EDGE, EDGE + COLS)
    at = slice(FEAT, FEAT + LANES)
    low = col_lo_ref[:, at].astype(F32)
    high = col_hi_ref[:, at].astype(F32)
    for r in range(ROWS):
        c_ref[1, r + 1, EDGE - 1 : EDGE, :] = low[r : r + 1, :]
        c_ref[1, r + 1, EDGE + COLS : EDGE + COLS + 1, :] = high[r : r + 1, :]
    for spot, held, halo_ref, flag in (
        (0, 1, row_lo_ref, lax.axis_index("gx") > 0),
        (ROWS + 1, ROWS, row_hi_ref, lax.axis_index("gx") < lax.axis_size("gx") - 1),
    ):
        halo = halo_ref[:, at].astype(F32)
        c_ref[0, spot, inside, :] = jnp.where(flag, halo, -c_ref[0, held, inside, :])


def advect_into(v_ref, c_ref, r, pick, x_ref, adv_ref, here):
    def read(ref, f, row, which):
        parts = [ref[f, row, at, :] for at in pick[which]]
        return parts[0] if len(parts) == 1 else jnp.concatenate(parts, axis=0)

    k = weights_of(
        read(c_ref, 0, r - 1, 0), read(c_ref, 0, r, 0), read(c_ref, 0, r + 1, 0),
        read(c_ref, 1, r, 1), read(c_ref, 1, r, 0), read(c_ref, 1, r, 2),
    )
    for f in range(FIELDS):
        at = slice(f * LANES, (f + 1) * LANES)
        moved = combine(
            k, read(v_ref, f, r, 0), read(v_ref, f, r - 1, 0), read(v_ref, f, r + 1, 0),
            read(v_ref, f, r, 1), read(v_ref, f, r, 2),
        )
        adv_ref[here, at] = moved
        x_ref[here, at] = moved.astype(BF16)


def rim_kernel(
    mask_ref, row_lo_ref, row_hi_ref, col_lo_ref, col_hi_ref,
    w1_ref, b1_ref, w2_ref, b2_ref, w3_ref, _v, _c,
    v_ref, c_ref, out_ref, send_ref, x_ref, adv_ref, h1_ref, h2_ref,
):
    halo = (row_lo_ref, row_hi_ref, col_lo_ref, col_hi_ref)
    fill_halo(v_ref, *halo)
    fill_speed_halo(c_ref, *halo)
    whole = [[at] for at in sides(EDGE, COLS)]
    edge = [list(pair) for pair in zip(sides(EDGE, EDGE), sides(COLS, EDGE))]
    places = []
    for r, spot in ((1, 0), (ROWS, COLS)):
        advect_into(v_ref, c_ref, r, whole, x_ref, adv_ref, slice(spot, spot + COLS))
        places.append((r, slice(EDGE, EDGE + COLS), slice(spot, spot + COLS)))

    def edge_row(i, carry):
        spot = pl.multiple_of(2 * COLS + i * 2 * EDGE, 2 * EDGE)
        advect_into(v_ref, c_ref, i + 2, edge, x_ref, adv_ref, pl.ds(spot, 2 * EDGE))
        return carry

    lax.fori_loop(0, ROWS - 2, edge_row, 0)
    for r in range(2, ROWS):
        spot = 2 * COLS + (r - 2) * 2 * EDGE
        places.append((r, slice(EDGE, 2 * EDGE), slice(spot, spot + EDGE)))
        places.append((r, slice(COLS, COLS + EDGE), slice(spot + EDGE, spot + 2 * EDGE)))

    def emit(n, heat):
        for m in range(0, heat.shape[1], LANES):
            at = slice(n + m, n + m + LANES)
            for r, columns, here in places:
                lit = mask_ref[r - 1, columns.start - EDGE : columns.stop - EDGE, :]
                out_ref[(n + m) // LANES, r, columns, :] = (
                    adv_ref[here, at] + lit * heat[here, m : m + LANES]
                )

    net(x_ref[...], h1_ref, h2_ref, w1_ref, b1_ref, w2_ref, b2_ref, w3_ref, emit)
    for f in range(FIELDS):
        send_ref[:, f * LANES : (f + 1) * LANES] = out_ref[f, ROWS, EDGE : EDGE + COLS, :].astype(BF16)


def held_weights(weights):
    return tuple(in_vmem(w) if w.dtype == BF16 else w for w in weights)


def net_scratch(many, hidden):
    return [
        pltpu.VMEM((many, FEAT), BF16),
        pltpu.VMEM((many, FEAT), F32),
        pltpu.VMEM((many, hidden), BF16),
        pltpu.VMEM((many, hidden), BF16),
    ]


def rim(state, speeds, mask, halo, weights):
    near = (in_vmem(mask), *halo, *held_weights(weights))
    return pl.pallas_call(
        rim_kernel,
        in_specs=[VMEM] * (len(near) + 2),
        out_specs=[VMEM] * 4,
        out_shape=[
            vmem_out((FIELDS, *MARGIN), F32),
            vmem_out((2, *MARGIN), F32),
            vmem_out((FIELDS, *MARGIN), F32),
            jax.ShapeDtypeStruct((COLS, FEAT), BF16),
        ],
        input_output_aliases={len(near): 0, len(near) + 1: 1},
        scratch_shapes=net_scratch(RIM, weights[2].shape[0]),
        compiler_params=params(10),
        cost_estimate=cost(3_000_000_000, 4 << 20),
        name="rim",
    )(*near, in_vmem(state), in_vmem(speeds))


def piece_kernel(
    number, v_ref, c_ref, mask_ref, w1_ref, b1_ref, w2_ref, b2_ref, w3_ref, _, out_ref, *rest
):
    send, (x_ref, adv_ref, h1_ref, h2_ref) = rest[:-4], rest[-4:]
    first, count = PIECES[number]
    pick = [[at] for at in sides(2 * EDGE, INNER)]
    for j in range(count):
        here = slice(j * INNER, (j + 1) * INNER)
        advect_into(v_ref, c_ref, first + j + 1, pick, x_ref, adv_ref, here)

    def emit(n, heat):
        for j in range(count):
            here = slice(j * INNER, (j + 1) * INNER)
            lit = mask_ref[first + j, EDGE : EDGE + INNER, :]
            for m in range(0, heat.shape[1], LANES):
                out_ref[(n + m) // LANES, first + j + 1, 2 * EDGE : 2 * EDGE + INNER, :] = (
                    adv_ref[here, n + m : n + m + LANES] + lit * heat[here, m : m + LANES]
                )

    net(x_ref[...], h1_ref, h2_ref, w1_ref, b1_ref, w2_ref, b2_ref, w3_ref, emit)
    for f in range(FIELDS):
        at = slice(f * LANES, (f + 1) * LANES)
        if number == 0:
            send[0][:, at] = out_ref[f, 1, EDGE : EDGE + COLS, :].astype(BF16)
        if number == 1:
            send[0][:, at] = out_ref[f, 1 : ROWS + 1, EDGE + COLS - 1].astype(BF16)
        if number == 2:
            send[0][:, at] = out_ref[f, 1 : ROWS + 1, EDGE].astype(BF16)


def piece(number, state, speeds, mask, weights, target):
    near = (in_vmem(state), in_vmem(speeds), in_vmem(mask), *held_weights(weights), in_vmem(target))
    outs = [vmem_out((FIELDS, *MARGIN), F32)]
    if number < 3:
        outs += [jax.ShapeDtypeStruct((COLS if number == 0 else ROWS, FEAT), BF16)]
    return pl.pallas_call(
        lambda *refs: piece_kernel(number, *refs),
        in_specs=[VMEM] * len(near),
        out_specs=[VMEM] * len(outs),
        out_shape=outs,
        input_output_aliases={len(near) - 1: 0},
        scratch_shapes=net_scratch(PIECES[number][1] * INNER, weights[2].shape[0]),
        compiler_params=params(10),
        cost_estimate=cost(2_000_000_000, 1 << 20),
        name=f"piece_{number}",
    )(*near)


def final_kernel(
    c_ref, mask_ref, row_lo_ref, row_hi_ref, col_lo_ref, col_hi_ref,
    w1_ref, b1_ref, w2_ref, b2_ref, w3_ref, place_ref, tags_ref, _,
    v_ref, out_hbm, pack_hbm, out_ref, pack_ref, x_ref, adv_ref, h1_ref, h2_ref, out_sems, pack_sems,
):
    fill_halo(v_ref, row_lo_ref, row_hi_ref, col_lo_ref, col_hi_ref)
    pick = [[at] for at in sides(EDGE, COLS)]

    def store(g):
        rows = pl.ds(g * GROUP, GROUP)
        return pltpu.make_async_copy(out_ref.at[:, rows], out_hbm.at[:, rows], out_sems.at[g])

    def body(g, carry):
        for j in range(GROUP):
            here = slice(j * COLS, (j + 1) * COLS)
            advect_into(v_ref, c_ref, g * GROUP + j + 1, pick, x_ref, adv_ref, here)

        def emit(n, heat):
            for j in range(GROUP):
                r = g * GROUP + j
                here = slice(j * COLS, (j + 1) * COLS)
                for m in range(0, heat.shape[1], LANES):
                    out_ref[(n + m) // LANES, r] = (
                        adv_ref[here, n + m : n + m + LANES] + mask_ref[r] * heat[here, m : m + LANES]
                    )

        net(x_ref[...], h1_ref, h2_ref, w1_ref, b1_ref, w2_ref, b2_ref, w3_ref, emit)
        store(g).start()
        return carry

    lax.fori_loop(0, ROWS // GROUP, body, 0)
    stores = [store(g) for g in range(ROWS // GROUP)]
    flat = out_ref.reshape(FIELDS * CELLS, LANES)
    half = FEAT // 2
    columns = [
        jnp.concatenate(
            [flat[pl.ds(f * CELLS + c, SEGS, stride=2), :] for f in (2, 3)], axis=1
        ).astype(BF16)
        for c in range(2)
    ]
    pack_ref[:, 2 * FEAT :] = tags_ref[...]
    for i, b in enumerate(range(0, SEGS, 256)):
        for q in range(2):
            for c in range(2):
                pack_ref[b : b + 256, q * FEAT + c * half : q * FEAT + (c + 1) * half] = dot(
                    place_ref[q, b : b + 256, :], columns[c]
                ).astype(BF16)
        at = pl.ds(b, 256)
        stores.append(pltpu.make_async_copy(pack_ref.at[at], pack_hbm.at[at], pack_sems.at[i]))
        stores[-1].start()
    for copy in stores:
        copy.wait()


def final(state, speeds, mask, halo, weights, place, tags):
    near = (
        in_vmem(speeds), in_vmem(mask), *halo, *held_weights(weights), in_vmem(place), in_vmem(tags),
        in_vmem(state),
    )
    _, out, packed = pl.pallas_call(
        final_kernel,
        in_specs=[VMEM] * len(near),
        out_specs=[VMEM, HBM, HBM],
        out_shape=[
            vmem_out((FIELDS, *MARGIN), F32),
            hbm_out((FIELDS, ROWS, COLS, LANES), F32),
            hbm_out((SEGS, 2 * FEAT + LANES), BF16),
        ],
        input_output_aliases={len(near) - 1: 0},
        scratch_shapes=[
            pltpu.VMEM((FIELDS, ROWS, COLS, LANES), F32),
            pltpu.VMEM((SEGS, 2 * FEAT + LANES), BF16),
            *net_scratch(GROUP * COLS, weights[2].shape[0]),
            pltpu.SemaphoreType.DMA((ROWS // GROUP,)),
            pltpu.SemaphoreType.DMA((SEGS // 256,)),
        ],
        compiler_params=params(18),
        cost_estimate=cost(12_000_000_000, 4 << 20),
        name="final",
    )(*near)
    return out, packed


def unturn_kernel(t_hbm, out_ref, t_ref, stage_ref, in_sems, sems):
    size = LANES * ROWS
    loads = [pltpu.make_async_copy(t_hbm.at[f], t_ref.at[f], in_sems.at[f]) for f in range(FIELDS)]
    stores = [
        pltpu.make_async_copy(stage_ref.at[f], out_ref.at[pl.ds(f * size, size)], sems.at[f])
        for f in range(FIELDS)
    ]
    for load in loads:
        load.start()
    for f in range(FIELDS):
        loads[f].wait()
        for r in range(ROWS):
            stage_ref[f, pl.ds(r, LANES, stride=ROWS), :] = t_ref[f, r].T
        stores[f].start()
    for store in stores:
        store.wait()


def unturn(state):
    return pl.pallas_call(
        unturn_kernel,
        in_specs=[HBM],
        out_specs=HBM,
        out_shape=hbm_out((FIELDS * LANES * ROWS, COLS), F32),
        scratch_shapes=[
            pltpu.VMEM((FIELDS, ROWS, COLS, LANES), F32),
            pltpu.VMEM((FIELDS, LANES * ROWS, COLS), F32),
            pltpu.SemaphoreType.DMA((FIELDS,)),
            pltpu.SemaphoreType.DMA((FIELDS,)),
        ],
        compiler_params=params(12),
        cost_estimate=cost(1_000_000_000, 8 << 20),
        name="unturn",
    )(in_hbm(state))


def chem_kernel(
    arr_ref, regrid_ref, w1_ref, b1_ref, w2_hbm, out_hbm,
    want_ref, mix_ref, x_ref, h_ref, out_ref, w2_ref, sems, w_sem,
):
    w2_load = pltpu.make_async_copy(w2_hbm, w2_ref, w_sem.at[0])
    w2_load.start()
    from_cell = iota((LANES, LANES), 0)
    to_lane = iota((LANES, LANES), 1)
    source_cell = jnp.where(to_lane < 64, 2 * to_lane, 2 * (to_lane - 64) + 1)
    split = (from_cell == source_cell).astype(F32).astype(BF16)
    mix_ref[...] = dot(regrid_ref[...], split).astype(BF16)
    lane = iota((8, LANES), 1)
    which = iota((8, LANES), 0)
    pick = jnp.where(lane == 2 * which, 32.0, jnp.where(lane == 2 * which + 1, 1.0, 0.0))
    pick = jnp.where(which < 2, pick, 0.0).astype(BF16)
    want_ref[...] = dot_nt(pick, arr_ref[:, 2 * FEAT :]).astype(jnp.int32) - 1
    span = 256
    half = FEAT // 2
    stores = []
    for i in range(SEGS // span):
        start = i * span
        placed = []
        for q in range(2):
            chosen = (iota((span, SEGS), 0) + start == want_ref[q : q + 1, :]).astype(F32).astype(BF16)
            placed.append(dot(chosen, arr_ref[:, q * FEAT : (q + 1) * FEAT]))
        placed = (placed[0] + placed[1]).astype(BF16)
        for b in range(span // 64):
            cells = jnp.concatenate(
                [placed[b * 64 : (b + 1) * 64, :half], placed[b * 64 : (b + 1) * 64, half:]], axis=0
            )
            spot = 2 * start + b * LANES
            x_ref[i % 2, b * LANES : (b + 1) * LANES, :] = dot(
                mix_ref[spot : spot + LANES, :], cells
            ).astype(BF16)
        x = x_ref[i % 2]
        for n in range(0, w1_ref.shape[1], 256):
            u = dot(x, w1_ref[:, n : n + 256]) + b1_ref[:, n : n + 256]
            h_ref[i % 2, :, n : n + 256] = silu(u).astype(BF16)
        if i == 0:
            w2_load.wait()
        rows = slice(2 * start, 2 * (start + span))
        out_ref[rows, :] = dot(h_ref[i % 2], w2_ref[...]).astype(BF16)
        at = pl.ds(2 * start, 2 * span)
        stores.append(pltpu.make_async_copy(out_ref.at[at], out_hbm.at[at], sems.at[i]))
        stores[-1].start()
    for store in stores:
        store.wait()


def chem(arrived, regrid_weights, w1, b1, w2):
    return pl.pallas_call(
        chem_kernel,
        in_specs=[VMEM] * 4 + [HBM],
        out_specs=HBM,
        out_shape=hbm_out((CELLS, w2.shape[1]), BF16),
        scratch_shapes=[
            pltpu.VMEM((8, SEGS), jnp.int32),
            pltpu.VMEM((CELLS, LANES), BF16),
            pltpu.VMEM((2, 512, FEAT // 2), BF16),
            pltpu.VMEM((2, 512, w1.shape[1]), BF16),
            pltpu.VMEM((CELLS, w2.shape[1]), BF16),
            pltpu.VMEM(w2.shape, BF16),
            pltpu.SemaphoreType.DMA((SEGS // 256,)),
            pltpu.SemaphoreType.DMA((1,)),
        ],
        compiler_params=params(14),
        cost_estimate=cost(4_400_000_000, 4 << 20),
        name="chem",
    )(
        in_vmem(arrived),
        in_vmem(regrid_weights.reshape(CELLS, LANES)),
        in_vmem(w1),
        b1,
        in_hbm(w2),
    )


def rows_up(x):
    return lax.ppermute(x, "gx", [(i, i + 1) for i in range(lax.axis_size("gx") - 1)])


def rows_down(x):
    return lax.ppermute(x, "gx", [(i + 1, i) for i in range(lax.axis_size("gx") - 1)])


def columns_right(x):
    count = lax.axis_size("gy")
    return lax.ppermute(x, "gy", [(i, (i + 1) % count) for i in range(count)])


def columns_left(x):
    count = lax.axis_size("gy")
    return lax.ppermute(x, "gy", [((i + 1) % count, i) for i in range(count)])


def local(
    fields, courant, sun_columns, rad_w1, rad_b1, rad_w2, rad_b2, rad_w3,
    segment_route, regrid_weights, chem_w1, chem_b1, chem_w2,
):
    weights = (rad_w1, rad_b1.reshape(1, -1), rad_w2, rad_b2.reshape(1, -1), rad_w3)

    state, speeds, row_lo, row_hi, col_lo, col_hi = turn(fields, courant)
    halo = (rows_up(row_hi), rows_down(row_lo), columns_right(col_hi), columns_left(col_lo))
    mask, place, tags = plan(sun_columns, segment_route)
    state, speeds, target, row_hi = rim(state, speeds, mask, halo, weights)
    row_hi = rows_up(row_hi)
    target, row_lo = piece(0, state, speeds, mask, weights, target)
    row_lo = rows_down(row_lo)
    target, col_hi = piece(1, state, speeds, mask, weights, target)
    col_hi = columns_right(col_hi)
    target, col_lo = piece(2, state, speeds, mask, weights, target)
    col_lo = columns_left(col_lo)
    (target,) = piece(3, state, speeds, mask, weights, target)
    halo = (row_hi, row_lo, col_hi, col_lo)
    state, packed = final(target, speeds, mask, halo, weights, place, tags)
    tiles = lax.axis_size("gx") * lax.axis_size("gy")
    packed = packed.reshape(tiles, SEGS // tiles, packed.shape[1])
    arrived = lax.all_to_all(packed, ("gx", "gy"), split_axis=0, concat_axis=0, tiled=True)
    fields_out = unturn(state).reshape(fields.shape)
    output = chem(
        arrived.reshape(SEGS, arrived.shape[2]), regrid_weights, chem_w1, chem_b1.reshape(1, -1), chem_w2
    )
    return fields_out, output.reshape(1, 1, CELLS, -1)


def solution(mesh):
    return jax.shard_map(
        local,
        mesh=mesh,
        in_specs=(
            P(None, None, "gx", "gy"),
            P(None, None, "gx", "gy"),
            P("gx", "gy", None),
            P(),
            P(),
            P(),
            P(),
            P(),
            P(None, "gx", "gy", None),
            P("gx", "gy", None, None, None),
            P(),
            P(),
            P(),
        ),
        out_specs=(P(None, None, "gx", "gy"), P("gx", "gy", None, None)),
        check_vma=False,
    )
```

time: 122 us -> 113 us (0.926)
  Pallas kernels: 55.3 us -> 46.5 us
  starting transfers between devices: 35.8 us -> 34.3 us
  waiting for transfers between devices: 29.5 us -> 30.8 us
    pallas_call x4 -> x8, Pallas kernels: 43 us -> 34.2 us  [the longest x1 15.5 us: final(): pl.pallas_call(final_kernel, in_specs=[VMEM] * len(near), out_specs=[VMEM...]
    all_to_all x1, starting transfers between devices: 16.3 us -> 14.8 us  [local(): lax.all_to_all(packed, ('gx', 'gy'), split_axis=0, concat_axis=0, tiled=T...]
    ppermute x8, waiting for transfers between devices: 1 us -> 2.31 us  [the longest x2 2.3 us: rows_down(): lax.ppermute(x, 'gx', [(i + 1, i) for i in range(lax.axis_size('gx') - 1)])]
  transfers between devices with their start and end apart: 9 -> 9, of which waited for: 4 -> 2; matrix products, arithmetic and copies ran while one was open for 0% -> 0% of each run, Pallas kernels for 7% -> 14%
where the time goes in v3:
time: 113 us
  Pallas kernels  46.5 us (41%)
  starting transfers between devices  34.3 us (30%)
  waiting for transfers between devices  30.8 us (27%)
    all_to_all x1, waiting for transfers between devices, local(): lax.all_to_all(packed, ('gx', 'gy'), split_axis=0, concat_axis=0, tiled=T...  28.5 us
    pallas_call x1, Pallas kernels, final(): pl.pallas_call(final_kernel, in_specs=[VMEM] * len(near), out_specs=[VMEM...  15.5 us
    all_to_all x1, starting transfers between devices, local(): lax.all_to_all(packed, ('gx', 'gy'), split_axis=0, concat_axis=0, tiled=T...  14.8 us
    pallas_call x4, Pallas kernels, piece(): pl.pallas_call(lambda *refs: piece_kernel(number, *refs), in_specs=[VMEM]...  9.54 us
    pallas_call x1, Pallas kernels, chem(): pl.pallas_call(chem_kernel, in_specs=[VMEM] * 4 + [HBM], out_specs=HBM, o...  8.28 us
    ppermute x2, starting transfers between devices, columns_right(): return lax.ppermute(x, 'gy', [(i, (i + 1) % count) for i in range(count)])  7.3 us
    ppermute x2, starting transfers between devices, rows_up(): lax.ppermute(x, 'gx', [(i, i + 1) for i in range(lax.axis_size('gx') - 1)])  7.21 us
    pallas_call x1, Pallas kernels, unturn(): pl.pallas_call(unturn_kernel, in_specs=[HBM], out_specs=HBM, out_shape=hb...  3.97 us
  transfers between devices with their start and end apart: 9, of which 2 were waited for; matrix products, arithmetic and copies ran while one was open for 0% of the time, Pallas kernels for 14%

profile of v3, /device:TPU:1, one launch (start us, length us, event | category | flops | bytes accessed | tf_op | source)
XLA Modules:
  0.0 112.7 jit_solution(8231385757148592058)
XLA Ops:
  0.6 0.0 copy-start.7
  0.6 0.0 copy-start.8
  0.7 3.6 %turn.1 = (f32[4,18,144,128]{3,2,1,0:T(8,128)S(1)}, f32[2,18,144,128]{3,2,1,0:T(8,128)S(1)}, bf16[128,640]{1,0:T(8,128)(2,1)S(1)}, bf16[128,640]{1,0:T(8,128)(2,...) custom-call(f32[8192,128]{1,0:T(8,128)} %bitcast.29, f32[4096,128]{1,0:T(8,128)} %bitcast.30), custom_call_target="tpu_custom_call" | custom-call | flops 4000000000 | bytes 12582912 | tf_op jit(solution)/shard_map/turn/pallas_call | solution.py:113
  4.3 3.1 %collective-permute-start.2 = (bf16[16,640]{1,0:T(8,128)(2,1)S(1)}, bf16[16,640]{1,0:T(8,128)(2,1)S(1)}, u32[]{:S(2)}, u32[]{:S(2)}) collective-permute-start(bf16[16,640]{1,0:T(8,128)(2,1)S(1)} %get-tuple-element.26), channel_id=1, source_target_pairs={{0,1},{1,2},{2,3},{3,4},{4,5},{5,6},{6,7},{7,8},{8,9},{9,10},{10,1... | collective-permute-start | bytes 61448 | tf_op jit(solution)/shard_map/ppermute | solution.py:611
  7.4 0.0 collective-permute-start.3
  7.4 3.2 %collective-permute-start = (bf16[128,640]{1,0:T(8,128)(2,1)S(1)}, bf16[128,640]{1,0:T(8,128)(2,1)S(1)}, u32[]{:S(2)}, u32[]{:S(2)}) collective-permute-start(bf16[128,640]{1,0:T(8,128)(2,1)S(1)} %get-tuple-element.24), channel_id=1, source_target_pairs={{0,16},{16,32},{32,48},{48,64},{64,80},{80,96},{96,112},{1,17},{17... | collective-permute-start | bytes 491528 | tf_op jit(solution)/shard_map/ppermute | solution.py:602
  10.6 1.3 %collective-permute-start.1 = (bf16[128,640]{1,0:T(8,128)(2,1)S(1)}, bf16[128,640]{1,0:T(8,128)(2,1)S(1)}, u32[]{:S(2)}, u32[]{:S(2)}) collective-permute-start(bf16[128,640]{1,0:T(8,128)(2,1)S(1)} %get-tuple-element.25), channel_id=1, source_target_pairs={{16,0},{32,16},{48,32},{64,48},{80,64},{96,80},{112,96},{17,1},{33... | collective-permute-start | bytes 491528 | tf_op jit(solution)/shard_map/ppermute | solution.py:606
  11.9 0.0 copy-done.7
  11.9 0.0 copy-done.8
  11.9 0.0 copy-start
  11.9 0.0 copy-start.1
  11.9 0.0 copy-start.2
  11.9 0.0 copy-start.3
  11.9 0.0 copy-start.4
  12.0 2.3 %plan.1 = (f32[16,128,128]{2,1,0:T(8,128)S(1)}, bf16[2,1024,1024]{2,1,0:T(8,128)(2,1)S(1)}, bf16[1024,128]{1,0:T(8,128)(2,1)S(1)}) custom-call(s32[1,2048]{1,0:T(1,128)S(1)} %bitcast.25, s32[2,1,1,1024]{3,2,1,0:T(1,128)S(1)} %copy-done.8), custom_call_target="tpu_custom_call" | custom-call | flops 3000000000 | bytes 1048576 | tf_op jit(solution)/shard_map/plan/pallas_call | solution.py:175
  14.3 0.0 collective-permute-done.2.col_lo_ref
  14.3 0.0 collective-permute-done.3.col_hi_ref
  14.3 0.0 collective-permute-done.row_lo_ref
  14.3 2.3 %collective-permute-done.1.row_hi_ref = bf16[128,640]{1,0:T(8,128)(2,1)S(1)} collective-permute-done((bf16[128,640]{1,0:T(8,128)(2,1)S(1)}, bf16[128,640]{1,0:T(8,128)(2,1)S(1)}, u32[]{:S(2)}, u32[]{:S(2)}) %collective-permute-start.1) | collective-permute-done | bytes 163872 | tf_op jit(solution)/shard_map/ppermute | solution.py:606
  16.6 0.0 copy-done
  16.6 0.0 copy-done.1
  16.6 0.0 copy-done.2
  16.6 0.0 copy-done.3
  16.7 0.0 copy-done.4
  16.7 3.2 %rim.1 = (f32[4,18,144,128]{3,2,1,0:T(8,128)S(1)}, f32[2,18,144,128]{3,2,1,0:T(8,128)S(1)}, f32[4,18,144,128]{3,2,1,0:T(8,128)S(1)}, bf16[128,512]{1,0:T(8,128)(2,1)S(1)}) custom-call(f32[16,128,128]{2,1,0:T(8,128)S(1)} %get-tuple-element.23.mask_ref.refs_2_, ...), custom_call_target="tpu_custom_call", output_to_operand_aliasing={{0}: (10, {}), {1}: (11, {})} | custom-call | flops 3000000000 | bytes 4194304 | tf_op jit(solution)/shard_map/rim/pallas_call | solution.py:339
  19.9 4.0 %collective-permute-start.4 = (bf16[128,512]{1,0:T(8,128)(2,1)S(1)}, bf16[128,512]{1,0:T(8,128)(2,1)S(1)}, u32[]{:S(2)}, u32[]{:S(2)}) collective-permute-start(bf16[128,512]{1,0:T(8,128)(2,1)S(1)} %get-tuple-element.31), channel_id=1, source_target_pairs={{0,16},{16,32},{32,48},{48,64},{64,80},{80,96},{96,112},{1,17},{17... | collective-permute-start | bytes 393224 | tf_op jit(solution)/shard_map/ppermute | solution.py:602
  23.9 2.6 %piece_0.1 = (f32[4,18,144,128]{3,2,1,0:T(8,128)S(1)}, bf16[128,512]{1,0:T(8,128)(2,1)S(1)}) custom-call(f32[4,18,144,128]{3,2,1,0:T(8,128)S(1)} %get-tuple-element.32.refs_0_, f32[2,18,144,128]{3,2,1,0:T(8,128)S(1)} %get-tuple-element.30.refs_1_.c_ref, f32[16,128,128]{2,1,0:T(8,128)S(1)} %get-tuple-element.23.mask_ref.refs_2_, ...), custom_call_target="tpu_custom_call", output_to_operand_aliasing={{0}: (8, {})} | custom-call | flops 2000000000 | bytes 1048576 | tf_op jit(solution)/shard_map/piece_0/pallas_call | solution.py:392
  26.5 1.5 %collective-permute-start.5 = (bf16[128,512]{1,0:T(8,128)(2,1)S(1)}, bf16[128,512]{1,0:T(8,128)(2,1)S(1)}, u32[]{:S(2)}, u32[]{:S(2)}) collective-permute-start(bf16[128,512]{1,0:T(8,128)(2,1)S(1)} %get-tuple-element.34), channel_id=1, source_target_pairs={{16,0},{32,16},{48,32},{64,48},{80,64},{96,80},{112,96},{17,1},{33... | collective-permute-start | bytes 393224 | tf_op jit(solution)/shard_map/ppermute | solution.py:606
  28.0 2.7 %piece_1.1 = (f32[4,18,144,128]{3,2,1,0:T(8,128)S(1)}, bf16[16,512]{1,0:T(8,128)(2,1)S(1)}) custom-call(f32[4,18,144,128]{3,2,1,0:T(8,128)S(1)} %get-tuple-element.32.refs_0_, f32[2,18,144,128]{3,2,1,0:T(8,128)S(1)} %get-tuple-element.30.refs_1_.c_ref, f32[16,128,128]{2,1,0:T(8,128)S(1)} %get-tuple-element.23.mask_ref.refs_2_, ...), custom_call_target="tpu_custom_call", output_to_operand_aliasing={{0}: (8, {})} | custom-call | flops 2000000000 | bytes 1048576 | tf_op jit(solution)/shard_map/piece_1/pallas_call | solution.py:392
  30.7 4.2 %collective-permute-start.6 = (bf16[16,512]{1,0:T(8,128)(2,1)S(1)}, bf16[16,512]{1,0:T(8,128)(2,1)S(1)}, u32[]{:S(2)}, u32[]{:S(2)}) collective-permute-start(bf16[16,512]{1,0:T(8,128)(2,1)S(1)} %get-tuple-element.36), channel_id=1, source_target_pairs={{0,1},{1,2},{2,3},{3,4},{4,5},{5,6},{6,7},{7,8},{8,9},{9,10},{10,1... | collective-permute-start | bytes 49160 | tf_op jit(solution)/shard_map/ppermute | solution.py:611
  34.9 2.1 %piece_2.1 = (f32[4,18,144,128]{3,2,1,0:T(8,128)S(1)}, bf16[16,512]{1,0:T(8,128)(2,1)S(1)}) custom-call(f32[4,18,144,128]{3,2,1,0:T(8,128)S(1)} %get-tuple-element.32.refs_0_, f32[2,18,144,128]{3,2,1,0:T(8,128)S(1)} %get-tuple-element.30.refs_1_.c_ref, f32[16,128,128]{2,1,0:T(8,128)S(1)} %get-tuple-element.23.mask_ref.refs_2_, ...), custom_call_target="tpu_custom_call", output_to_operand_aliasing={{0}: (8, {})} | custom-call | flops 2000000000 | bytes 1048576 | tf_op jit(solution)/shard_map/piece_2/pallas_call | solution.py:392
  37.0 2.2 %collective-permute-start.7 = (bf16[16,512]{1,0:T(8,128)(2,1)S(1)}, bf16[16,512]{1,0:T(8,128)(2,1)S(1)}, u32[]{:S(2)}, u32[]{:S(2)}) collective-permute-start(bf16[16,512]{1,0:T(8,128)(2,1)S(1)} %get-tuple-element.38), channel_id=1, source_target_pairs={{1,0},{2,1},{3,2},{4,3},{5,4},{6,5},{7,6},{8,7},{9,8},{10,9},{11,1... | collective-permute-start | bytes 49160 | tf_op jit(solution)/shard_map/ppermute | solution.py:616
  39.2 2.1 %piece_3.1._ = f32[4,18,144,128]{3,2,1,0:T(8,128)S(1)} custom-call(f32[4,18,144,128]{3,2,1,0:T(8,128)S(1)} %get-tuple-element.32.refs_0_, f32[2,18,144,128]{3,2,1,0:T(8,128)S(1)} %get-tuple-element.30.refs_1_.c_ref, f32[16,128,128]{2,1,0:T(8,128)S(1)} %get-tuple-element.23.mask_ref.refs_2_, ...), custom_call_target="tpu_custom_call", output_to_operand_aliasing={{}: (8, {})} | custom-call | flops 2000000000 | bytes 1048576 | tf_op jit(solution)/shard_map/piece_3/pallas_call | solution.py:392
  41.4 0.0 collective-permute-done.6.col_lo_ref
  41.4 0.0 collective-permute-done.7.col_hi_ref
  41.4 0.0 collective-permute-done.4.row_lo_ref
  41.4 0.0 collective-permute-done.5.row_hi_ref
  41.4 15.5 %final.1 = (f32[4,18,144,128]{3,2,1,0:T(8,128)S(1)}, f32[4,16,128,128]{3,2,1,0:T(8,128)}, bf16[1024,1152]{1,0:T(8,128)(2,1)}) custom-call(f32[2,18,144,128]{3,2,1,0:T(8,128)S(1)} %get-tuple-element.30.refs_1_.c_ref, f32[16,128,128]{2,1,0:T(8,128)S(1)} %get-tuple-element.23.mask_ref.refs_2_, ...), custom_call_target="tpu_custom_call", output_to_operand_aliasing={{0}: (13, {})} | custom-call | flops 12000000000 | bytes 4194304 | tf_op jit(solution)/shard_map/final/pallas_call | solution.py:464
  56.9 14.8 %all-to-all-start = ((bf16[128,8,1152]{2,1,0:T(8,128)(2,1)}), bf16[128,8,1152]{2,1,0:T(8,128)(2,1)S(1)}, u32[]{:S(2)}, u32[]{:S(2)}) async-start(bf16[128,8,1152]{2,1,0:T(8,128)(2,1)} %bitcast.28), calls=%async_computation | async-start | bytes 4718592 | tf_op jit(solution)/shard_map/all_to_all | solution.py:641
  71.7 0.0 copy-start.5
  71.7 0.0 copy-start.6
  71.7 0.0 copy-start.9
  71.7 4.0 %unturn.1 = f32[8192,128]{1,0:T(8,128)} custom-call(f32[4,16,128,128]{3,2,1,0:T(8,128)} %get-tuple-element.42.t_hbm), custom_call_target="tpu_custom_call" | custom-call | flops 1000000000 | bytes 8388608 | tf_op jit(solution)/shard_map/unturn/pallas_call | solution.py:507
  75.7 28.5 %all-to-all-done = bf16[128,8,1152]{2,1,0:T(8,128)(2,1)S(1)} async-done(((bf16[128,8,1152]{2,1,0:T(8,128)(2,1)}), bf16[128,8,1152]{2,1,0:T(8,128)(2,1)S(1)}, u32[]{:S(2)}, u32[]{:S(2)}) %all-to-all-start) | async-done | bytes 2359328 | tf_op jit(solution)/shard_map/all_to_all | solution.py:641
  104.2 0.0 copy-done.5
  104.2 0.0 copy-done.6
  104.2 0.0 copy-done.9
  104.2 8.3 %chem.1 = bf16[2048,256]{1,0:T(8,128)(2,1)} custom-call(bf16[1024,1152]{1,0:T(8,128)(2,1)S(1)} %bitcast.11, bf16[2048,128]{1,0:T(8,128)(2,1)S(1)} %bitcast.24, bf16[256,1024]{1,0:T(8,128)(2,1)S(1)} %copy-done.6, f32[1,1024]{1,0:T(1,128)S(1)} %bitcast.26, bf16[1024,256]{1,0:T(8,128)(2,1)} %w2_hbm.1), custom_call_target="tpu_custom_call" | custom-call | flops 4400000000 | bytes 4194304 | tf_op jit(solution)/shard_map/chem/pallas_call | solution.py:574
Async XLA Ops:
  0.6 11.2 %copy-start.7 = (s32[1,1,2048]{2,1,0:T(1,128)S(1)}, s32[1,1,2048]{2,1,0:T(1,128)}, u32[]{:S(2)}) copy-start(s32[1,1,2048]{2,1,0:T(1,128)} %param.15) | copy-start | bytes 24580
  0.6 11.2 %copy-start.8 = (s32[2,1,1,1024]{3,2,1,0:T(1,128)S(1)}, s32[2,1,1,1024]{3,2,1,0:T(1,128)}, u32[]{:S(2)}) copy-start(s32[2,1,1,1024]{3,2,1,0:T(1,128)} %route_ref.1) | copy-start | bytes 24580
  4.3 10.0 %collective-permute-start.2 = (bf16[16,640]{1,0:T(8,128)(2,1)S(1)}, bf16[16,640]{1,0:T(8,128)(2,1)S(1)}, u32[]{:S(2)}, u32[]{:S(2)}) collective-permute-start(bf16[16,640]{1,0:T(8,128)(2,1)S(1)} %get-tuple-element.26), channel_id=1, source_target_pairs={{0,1},{1,2},{2,3},{3,4},{4,5},{5,6},{6,7},{7,8},{8,9},{9,10},{10,1... | collective-permute-start | bytes 61448 | tf_op jit(solution)/shard_map/ppermute | solution.py:611
  7.4 7.0 %collective-permute-start.3 = (bf16[16,640]{1,0:T(8,128)(2,1)S(1)}, bf16[16,640]{1,0:T(8,128)(2,1)S(1)}, u32[]{:S(2)}, u32[]{:S(2)}) collective-permute-start(bf16[16,640]{1,0:T(8,128)(2,1)S(1)} %get-tuple-element.27), channel_id=1, source_target_pairs={{1,0},{2,1},{3,2},{4,3},{5,4},{6,5},{7,6},{8,7},{9,8},{10,9},{11,1... | collective-permute-start | bytes 61448 | tf_op jit(solution)/shard_map/ppermute | solution.py:616
  7.4 7.0 %collective-permute-start = (bf16[128,640]{1,0:T(8,128)(2,1)S(1)}, bf16[128,640]{1,0:T(8,128)(2,1)S(1)}, u32[]{:S(2)}, u32[]{:S(2)}) collective-permute-start(bf16[128,640]{1,0:T(8,128)(2,1)S(1)} %get-tuple-element.24), channel_id=1, source_target_pairs={{0,16},{16,32},{32,48},{48,64},{64,80},{80,96},{96,112},{1,17},{17... | collective-permute-start | bytes 491528 | tf_op jit(solution)/shard_map/ppermute | solution.py:602
  10.6 6.1 %collective-permute-start.1 = (bf16[128,640]{1,0:T(8,128)(2,1)S(1)}, bf16[128,640]{1,0:T(8,128)(2,1)S(1)}, u32[]{:S(2)}, u32[]{:S(2)}) collective-permute-start(bf16[128,640]{1,0:T(8,128)(2,1)S(1)} %get-tuple-element.25), channel_id=1, source_target_pairs={{16,0},{32,16},{48,32},{64,48},{80,64},{96,80},{112,96},{17,1},{33... | collective-permute-start | bytes 491528 | tf_op jit(solution)/shard_map/ppermute | solution.py:606
  11.9 4.7 %copy-start = (bf16[1024,1024]{1,0:T(8,128)(2,1)S(1)}, bf16[1024,1024]{1,0:T(8,128)(2,1)}, u32[]{:S(2)}) copy-start(bf16[1024,1024]{1,0:T(8,128)(2,1)} %w2_ref.3) | copy-start | bytes 6291460
  11.9 4.7 %copy-start.1 = (bf16[512,1024]{1,0:T(8,128)(2,1)S(1)}, bf16[512,1024]{1,0:T(8,128)(2,1)}, u32[]{:S(2)}) copy-start(bf16[512,1024]{1,0:T(8,128)(2,1)} %w1_ref.4) | copy-start | bytes 3145732
  11.9 4.7 %copy-start.2 = (bf16[1024,512]{1,0:T(8,128)(2,1)S(1)}, bf16[1024,512]{1,0:T(8,128)(2,1)}, u32[]{:S(2)}) copy-start(bf16[1024,512]{1,0:T(8,128)(2,1)} %w3_ref.3) | copy-start | bytes 3145732
  11.9 4.7 %copy-start.3 = (f32[1024]{0:T(1024)S(1)}, f32[1024]{0:T(1024)}, u32[]{:S(2)}) copy-start(f32[1024]{0:T(1024)} %param.17) | copy-start | bytes 12292
  11.9 4.7 %copy-start.4 = (f32[1024]{0:T(1024)S(1)}, f32[1024]{0:T(1024)}, u32[]{:S(2)}) copy-start(f32[1024]{0:T(1024)} %param.19) | copy-start | bytes 12292
  19.9 21.5 %collective-permute-start.4 = (bf16[128,512]{1,0:T(8,128)(2,1)S(1)}, bf16[128,512]{1,0:T(8,128)(2,1)S(1)}, u32[]{:S(2)}, u32[]{:S(2)}) collective-permute-start(bf16[128,512]{1,0:T(8,128)(2,1)S(1)} %get-tuple-element.31), channel_id=1, source_target_pairs={{0,16},{16,32},{32,48},{48,64},{64,80},{80,96},{96,112},{1,17},{17... | collective-permute-start | bytes 393224 | tf_op jit(solution)/shard_map/ppermute | solution.py:602
  26.5 14.9 %collective-permute-start.5 = (bf16[128,512]{1,0:T(8,128)(2,1)S(1)}, bf16[128,512]{1,0:T(8,128)(2,1)S(1)}, u32[]{:S(2)}, u32[]{:S(2)}) collective-permute-start(bf16[128,512]{1,0:T(8,128)(2,1)S(1)} %get-tuple-element.34), channel_id=1, source_target_pairs={{16,0},{32,16},{48,32},{64,48},{80,64},{96,80},{112,96},{17,1},{33... | collective-permute-start | bytes 393224 | tf_op jit(solution)/shard_map/ppermute | solution.py:606
  30.7 10.7 %collective-permute-start.6 = (bf16[16,512]{1,0:T(8,128)(2,1)S(1)}, bf16[16,512]{1,0:T(8,128)(2,1)S(1)}, u32[]{:S(2)}, u32[]{:S(2)}) collective-permute-start(bf16[16,512]{1,0:T(8,128)(2,1)S(1)} %get-tuple-element.36), channel_id=1, source_target_pairs={{0,1},{1,2},{2,3},{3,4},{4,5},{5,6},{6,7},{7,8},{8,9},{9,10},{10,1... | collective-permute-start | bytes 49160 | tf_op jit(solution)/shard_map/ppermute | solution.py:611
  37.0 4.4 %collective-permute-start.7 = (bf16[16,512]{1,0:T(8,128)(2,1)S(1)}, bf16[16,512]{1,0:T(8,128)(2,1)S(1)}, u32[]{:S(2)}, u32[]{:S(2)}) collective-permute-start(bf16[16,512]{1,0:T(8,128)(2,1)S(1)} %get-tuple-element.38), channel_id=1, source_target_pairs={{1,0},{2,1},{3,2},{4,3},{5,4},{6,5},{7,6},{8,7},{9,8},{10,9},{11,1... | collective-permute-start | bytes 49160 | tf_op jit(solution)/shard_map/ppermute | solution.py:616
  56.9 47.3 %all-to-all-start = ((bf16[128,8,1152]{2,1,0:T(8,128)(2,1)}), bf16[128,8,1152]{2,1,0:T(8,128)(2,1)S(1)}, u32[]{:S(2)}, u32[]{:S(2)}) async-start(bf16[128,8,1152]{2,1,0:T(8,128)(2,1)} %bitcast.28), calls=%async_computation | async-start | bytes 4718592 | tf_op jit(solution)/shard_map/all_to_all | solution.py:641
  71.7 32.5 %copy-start.5 = (bf16[1,1,16,128,128]{4,3,2,1,0:T(8,128)(2,1)S(1)}, bf16[1,1,16,128,128]{4,3,2,1,0:T(8,128)(2,1)}, u32[]{:S(2)}) copy-start(bf16[1,1,16,128,128]{4,3,2,1,0:T(8,128)(2,1)} %param.22) | copy-start | bytes 1572868
  71.7 32.5 %copy-start.6 = (bf16[256,1024]{1,0:T(8,128)(2,1)S(1)}, bf16[256,1024]{1,0:T(8,128)(2,1)}, u32[]{:S(2)}) copy-start(bf16[256,1024]{1,0:T(8,128)(2,1)} %w1_ref.5) | copy-start | bytes 1572868
  71.7 32.5 %copy-start.9 = (f32[1024]{0:T(1024)S(1)}, f32[1024]{0:T(1024)}, u32[]{:S(2)}) copy-start(f32[1024]{0:T(1024)} %param.24) | copy-start | bytes 12292

commit v4 on v3

--- a/solution.py
+++ b/solution.py
@@ -15,8 +15,9 @@
 CELLS = ROWS * COLS
 SEGS = CELLS // 2
 EDGE = 8
-GROUP = 4
-PIECES = ((1, 4), (5, 4), (9, 3), (12, 3))
+GROUP = 8
+SPAN = 512
+PIECES = ((1, 5), (6, 9))
 INNER = COLS - 2 * EDGE
 RIM = 2 * COLS + (ROWS - 2) * 2 * EDGE
 MARGIN = (ROWS + 2, COLS + 2 * EDGE, LANES)
@@ -283,8 +284,9 @@
 
 def rim_kernel(
     mask_ref, row_lo_ref, row_hi_ref, col_lo_ref, col_hi_ref,
-    w1_ref, b1_ref, w2_ref, b2_ref, w3_ref, _v, _c,
-    v_ref, c_ref, out_ref, send_ref, x_ref, adv_ref, h1_ref, h2_ref,
+    w1_ref, b1_ref, w2_ref, b2_ref, w3_ref, _v, _c, _out,
+    v_ref, c_ref, out_ref, row_lo_out, row_hi_out, col_lo_out, col_hi_out,
+    x_ref, adv_ref, h1_ref, h2_ref,
 ):
     halo = (row_lo_ref, row_hi_ref, col_lo_ref, col_hi_ref)
     fill_halo(v_ref, *halo)
@@ -318,7 +320,11 @@
 
     net(x_ref[...], h1_ref, h2_ref, w1_ref, b1_ref, w2_ref, b2_ref, w3_ref, emit)
     for f in range(FIELDS):
-        send_ref[:, f * LANES : (f + 1) * LANES] = out_ref[f, ROWS, EDGE : EDGE + COLS, :].astype(BF16)
+        at = slice(f * LANES, (f + 1) * LANES)
+        row_lo_out[:, at] = out_ref[f, 1, EDGE : EDGE + COLS, :].astype(BF16)
+        row_hi_out[:, at] = out_ref[f, ROWS, EDGE : EDGE + COLS, :].astype(BF16)
+        col_lo_out[:, at] = out_ref[f, 1 : ROWS + 1, EDGE].astype(BF16)
+        col_hi_out[:, at] = out_ref[f, 1 : ROWS + 1, EDGE + COLS - 1].astype(BF16)
 
 
 def held_weights(weights):
@@ -334,30 +340,31 @@
     ]
 
 
-def rim(state, speeds, mask, halo, weights):
+def rim(state, speeds, mask, halo, weights, target):
     near = (in_vmem(mask), *halo, *held_weights(weights))
     return pl.pallas_call(
         rim_kernel,
-        in_specs=[VMEM] * (len(near) + 2),
-        out_specs=[VMEM] * 4,
+        in_specs=[VMEM] * (len(near) + 3),
+        out_specs=[VMEM] * 7,
         out_shape=[
             vmem_out((FIELDS, *MARGIN), F32),
             vmem_out((2, *MARGIN), F32),
             vmem_out((FIELDS, *MARGIN), F32),
-            jax.ShapeDtypeStruct((COLS, FEAT), BF16),
-        ],
-        input_output_aliases={len(near): 0, len(near) + 1: 1},
+            *[jax.ShapeDtypeStruct((COLS, FEAT), BF16)] * 2,
+            *[jax.ShapeDtypeStruct((ROWS, FEAT), BF16)] * 2,
+        ],
+        input_output_aliases={len(near) + i: i for i in range(3)},
         scratch_shapes=net_scratch(RIM, weights[2].shape[0]),
         compiler_params=params(10),
         cost_estimate=cost(3_000_000_000, 4 << 20),
         name="rim",
-    )(*near, in_vmem(state), in_vmem(speeds))
+    )(*near, in_vmem(state), in_vmem(speeds), in_vmem(target))
 
 
 def piece_kernel(
-    number, v_ref, c_ref, mask_ref, w1_ref, b1_ref, w2_ref, b2_ref, w3_ref, _, out_ref, *rest
+    number, v_ref, c_ref, mask_ref, w1_ref, b1_ref, w2_ref, b2_ref, w3_ref, *rest
 ):
-    send, (x_ref, adv_ref, h1_ref, h2_ref) = rest[:-4], rest[-4:]
+    out_ref, x_ref, adv_ref, h1_ref, h2_ref = rest[-5:]
     first, count = PIECES[number]
     pick = [[at] for at in sides(2 * EDGE, INNER)]
     for j in range(count):
@@ -374,30 +381,21 @@
                 )
 
     net(x_ref[...], h1_ref, h2_ref, w1_ref, b1_ref, w2_ref, b2_ref, w3_ref, emit)
-    for f in range(FIELDS):
-        at = slice(f * LANES, (f + 1) * LANES)
-        if number == 0:
-            send[0][:, at] = out_ref[f, 1, EDGE : EDGE + COLS, :].astype(BF16)
-        if number == 1:
-            send[0][:, at] = out_ref[f, 1 : ROWS + 1, EDGE + COLS - 1].astype(BF16)
-        if number == 2:
-            send[0][:, at] = out_ref[f, 1 : ROWS + 1, EDGE].astype(BF16)
-
-
-def piece(number, state, speeds, mask, weights, target):
-    near = (in_vmem(state), in_vmem(speeds), in_vmem(mask), *held_weights(weights), in_vmem(target))
-    outs = [vmem_out((FIELDS, *MARGIN), F32)]
-    if number < 3:
-        outs += [jax.ShapeDtypeStruct((COLS if number == 0 else ROWS, FEAT), BF16)]
+
+
+def piece(number, state, speeds, mask, weights, target=None):
+    near = (in_vmem(state), in_vmem(speeds), in_vmem(mask), *held_weights(weights))
+    if target is not None:
+        near += (in_vmem(target),)
     return pl.pallas_call(
         lambda *refs: piece_kernel(number, *refs),
         in_specs=[VMEM] * len(near),
-        out_specs=[VMEM] * len(outs),
-        out_shape=outs,
-        input_output_aliases={len(near) - 1: 0},
+        out_specs=VMEM,
+        out_shape=vmem_out((FIELDS, *MARGIN), F32),
+        input_output_aliases={} if target is None else {len(near) - 1: 0},
         scratch_shapes=net_scratch(PIECES[number][1] * INNER, weights[2].shape[0]),
-        compiler_params=params(10),
-        cost_estimate=cost(2_000_000_000, 1 << 20),
+        compiler_params=params(12),
+        cost_estimate=cost(2_000_000_000 * (1 + 2 * number), 1 << 20),
         name=f"piece_{number}",
     )(*near)
 
@@ -478,7 +476,7 @@
             pltpu.SemaphoreType.DMA((ROWS // GROUP,)),
             pltpu.SemaphoreType.DMA((SEGS // 256,)),
         ],
-        compiler_params=params(18),
+        compiler_params=params(24),
         cost_estimate=cost(12_000_000_000, 4 << 20),
         name="final",
     )(*near)
@@ -537,10 +535,15 @@
     pick = jnp.where(lane == 2 * which, 32.0, jnp.where(lane == 2 * which + 1, 1.0, 0.0))
     pick = jnp.where(which < 2, pick, 0.0).astype(BF16)
     want_ref[...] = dot_nt(pick, arr_ref[:, 2 * FEAT :]).astype(jnp.int32) - 1
-    span = 256
+    span = SPAN
     half = FEAT // 2
-    stores = []
-    for i in range(SEGS // span):
+    w2_load.wait()
+
+    def store(i):
+        at = pl.ds(pl.multiple_of(2 * span * i, 2 * span), 2 * span)
+        return pltpu.make_async_copy(out_ref.at[at], out_hbm.at[at], sems.at[i])
+
+    def body(i, carry):
         start = i * span
         placed = []
         for q in range(2):
@@ -551,23 +554,20 @@
             cells = jnp.concatenate(
                 [placed[b * 64 : (b + 1) * 64, :half], placed[b * 64 : (b + 1) * 64, half:]], axis=0
             )
-            spot = 2 * start + b * LANES
-            x_ref[i % 2, b * LANES : (b + 1) * LANES, :] = dot(
-                mix_ref[spot : spot + LANES, :], cells
-            ).astype(BF16)
-        x = x_ref[i % 2]
+            spot = pl.multiple_of(2 * start + b * LANES, LANES)
+            x_ref[b * LANES : (b + 1) * LANES, :] = dot(mix_ref[pl.ds(spot, LANES), :], cells).astype(BF16)
+        x = x_ref[...]
         for n in range(0, w1_ref.shape[1], 256):
             u = dot(x, w1_ref[:, n : n + 256]) + b1_ref[:, n : n + 256]
-            h_ref[i % 2, :, n : n + 256] = silu(u).astype(BF16)
-        if i == 0:
-            w2_load.wait()
-        rows = slice(2 * start, 2 * (start + span))
-        out_ref[rows, :] = dot(h_ref[i % 2], w2_ref[...]).astype(BF16)
-        at = pl.ds(2 * start, 2 * span)
-        stores.append(pltpu.make_async_copy(out_ref.at[at], out_hbm.at[at], sems.at[i]))
-        stores[-1].start()
-    for store in stores:
-        store.wait()
+            h_ref[:, n : n + 256] = silu(u).astype(BF16)
+        rows = pl.ds(pl.multiple_of(2 * start, 2 * span), 2 * span)
+        out_ref[rows, :] = dot(h_ref[...], w2_ref[...]).astype(BF16)
+        store(i).start()
+        return carry
+
+    lax.fori_loop(0, SEGS // span, body, 0)
+    for i in range(SEGS // span):
+        store(i).wait()
 
 
 def chem(arrived, regrid_weights, w1, b1, w2):
@@ -579,14 +579,14 @@
         scratch_shapes=[
             pltpu.VMEM((8, SEGS), jnp.int32),
             pltpu.VMEM((CELLS, LANES), BF16),
-            pltpu.VMEM((2, 512, FEAT // 2), BF16),
-            pltpu.VMEM((2, 512, w1.shape[1]), BF16),
+            pltpu.VMEM((2 * SPAN, FEAT // 2), BF16),
+            pltpu.VMEM((2 * SPAN, w1.shape[1]), BF16),
             pltpu.VMEM((CELLS, w2.shape[1]), BF16),
             pltpu.VMEM(w2.shape, BF16),
-            pltpu.SemaphoreType.DMA((SEGS // 256,)),
+            pltpu.SemaphoreType.DMA((SEGS // SPAN,)),
             pltpu.SemaphoreType.DMA((1,)),
         ],
-        compiler_params=params(14),
+        compiler_params=params(20),
         cost_estimate=cost(4_400_000_000, 4 << 20),
         name="chem",
     )(
@@ -599,11 +599,13 @@
 
 
 def rows_up(x):
-    return lax.ppermute(x, "gx", [(i, i + 1) for i in range(lax.axis_size("gx") - 1)])
+    count = lax.axis_size("gx")
+    return lax.ppermute(x, "gx", [(i, (i + 1) % count) for i in range(count)])
 
 
 def rows_down(x):
-    return lax.ppermute(x, "gx", [(i + 1, i) for i in range(lax.axis_size("gx") - 1)])
+    count = lax.axis_size("gx")
+    return lax.ppermute(x, "gx", [((i + 1) % count, i) for i in range(count)])
 
 
 def columns_right(x):
@@ -625,16 +627,12 @@
     state, speeds, row_lo, row_hi, col_lo, col_hi = turn(fields, courant)
     halo = (rows_up(row_hi), rows_down(row_lo), columns_right(col_hi), columns_left(col_lo))
     mask, place, tags = plan(sun_columns, segment_route)
-    state, speeds, target, row_hi = rim(state, speeds, mask, halo, weights)
-    row_hi = rows_up(row_hi)
-    target, row_lo = piece(0, state, speeds, mask, weights, target)
-    row_lo = rows_down(row_lo)
-    target, col_hi = piece(1, state, speeds, mask, weights, target)
-    col_hi = columns_right(col_hi)
-    target, col_lo = piece(2, state, speeds, mask, weights, target)
-    col_lo = columns_left(col_lo)
-    (target,) = piece(3, state, speeds, mask, weights, target)
-    halo = (row_hi, row_lo, col_hi, col_lo)
+    target = piece(0, state, speeds, mask, weights)
+    state, speeds, target, row_lo, row_hi, col_lo, col_hi = rim(
+        state, speeds, mask, halo, weights, target
+    )
+    halo = (rows_up(row_hi), rows_down(row_lo), columns_right(col_hi), columns_left(col_lo))
+    target = piece(1, state, speeds, mask, weights, target)
     state, packed = final(target, speeds, mask, halo, weights, place, tags)
     tiles = lax.axis_size("gx") * lax.axis_size("gy")
     packed = packed.reshape(tiles, SEGS // tiles, packed.shape[1])

time: 113 us -> 99.6 us (0.88)
  starting transfers between devices: 34.3 us -> 25.2 us
  Pallas kernels: 46.5 us -> 44.4 us
  waiting for transfers between devices: 30.8 us -> 28.7 us
    all_to_all x1, starting transfers between devices: 14.8 us -> 9.34 us  [local(): lax.all_to_all(packed, ('gx', 'gy'), split_axis=0, concat_axis=0, tiled=T...]
    ppermute x4, starting transfers between devices: 9.97 us -> 7.15 us  [the longest x2 5.85 us: rows_down(): return lax.ppermute(x, 'gx', [((i + 1) % count, i) for i in range(count)])]
    ppermute x4, waiting for transfers between devices: 2.3 us -> 0.01 us  [the longest x2 0.01 us: rows_up(): return lax.ppermute(x, 'gx', [(i, (i + 1) % count) for i in range(count)])]
    pallas_call x4 -> x2, Pallas kernels: 9.54 us -> 8.99 us  [piece(): pl.pallas_call(lambda *refs: piece_kernel(number, *refs), in_specs=[VMEM]...]
  transfers between devices with their start and end apart: 9 -> 9, of which waited for: 2 -> 1; matrix products, arithmetic and copies ran while one was open for 0% -> 0% of each run, Pallas kernels for 14% -> 15%
where the time goes in v4:
time: 99.6 us; the launch traced here: 99.4 us
  Pallas kernels  44.4 us (45%)
  waiting for transfers between devices  28.7 us (29%)
  starting transfers between devices  25.2 us (25%)
  between operations  1.05 us (1%)
    all_to_all x1, waiting for transfers between devices, local(): lax.all_to_all(packed, ('gx', 'gy'), split_axis=0, concat_axis=0, tiled=T...  28.7 us
    pallas_call x1, Pallas kernels, final(): pl.pallas_call(final_kernel, in_specs=[VMEM] * len(near), out_specs=[VMEM...  14.8 us
    all_to_all x1, starting transfers between devices, local(): lax.all_to_all(packed, ('gx', 'gy'), split_axis=0, concat_axis=0, tiled=T...  9.34 us
    pallas_call x2, Pallas kernels, piece(): pl.pallas_call(lambda *refs: piece_kernel(number, *refs), in_specs=[VMEM]...  8.99 us
    pallas_call x1, Pallas kernels, chem(): pl.pallas_call(chem_kernel, in_specs=[VMEM] * 4 + [HBM], out_specs=HBM, o...  7.37 us
    ppermute x2, starting transfers between devices, columns_right(): return lax.ppermute(x, 'gy', [(i, (i + 1) % count) for i in range(count)])  6.73 us
    ppermute x2, starting transfers between devices, rows_down(): return lax.ppermute(x, 'gx', [((i + 1) % count, i) for i in range(count)])  5.85 us
    pallas_call x1, Pallas kernels, unturn(): pl.pallas_call(unturn_kernel, in_specs=[HBM], out_specs=HBM, out_shape=hb...  3.97 us
  transfers between devices with their start and end apart: 9, of which 1 were waited for; matrix products, arithmetic and copies ran while one was open for 0% of the time, Pallas kernels for 15%

profile of v4, /device:TPU:1, one launch (start us, length us, event | category | flops | bytes accessed | tf_op | source)
XLA Modules:
  0.0 99.4 jit_solution(13320990386741397374)
XLA Ops:
  0.6 0.0 copy-start.7
  0.6 0.0 copy-start.8
  0.7 3.6 %turn.1 = (f32[4,18,144,128]{3,2,1,0:T(8,128)S(1)}, f32[2,18,144,128]{3,2,1,0:T(8,128)S(1)}, bf16[128,640]{1,0:T(8,128)(2,1)S(1)}, bf16[128,640]{1,0:T(8,128)(2,...) custom-call(f32[8192,128]{1,0:T(8,128)} %bitcast.25, f32[4096,128]{1,0:T(8,128)} %bitcast.26), custom_call_target="tpu_custom_call" | custom-call | flops 4000000000 | bytes 12582912 | tf_op jit(solution)/shard_map/turn/pallas_call | solution.py:114
  4.3 3.1 %collective-permute-start.2 = (bf16[16,640]{1,0:T(8,128)(2,1)S(1)}, bf16[16,640]{1,0:T(8,128)(2,1)S(1)}, u32[]{:S(2)}, u32[]{:S(2)}) collective-permute-start(bf16[16,640]{1,0:T(8,128)(2,1)S(1)} %get-tuple-element.23), channel_id=1, source_target_pairs={{0,1},{1,2},{2,3},{3,4},{4,5},{5,6},{6,7},{7,8},{8,9},{9,10},{10,1... | collective-permute-start | bytes 61448 | tf_op jit(solution)/shard_map/ppermute | solution.py:613
  7.4 0.0 collective-permute-start.3
  7.4 1.3 %collective-permute-start = (bf16[128,640]{1,0:T(8,128)(2,1)S(1)}, bf16[128,640]{1,0:T(8,128)(2,1)S(1)}, u32[]{:S(2)}, u32[]{:S(2)}) collective-permute-start(bf16[128,640]{1,0:T(8,128)(2,1)S(1)} %get-tuple-element.21), channel_id=1, source_target_pairs={{0,16},{16,32},{32,48},{48,64},{64,80},{80,96},{96,112},{112,0},{1... | collective-permute-start | bytes 491528 | tf_op jit(solution)/shard_map/ppermute | solution.py:603
  8.7 2.3 %collective-permute-start.1 = (bf16[128,640]{1,0:T(8,128)(2,1)S(1)}, bf16[128,640]{1,0:T(8,128)(2,1)S(1)}, u32[]{:S(2)}, u32[]{:S(2)}) collective-permute-start(bf16[128,640]{1,0:T(8,128)(2,1)S(1)} %get-tuple-element.22), channel_id=1, source_target_pairs={{16,0},{32,16},{48,32},{64,48},{80,64},{96,80},{112,96},{0,112},{1... | collective-permute-start | bytes 491528 | tf_op jit(solution)/shard_map/ppermute | solution.py:608
  10.9 0.0 copy-done.7
  10.9 0.0 copy-done.8
  10.9 0.0 copy-start
  10.9 0.0 copy-start.1
  11.0 0.0 copy-start.2
  11.0 0.0 copy-start.3
  11.0 0.0 copy-start.4
  11.0 2.4 %plan.1 = (f32[16,128,128]{2,1,0:T(8,128)S(1)}, bf16[2,1024,1024]{2,1,0:T(8,128)(2,1)S(1)}, bf16[1024,128]{1,0:T(8,128)(2,1)S(1)}) custom-call(s32[1,2048]{1,0:T(1,128)S(1)} %bitcast.21, s32[2,1,1,1024]{3,2,1,0:T(1,128)S(1)} %copy-done.8), custom_call_target="tpu_custom_call" | custom-call | flops 3000000000 | bytes 1048576 | tf_op jit(solution)/shard_map/plan/pallas_call | solution.py:176
  13.3 0.0 copy-done
  13.4 0.0 copy-done.1
  13.4 0.0 copy-done.2
  13.4 0.0 copy-done.3
  13.4 0.0 copy-done.4
  13.4 3.3 %piece_0.1._out = f32[4,18,144,128]{3,2,1,0:T(8,128)S(1)} custom-call(f32[4,18,144,128]{3,2,1,0:T(8,128)S(1)} %get-tuple-element.25.refs_0_._v, f32[2,18,144,128]{3,2,1,0:T(8,128)S(1)} %get-tuple-element.26.refs_1_._c, f32[16,128,128]{2,1,0:T(8,128)S(1)} %get-tuple-element.20.refs_2_.mask_ref, bf16[512,1024]{1,0:T(8,128)(2,1)S(1)} %copy-done.1, ...), custom_call_target="tpu_custom_call" | custom-call | flops 2000000000 | bytes 1048576 | tf_op jit(solution)/shard_map/piece_0/pallas_call | solution.py:390
  16.7 0.0 collective-permute-done.2.col_lo_ref
  16.7 0.0 collective-permute-done.3.col_hi_ref
  16.7 0.0 collective-permute-done.row_lo_ref
  16.7 0.0 collective-permute-done.1.row_hi_ref
  16.7 3.3 %rim.1 = (f32[4,18,144,128]{3,2,1,0:T(8,128)S(1)}, f32[2,18,144,128]{3,2,1,0:T(8,128)S(1)}, f32[4,18,144,128]{3,2,1,0:T(8,128)S(1)}, bf16[128,512]{1,0:T(8,128)(...) custom-call(f32[16,128,128]{2,1,0:T(8,128)S(1)} %get-tuple-element.2, ...), custom_call_target="tpu_custom_call", output_to_operand_aliasing={{0}: (10, {}), {1}: (11, {}), {2}: (12, {})} | custom-call | flops 3000000000 | bytes 4194304 | tf_op jit(solution)/shard_map/rim/pallas_call | solution.py:345
  20.1 3.6 %collective-permute-start.6 = (bf16[16,512]{1,0:T(8,128)(2,1)S(1)}, bf16[16,512]{1,0:T(8,128)(2,1)S(1)}, u32[]{:S(2)}, u32[]{:S(2)}) collective-permute-start(bf16[16,512]{1,0:T(8,128)(2,1)S(1)} %get-tuple-element.30), channel_id=1, source_target_pairs={{0,1},{1,2},{2,3},{3,4},{4,5},{5,6},{6,7},{7,8},{8,9},{9,10},{10,1... | collective-permute-start | bytes 49160 | tf_op jit(solution)/shard_map/ppermute | solution.py:613
  23.7 1.9 %collective-permute-start.7 = (bf16[16,512]{1,0:T(8,128)(2,1)S(1)}, bf16[16,512]{1,0:T(8,128)(2,1)S(1)}, u32[]{:S(2)}, u32[]{:S(2)}) collective-permute-start(bf16[16,512]{1,0:T(8,128)(2,1)S(1)} %get-tuple-element.31), channel_id=1, source_target_pairs={{1,0},{2,1},{3,2},{4,3},{5,4},{6,5},{7,6},{8,7},{9,8},{10,9},{11,1... | collective-permute-start | bytes 49160 | tf_op jit(solution)/shard_map/ppermute | solution.py:618
  25.6 0.0 collective-permute-start.4
  25.6 3.6 %collective-permute-start.5 = (bf16[128,512]{1,0:T(8,128)(2,1)S(1)}, bf16[128,512]{1,0:T(8,128)(2,1)S(1)}, u32[]{:S(2)}, u32[]{:S(2)}) collective-permute-start(bf16[128,512]{1,0:T(8,128)(2,1)S(1)} %get-tuple-element.29), channel_id=1, source_target_pairs={{16,0},{32,16},{48,32},{64,48},{80,64},{96,80},{112,96},{0,112},{1... | collective-permute-start | bytes 393224 | tf_op jit(solution)/shard_map/ppermute | solution.py:608
  29.2 5.7 %piece_1.1._ = f32[4,18,144,128]{3,2,1,0:T(8,128)S(1)} custom-call(f32[4,18,144,128]{3,2,1,0:T(8,128)S(1)} %get-tuple-element.34.refs_0_, f32[2,18,144,128]{3,2,1,0:T(8,128)S(1)} %get-tuple-element.27.refs_1_.c_ref, f32[16,128,128]{2,1,0:T(8,128)S(1)} %get-tuple-element.20.refs_2_.mask_ref, ...), custom_call_target="tpu_custom_call", output_to_operand_aliasing={{}: (8, {})} | custom-call | flops 6000000000 | bytes 1048576 | tf_op jit(solution)/shard_map/piece_1/pallas_call | solution.py:390
  34.9 0.0 collective-permute-done.6.col_lo_ref
  34.9 0.0 collective-permute-done.7.col_hi_ref
  34.9 0.0 collective-permute-done.4.row_lo_ref
  35.0 0.0 collective-permute-done.5.row_hi_ref
  35.0 14.8 %final.1 = (f32[4,18,144,128]{3,2,1,0:T(8,128)S(1)}, f32[4,16,128,128]{3,2,1,0:T(8,128)}, bf16[1024,1152]{1,0:T(8,128)(2,1)}) custom-call(f32[2,18,144,128]{3,2,1,0:T(8,128)S(1)} %get-tuple-element.27.refs_1_.c_ref, f32[16,128,128]{2,1,0:T(8,128)S(1)} %get-tuple-element.20.refs_2_.mask_ref, ...), custom_call_target="tpu_custom_call", output_to_operand_aliasing={{0}: (13, {})} | custom-call | flops 12000000000 | bytes 4194304 | tf_op jit(solution)/shard_map/final/pallas_call | solution.py:462
  49.8 9.3 %all-to-all-start = ((bf16[128,8,1152]{2,1,0:T(8,128)(2,1)}), bf16[128,8,1152]{2,1,0:T(8,128)(2,1)S(1)}, u32[]{:S(2)}, u32[]{:S(2)}) async-start(bf16[128,8,1152]{2,1,0:T(8,128)(2,1)} %bitcast.24), calls=%async_computation | async-start | bytes 4718592 | tf_op jit(solution)/shard_map/all_to_all | solution.py:639
  59.1 0.0 copy-start.5
  59.1 0.0 copy-start.6
  59.2 0.0 copy-start.9
  59.2 4.0 %unturn.1 = f32[8192,128]{1,0:T(8,128)} custom-call(f32[4,16,128,128]{3,2,1,0:T(8,128)} %get-tuple-element.36.t_hbm), custom_call_target="tpu_custom_call" | custom-call | flops 1000000000 | bytes 8388608 | tf_op jit(solution)/shard_map/unturn/pallas_call | solution.py:505
  63.1 28.7 %all-to-all-done = bf16[128,8,1152]{2,1,0:T(8,128)(2,1)S(1)} async-done(((bf16[128,8,1152]{2,1,0:T(8,128)(2,1)}), bf16[128,8,1152]{2,1,0:T(8,128)(2,1)S(1)}, u32[]{:S(2)}, u32[]{:S(2)}) %all-to-all-start) | async-done | bytes 2359328 | tf_op jit(solution)/shard_map/all_to_all | solution.py:639
  91.8 0.0 copy-done.5
  91.8 0.0 copy-done.6
  91.8 0.0 copy-done.9
  91.8 7.4 %chem.1 = bf16[2048,256]{1,0:T(8,128)(2,1)} custom-call(bf16[1024,1152]{1,0:T(8,128)(2,1)S(1)} %bitcast.11, bf16[2048,128]{1,0:T(8,128)(2,1)S(1)} %bitcast.20, bf16[256,1024]{1,0:T(8,128)(2,1)S(1)} %copy-done.6, f32[1,1024]{1,0:T(1,128)S(1)} %bitcast.22, bf16[1024,256]{1,0:T(8,128)(2,1)} %w2_hbm.1), custom_call_target="tpu_custom_call" | custom-call | flops 4400000000 | bytes 4194304 | tf_op jit(solution)/shard_map/chem/pallas_call | solution.py:574
Async XLA Ops:
  0.6 10.3 %copy-start.7 = (s32[1,1,2048]{2,1,0:T(1,128)S(1)}, s32[1,1,2048]{2,1,0:T(1,128)}, u32[]{:S(2)}) copy-start(s32[1,1,2048]{2,1,0:T(1,128)} %param.15) | copy-start | bytes 24580
  0.6 10.3 %copy-start.8 = (s32[2,1,1,1024]{3,2,1,0:T(1,128)S(1)}, s32[2,1,1,1024]{3,2,1,0:T(1,128)}, u32[]{:S(2)}) copy-start(s32[2,1,1,1024]{3,2,1,0:T(1,128)} %route_ref.1) | copy-start | bytes 24580
  4.3 12.4 %collective-permute-start.2 = (bf16[16,640]{1,0:T(8,128)(2,1)S(1)}, bf16[16,640]{1,0:T(8,128)(2,1)S(1)}, u32[]{:S(2)}, u32[]{:S(2)}) collective-permute-start(bf16[16,640]{1,0:T(8,128)(2,1)S(1)} %get-tuple-element.23), channel_id=1, source_target_pairs={{0,1},{1,2},{2,3},{3,4},{4,5},{5,6},{6,7},{7,8},{8,9},{9,10},{10,1... | collective-permute-start | bytes 61448 | tf_op jit(solution)/shard_map/ppermute | solution.py:613
  7.4 9.4 %collective-permute-start.3 = (bf16[16,640]{1,0:T(8,128)(2,1)S(1)}, bf16[16,640]{1,0:T(8,128)(2,1)S(1)}, u32[]{:S(2)}, u32[]{:S(2)}) collective-permute-start(bf16[16,640]{1,0:T(8,128)(2,1)S(1)} %get-tuple-element.24), channel_id=1, source_target_pairs={{1,0},{2,1},{3,2},{4,3},{5,4},{6,5},{7,6},{8,7},{9,8},{10,9},{11,1... | collective-permute-start | bytes 61448 | tf_op jit(solution)/shard_map/ppermute | solution.py:618
  7.4 9.4 %collective-permute-start = (bf16[128,640]{1,0:T(8,128)(2,1)S(1)}, bf16[128,640]{1,0:T(8,128)(2,1)S(1)}, u32[]{:S(2)}, u32[]{:S(2)}) collective-permute-start(bf16[128,640]{1,0:T(8,128)(2,1)S(1)} %get-tuple-element.21), channel_id=1, source_target_pairs={{0,16},{16,32},{32,48},{48,64},{64,80},{80,96},{96,112},{112,0},{1... | collective-permute-start | bytes 491528 | tf_op jit(solution)/shard_map/ppermute | solution.py:603
  8.7 8.1 %collective-permute-start.1 = (bf16[128,640]{1,0:T(8,128)(2,1)S(1)}, bf16[128,640]{1,0:T(8,128)(2,1)S(1)}, u32[]{:S(2)}, u32[]{:S(2)}) collective-permute-start(bf16[128,640]{1,0:T(8,128)(2,1)S(1)} %get-tuple-element.22), channel_id=1, source_target_pairs={{16,0},{32,16},{48,32},{64,48},{80,64},{96,80},{112,96},{0,112},{1... | collective-permute-start | bytes 491528 | tf_op jit(solution)/shard_map/ppermute | solution.py:608
  10.9 2.4 %copy-start = (bf16[1024,1024]{1,0:T(8,128)(2,1)S(1)}, bf16[1024,1024]{1,0:T(8,128)(2,1)}, u32[]{:S(2)}) copy-start(bf16[1024,1024]{1,0:T(8,128)(2,1)} %w2_ref.3) | copy-start | bytes 6291460
  10.9 2.4 %copy-start.1 = (bf16[512,1024]{1,0:T(8,128)(2,1)S(1)}, bf16[512,1024]{1,0:T(8,128)(2,1)}, u32[]{:S(2)}) copy-start(bf16[512,1024]{1,0:T(8,128)(2,1)} %w1_ref.4) | copy-start | bytes 3145732
  11.0 2.4 %copy-start.2 = (bf16[1024,512]{1,0:T(8,128)(2,1)S(1)}, bf16[1024,512]{1,0:T(8,128)(2,1)}, u32[]{:S(2)}) copy-start(bf16[1024,512]{1,0:T(8,128)(2,1)} %w3_ref.3) | copy-start | bytes 3145732
  11.0 2.4 %copy-start.3 = (f32[1024]{0:T(1024)S(1)}, f32[1024]{0:T(1024)}, u32[]{:S(2)}) copy-start(f32[1024]{0:T(1024)} %param.17) | copy-start | bytes 12292
  11.0 2.4 %copy-start.4 = (f32[1024]{0:T(1024)S(1)}, f32[1024]{0:T(1024)}, u32[]{:S(2)}) copy-start(f32[1024]{0:T(1024)} %param.19) | copy-start | bytes 12292
  20.1 14.8 %collective-permute-start.6 = (bf16[16,512]{1,0:T(8,128)(2,1)S(1)}, bf16[16,512]{1,0:T(8,128)(2,1)S(1)}, u32[]{:S(2)}, u32[]{:S(2)}) collective-permute-start(bf16[16,512]{1,0:T(8,128)(2,1)S(1)} %get-tuple-element.30), channel_id=1, source_target_pairs={{0,1},{1,2},{2,3},{3,4},{4,5},{5,6},{6,7},{7,8},{8,9},{9,10},{10,1... | collective-permute-start | bytes 49160 | tf_op jit(solution)/shard_map/ppermute | solution.py:613
  23.7 11.2 %collective-permute-start.7 = (bf16[16,512]{1,0:T(8,128)(2,1)S(1)}, bf16[16,512]{1,0:T(8,128)(2,1)S(1)}, u32[]{:S(2)}, u32[]{:S(2)}) collective-permute-start(bf16[16,512]{1,0:T(8,128)(2,1)S(1)} %get-tuple-element.31), channel_id=1, source_target_pairs={{1,0},{2,1},{3,2},{4,3},{5,4},{6,5},{7,6},{8,7},{9,8},{10,9},{11,1... | collective-permute-start | bytes 49160 | tf_op jit(solution)/shard_map/ppermute | solution.py:618
  25.6 9.3 %collective-permute-start.4 = (bf16[128,512]{1,0:T(8,128)(2,1)S(1)}, bf16[128,512]{1,0:T(8,128)(2,1)S(1)}, u32[]{:S(2)}, u32[]{:S(2)}) collective-permute-start(bf16[128,512]{1,0:T(8,128)(2,1)S(1)} %get-tuple-element.28), channel_id=1, source_target_pairs={{0,16},{16,32},{32,48},{48,64},{64,80},{80,96},{96,112},{112,0},{1... | collective-permute-start | bytes 393224 | tf_op jit(solution)/shard_map/ppermute | solution.py:603
  25.6 9.3 %collective-permute-start.5 = (bf16[128,512]{1,0:T(8,128)(2,1)S(1)}, bf16[128,512]{1,0:T(8,128)(2,1)S(1)}, u32[]{:S(2)}, u32[]{:S(2)}) collective-permute-start(bf16[128,512]{1,0:T(8,128)(2,1)S(1)} %get-tuple-element.29), channel_id=1, source_target_pairs={{16,0},{32,16},{48,32},{64,48},{80,64},{96,80},{112,96},{0,112},{1... | collective-permute-start | bytes 393224 | tf_op jit(solution)/shard_map/ppermute | solution.py:608
  49.8 42.0 %all-to-all-start = ((bf16[128,8,1152]{2,1,0:T(8,128)(2,1)}), bf16[128,8,1152]{2,1,0:T(8,128)(2,1)S(1)}, u32[]{:S(2)}, u32[]{:S(2)}) async-start(bf16[128,8,1152]{2,1,0:T(8,128)(2,1)} %bitcast.24), calls=%async_computation | async-start | bytes 4718592 | tf_op jit(solution)/shard_map/all_to_all | solution.py:639
  59.1 32.7 %copy-start.5 = (bf16[1,1,16,128,128]{4,3,2,1,0:T(8,128)(2,1)S(1)}, bf16[1,1,16,128,128]{4,3,2,1,0:T(8,128)(2,1)}, u32[]{:S(2)}) copy-start(bf16[1,1,16,128,128]{4,3,2,1,0:T(8,128)(2,1)} %param.22) | copy-start | bytes 1572868
  59.1 32.7 %copy-start.6 = (bf16[256,1024]{1,0:T(8,128)(2,1)S(1)}, bf16[256,1024]{1,0:T(8,128)(2,1)}, u32[]{:S(2)}) copy-start(bf16[256,1024]{1,0:T(8,128)(2,1)} %w1_ref.5) | copy-start | bytes 1572868
  59.2 32.7 %copy-start.9 = (f32[1024]{0:T(1024)S(1)}, f32[1024]{0:T(1024)}, u32[]{:S(2)}) copy-start(f32[1024]{0:T(1024)} %param.24) | copy-start | bytes 12292

commit v5 on v4

--- a/solution.py
+++ b/solution.py
@@ -17,7 +17,7 @@
 EDGE = 8
 GROUP = 8
 SPAN = 512
-PIECES = ((1, 5), (6, 9))
+PIECES = ((1, 6), (7, 8))
 INNER = COLS - 2 * EDGE
 RIM = 2 * COLS + (ROWS - 2) * 2 * EDGE
 MARGIN = (ROWS + 2, COLS + 2 * EDGE, LANES)
@@ -70,6 +70,12 @@
 
 def iota(shape, dim):
     return lax.broadcasted_iota(jnp.int32, shape, dim)
+
+
+def one_hot(rows, wanted):
+    short = jnp.broadcast_to(wanted, (16, wanted.shape[1])).astype(jnp.int16)[0:1]
+    match = lax.broadcasted_iota(jnp.int16, (rows, wanted.shape[1]), 0) == short
+    return jnp.where(match, jnp.ones((), BF16), jnp.zeros((), BF16))
 
 
 def turn_kernel(f_hbm, c_hbm, t_ref, cc_ref, row_lo_ref, row_hi_ref, col_lo_ref, col_hi_ref, f_ref, c_ref, sems):
@@ -136,8 +142,8 @@
 
 def plan_kernel(sun_ref, route_ref, mask_ref, place_ref, tags_ref):
     slots = sun_ref[...]
-    low = (iota((COLS, CELLS), 0) == (slots & (COLS - 1))).astype(F32).astype(BF16)
-    high = (iota((LANES, CELLS), 0) == (slots >> 7)).astype(F32).astype(BF16)
+    low = one_hot(COLS, slots & (COLS - 1))
+    high = one_hot(LANES, slots >> 7)
     lit = dot_nt(low, high)
     for r in range(ROWS):
         mask_ref[r] = jnp.broadcast_to(lit[:, r : r + 1], (COLS, LANES))
@@ -155,6 +161,7 @@
         carry = carry + dot(goes16, ones)
     rank = jnp.concatenate(ranks, axis=1).astype(jnp.int32)
     row = target * 16 + rank
+    halves = [jnp.where((row & 1) == q, row >> 1, -1) for q in range(2)]
     index = iota((LANES, SEGS), 0)
     coarse = (arrival >> 5).astype(F32)
     fine = (arrival & 31).astype(F32)
@@ -165,8 +172,7 @@
     for b in range(SEGS // LANES):
         tags = jnp.zeros((LANES, LANES), F32)
         for q in range(2):
-            want = 2 * (iota((LANES, SEGS), 0) + b * LANES) + q
-            chosen = (row == want).astype(F32).astype(BF16)
+            chosen = one_hot(LANES, halves[q] - b * LANES)
             place_ref[q, b * LANES : (b + 1) * LANES, :] = chosen
             tags = tags + dot_nt(chosen, tag_rows[q])
         tags_ref[b * LANES : (b + 1) * LANES, :] = tags.astype(BF16)

time: 99.6 us -> 99.2 us (level)
  no operation moved by 1% of the time
where the time goes in v5:
time: 99.2 us; the launch traced here: 99 us
  Pallas kernels  43.9 us (44%)
  waiting for transfers between devices  28.5 us (29%)
  starting transfers between devices  25.1 us (25%)
  between operations  1.02 us (1%)
    all_to_all x1, waiting for transfers between devices, local(): lax.all_to_all(packed, ('gx', 'gy'), split_axis=0, concat_axis=0, tiled=T...  28.5 us
    pallas_call x1, Pallas kernels, final(): pl.pallas_call(final_kernel, in_specs=[VMEM] * len(near), out_specs=[VMEM...  14.8 us
    all_to_all x1, starting transfers between devices, local(): lax.all_to_all(packed, ('gx', 'gy'), split_axis=0, concat_axis=0, tiled=T...  9.52 us
    pallas_call x2, Pallas kernels, piece(): pl.pallas_call(lambda *refs: piece_kernel(number, *refs), in_specs=[VMEM]...  9.01 us
    pallas_call x1, Pallas kernels, chem(): pl.pallas_call(chem_kernel, in_specs=[VMEM] * 4 + [HBM], out_specs=HBM, o...  7.37 us
    ppermute x2, starting transfers between devices, columns_right(): return lax.ppermute(x, 'gy', [(i, (i + 1) % count) for i in range(count)])  6.41 us
    ppermute x2, starting transfers between devices, rows_down(): return lax.ppermute(x, 'gx', [((i + 1) % count, i) for i in range(count)])  5.85 us
    pallas_call x1, Pallas kernels, unturn(): pl.pallas_call(unturn_kernel, in_specs=[HBM], out_specs=HBM, out_shape=hb...  3.97 us
  transfers between devices with their start and end apart: 9, of which 1 were waited for; matrix products, arithmetic and copies ran while one was open for 0% of the time, Pallas kernels for 15%

profile of v5, /device:TPU:1, one launch (start us, length us, event | category | flops | bytes accessed | tf_op | source)
XLA Modules:
  0.0 99.0 jit_solution(15112624731426750702)
XLA Ops:
  0.6 0.0 copy-start.7
  0.6 0.0 copy-start.8
  0.7 3.6 %turn.1 = (f32[4,18,144,128]{3,2,1,0:T(8,128)S(1)}, f32[2,18,144,128]{3,2,1,0:T(8,128)S(1)}, bf16[128,640]{1,0:T(8,128)(2,1)S(1)}, bf16[128,640]{1,0:T(8,128)(2,...) custom-call(f32[8192,128]{1,0:T(8,128)} %bitcast.25, f32[4096,128]{1,0:T(8,128)} %bitcast.26), custom_call_target="tpu_custom_call" | custom-call | flops 4000000000 | bytes 12582912 | tf_op jit(solution)/shard_map/turn/pallas_call | solution.py:120
  4.3 3.1 %collective-permute-start.2 = (bf16[16,640]{1,0:T(8,128)(2,1)S(1)}, bf16[16,640]{1,0:T(8,128)(2,1)S(1)}, u32[]{:S(2)}, u32[]{:S(2)}) collective-permute-start(bf16[16,640]{1,0:T(8,128)(2,1)S(1)} %get-tuple-element.23), channel_id=1, source_target_pairs={{0,1},{1,2},{2,3},{3,4},{4,5},{5,6},{6,7},{7,8},{8,9},{9,10},{10,1... | collective-permute-start | bytes 61448 | tf_op jit(solution)/shard_map/ppermute | solution.py:619
  7.4 0.0 collective-permute-start.3
  7.4 1.3 %collective-permute-start = (bf16[128,640]{1,0:T(8,128)(2,1)S(1)}, bf16[128,640]{1,0:T(8,128)(2,1)S(1)}, u32[]{:S(2)}, u32[]{:S(2)}) collective-permute-start(bf16[128,640]{1,0:T(8,128)(2,1)S(1)} %get-tuple-element.21), channel_id=1, source_target_pairs={{0,16},{16,32},{32,48},{48,64},{64,80},{80,96},{96,112},{112,0},{1... | collective-permute-start | bytes 491528 | tf_op jit(solution)/shard_map/ppermute | solution.py:609
  8.7 2.3 %collective-permute-start.1 = (bf16[128,640]{1,0:T(8,128)(2,1)S(1)}, bf16[128,640]{1,0:T(8,128)(2,1)S(1)}, u32[]{:S(2)}, u32[]{:S(2)}) collective-permute-start(bf16[128,640]{1,0:T(8,128)(2,1)S(1)} %get-tuple-element.22), channel_id=1, source_target_pairs={{16,0},{32,16},{48,32},{64,48},{80,64},{96,80},{112,96},{0,112},{1... | collective-permute-start | bytes 491528 | tf_op jit(solution)/shard_map/ppermute | solution.py:614
  10.9 0.0 copy-done.7
  10.9 0.0 copy-done.8
  10.9 0.0 copy-start
  10.9 0.0 copy-start.1
  11.0 0.0 copy-start.2
  11.0 0.0 copy-start.3
  11.0 0.0 copy-start.4
  11.0 1.8 %plan.1 = (f32[16,128,128]{2,1,0:T(8,128)S(1)}, bf16[2,1024,1024]{2,1,0:T(8,128)(2,1)S(1)}, bf16[1024,128]{1,0:T(8,128)(2,1)S(1)}) custom-call(s32[1,2048]{1,0:T(1,128)S(1)} %bitcast.21, s32[2,1,1,1024]{3,2,1,0:T(1,128)S(1)} %copy-done.8), custom_call_target="tpu_custom_call" | custom-call | flops 3000000000 | bytes 1048576 | tf_op jit(solution)/shard_map/plan/pallas_call | solution.py:182
  12.8 0.0 copy-done
  12.8 0.0 copy-done.1
  12.8 0.3 copy-done.2
  13.1 0.0 copy-done.3
  13.1 0.0 copy-done.4
  13.1 3.9 %piece_0.1._out = f32[4,18,144,128]{3,2,1,0:T(8,128)S(1)} custom-call(f32[4,18,144,128]{3,2,1,0:T(8,128)S(1)} %get-tuple-element.25.refs_0_._v, f32[2,18,144,128]{3,2,1,0:T(8,128)S(1)} %get-tuple-element.26.refs_1_._c, f32[16,128,128]{2,1,0:T(8,128)S(1)} %get-tuple-element.20.refs_2_.mask_ref, bf16[512,1024]{1,0:T(8,128)(2,1)S(1)} %copy-done.1, ...), custom_call_target="tpu_custom_call" | custom-call | flops 2000000000 | bytes 1048576 | tf_op jit(solution)/shard_map/piece_0/pallas_call | solution.py:396
  17.0 0.0 collective-permute-done.2.col_lo_ref
  17.0 0.0 collective-permute-done.3.col_hi_ref
  17.0 0.0 collective-permute-done.row_lo_ref
  17.1 0.0 collective-permute-done.1.row_hi_ref
  17.1 3.3 %rim.1 = (f32[4,18,144,128]{3,2,1,0:T(8,128)S(1)}, f32[2,18,144,128]{3,2,1,0:T(8,128)S(1)}, f32[4,18,144,128]{3,2,1,0:T(8,128)S(1)}, bf16[128,512]{1,0:T(8,128)(...) custom-call(f32[16,128,128]{2,1,0:T(8,128)S(1)} %get-tuple-element.2, ...), custom_call_target="tpu_custom_call", output_to_operand_aliasing={{0}: (10, {}), {1}: (11, {}), {2}: (12, {})} | custom-call | flops 3000000000 | bytes 4194304 | tf_op jit(solution)/shard_map/rim/pallas_call | solution.py:351
  20.4 3.3 %collective-permute-start.6 = (bf16[16,512]{1,0:T(8,128)(2,1)S(1)}, bf16[16,512]{1,0:T(8,128)(2,1)S(1)}, u32[]{:S(2)}, u32[]{:S(2)}) collective-permute-start(bf16[16,512]{1,0:T(8,128)(2,1)S(1)} %get-tuple-element.30), channel_id=1, source_target_pairs={{0,1},{1,2},{2,3},{3,4},{4,5},{5,6},{6,7},{7,8},{8,9},{9,10},{10,1... | collective-permute-start | bytes 49160 | tf_op jit(solution)/shard_map/ppermute | solution.py:619
  23.7 2.1 %collective-permute-start.7 = (bf16[16,512]{1,0:T(8,128)(2,1)S(1)}, bf16[16,512]{1,0:T(8,128)(2,1)S(1)}, u32[]{:S(2)}, u32[]{:S(2)}) collective-permute-start(bf16[16,512]{1,0:T(8,128)(2,1)S(1)} %get-tuple-element.31), channel_id=1, source_target_pairs={{1,0},{2,1},{3,2},{4,3},{5,4},{6,5},{7,6},{8,7},{9,8},{10,9},{11,1... | collective-permute-start | bytes 49160 | tf_op jit(solution)/shard_map/ppermute | solution.py:624
  25.8 0.0 collective-permute-start.4
  25.8 3.6 %collective-permute-start.5 = (bf16[128,512]{1,0:T(8,128)(2,1)S(1)}, bf16[128,512]{1,0:T(8,128)(2,1)S(1)}, u32[]{:S(2)}, u32[]{:S(2)}) collective-permute-start(bf16[128,512]{1,0:T(8,128)(2,1)S(1)} %get-tuple-element.29), channel_id=1, source_target_pairs={{16,0},{32,16},{48,32},{64,48},{80,64},{96,80},{112,96},{0,112},{1... | collective-permute-start | bytes 393224 | tf_op jit(solution)/shard_map/ppermute | solution.py:614
  29.4 5.1 %piece_1.1._ = f32[4,18,144,128]{3,2,1,0:T(8,128)S(1)} custom-call(f32[4,18,144,128]{3,2,1,0:T(8,128)S(1)} %get-tuple-element.34.refs_0_, f32[2,18,144,128]{3,2,1,0:T(8,128)S(1)} %get-tuple-element.27.refs_1_.c_ref, f32[16,128,128]{2,1,0:T(8,128)S(1)} %get-tuple-element.20.refs_2_.mask_ref, ...), custom_call_target="tpu_custom_call", output_to_operand_aliasing={{}: (8, {})} | custom-call | flops 6000000000 | bytes 1048576 | tf_op jit(solution)/shard_map/piece_1/pallas_call | solution.py:396
  34.5 0.0 collective-permute-done.6.col_lo_ref
  34.5 0.0 collective-permute-done.7.col_hi_ref
  34.5 0.0 collective-permute-done.4.row_lo_ref
  34.5 0.0 collective-permute-done.5.row_hi_ref
  34.5 14.8 %final.1 = (f32[4,18,144,128]{3,2,1,0:T(8,128)S(1)}, f32[4,16,128,128]{3,2,1,0:T(8,128)}, bf16[1024,1152]{1,0:T(8,128)(2,1)}) custom-call(f32[2,18,144,128]{3,2,1,0:T(8,128)S(1)} %get-tuple-element.27.refs_1_.c_ref, f32[16,128,128]{2,1,0:T(8,128)S(1)} %get-tuple-element.20.refs_2_.mask_ref, ...), custom_call_target="tpu_custom_call", output_to_operand_aliasing={{0}: (13, {})} | custom-call | flops 12000000000 | bytes 4194304 | tf_op jit(solution)/shard_map/final/pallas_call | solution.py:468
  49.3 9.5 %all-to-all-start = ((bf16[128,8,1152]{2,1,0:T(8,128)(2,1)}), bf16[128,8,1152]{2,1,0:T(8,128)(2,1)S(1)}, u32[]{:S(2)}, u32[]{:S(2)}) async-start(bf16[128,8,1152]{2,1,0:T(8,128)(2,1)} %bitcast.24), calls=%async_computation | async-start | bytes 4718592 | tf_op jit(solution)/shard_map/all_to_all | solution.py:645
  58.9 0.0 copy-start.5
  58.9 0.0 copy-start.6
  58.9 0.0 copy-start.9
  58.9 4.0 %unturn.1 = f32[8192,128]{1,0:T(8,128)} custom-call(f32[4,16,128,128]{3,2,1,0:T(8,128)} %get-tuple-element.36.t_hbm), custom_call_target="tpu_custom_call" | custom-call | flops 1000000000 | bytes 8388608 | tf_op jit(solution)/shard_map/unturn/pallas_call | solution.py:511
  62.9 28.5 %all-to-all-done = bf16[128,8,1152]{2,1,0:T(8,128)(2,1)S(1)} async-done(((bf16[128,8,1152]{2,1,0:T(8,128)(2,1)}), bf16[128,8,1152]{2,1,0:T(8,128)(2,1)S(1)}, u32[]{:S(2)}, u32[]{:S(2)}) %all-to-all-start) | async-done | bytes 2359328 | tf_op jit(solution)/shard_map/all_to_all | solution.py:645
  91.4 0.0 copy-done.5
  91.4 0.0 copy-done.6
  91.4 0.0 copy-done.9
  91.4 7.4 %chem.1 = bf16[2048,256]{1,0:T(8,128)(2,1)} custom-call(bf16[1024,1152]{1,0:T(8,128)(2,1)S(1)} %bitcast.11, bf16[2048,128]{1,0:T(8,128)(2,1)S(1)} %bitcast.20, bf16[256,1024]{1,0:T(8,128)(2,1)S(1)} %copy-done.6, f32[1,1024]{1,0:T(1,128)S(1)} %bitcast.22, bf16[1024,256]{1,0:T(8,128)(2,1)} %w2_hbm.1), custom_call_target="tpu_custom_call" | custom-call | flops 4400000000 | bytes 4194304 | tf_op jit(solution)/shard_map/chem/pallas_call | solution.py:580
Async XLA Ops:
  0.6 10.3 %copy-start.7 = (s32[1,1,2048]{2,1,0:T(1,128)S(1)}, s32[1,1,2048]{2,1,0:T(1,128)}, u32[]{:S(2)}) copy-start(s32[1,1,2048]{2,1,0:T(1,128)} %param.15) | copy-start | bytes 24580
  0.6 10.3 %copy-start.8 = (s32[2,1,1,1024]{3,2,1,0:T(1,128)S(1)}, s32[2,1,1,1024]{3,2,1,0:T(1,128)}, u32[]{:S(2)}) copy-start(s32[2,1,1,1024]{3,2,1,0:T(1,128)} %route_ref.1) | copy-start | bytes 24580
  4.3 12.8 %collective-permute-start.2 = (bf16[16,640]{1,0:T(8,128)(2,1)S(1)}, bf16[16,640]{1,0:T(8,128)(2,1)S(1)}, u32[]{:S(2)}, u32[]{:S(2)}) collective-permute-start(bf16[16,640]{1,0:T(8,128)(2,1)S(1)} %get-tuple-element.23), channel_id=1, source_target_pairs={{0,1},{1,2},{2,3},{3,4},{4,5},{5,6},{6,7},{7,8},{8,9},{9,10},{10,1... | collective-permute-start | bytes 61448 | tf_op jit(solution)/shard_map/ppermute | solution.py:619
  7.4 9.7 %collective-permute-start.3 = (bf16[16,640]{1,0:T(8,128)(2,1)S(1)}, bf16[16,640]{1,0:T(8,128)(2,1)S(1)}, u32[]{:S(2)}, u32[]{:S(2)}) collective-permute-start(bf16[16,640]{1,0:T(8,128)(2,1)S(1)} %get-tuple-element.24), channel_id=1, source_target_pairs={{1,0},{2,1},{3,2},{4,3},{5,4},{6,5},{7,6},{8,7},{9,8},{10,9},{11,1... | collective-permute-start | bytes 61448 | tf_op jit(solution)/shard_map/ppermute | solution.py:624
  7.4 9.7 %collective-permute-start = (bf16[128,640]{1,0:T(8,128)(2,1)S(1)}, bf16[128,640]{1,0:T(8,128)(2,1)S(1)}, u32[]{:S(2)}, u32[]{:S(2)}) collective-permute-start(bf16[128,640]{1,0:T(8,128)(2,1)S(1)} %get-tuple-element.21), channel_id=1, source_target_pairs={{0,16},{16,32},{32,48},{48,64},{64,80},{80,96},{96,112},{112,0},{1... | collective-permute-start | bytes 491528 | tf_op jit(solution)/shard_map/ppermute | solution.py:609
  8.7 8.4 %collective-permute-start.1 = (bf16[128,640]{1,0:T(8,128)(2,1)S(1)}, bf16[128,640]{1,0:T(8,128)(2,1)S(1)}, u32[]{:S(2)}, u32[]{:S(2)}) collective-permute-start(bf16[128,640]{1,0:T(8,128)(2,1)S(1)} %get-tuple-element.22), channel_id=1, source_target_pairs={{16,0},{32,16},{48,32},{64,48},{80,64},{96,80},{112,96},{0,112},{1... | collective-permute-start | bytes 491528 | tf_op jit(solution)/shard_map/ppermute | solution.py:614
  10.9 1.8 %copy-start = (bf16[1024,1024]{1,0:T(8,128)(2,1)S(1)}, bf16[1024,1024]{1,0:T(8,128)(2,1)}, u32[]{:S(2)}) copy-start(bf16[1024,1024]{1,0:T(8,128)(2,1)} %w2_ref.3) | copy-start | bytes 6291460
  10.9 1.9 %copy-start.1 = (bf16[512,1024]{1,0:T(8,128)(2,1)S(1)}, bf16[512,1024]{1,0:T(8,128)(2,1)}, u32[]{:S(2)}) copy-start(bf16[512,1024]{1,0:T(8,128)(2,1)} %w1_ref.4) | copy-start | bytes 3145732
  11.0 2.2 %copy-start.2 = (bf16[1024,512]{1,0:T(8,128)(2,1)S(1)}, bf16[1024,512]{1,0:T(8,128)(2,1)}, u32[]{:S(2)}) copy-start(bf16[1024,512]{1,0:T(8,128)(2,1)} %w3_ref.3) | copy-start | bytes 3145732
  11.0 2.2 %copy-start.3 = (f32[1024]{0:T(1024)S(1)}, f32[1024]{0:T(1024)}, u32[]{:S(2)}) copy-start(f32[1024]{0:T(1024)} %param.17) | copy-start | bytes 12292
  11.0 2.1 %copy-start.4 = (f32[1024]{0:T(1024)S(1)}, f32[1024]{0:T(1024)}, u32[]{:S(2)}) copy-start(f32[1024]{0:T(1024)} %param.19) | copy-start | bytes 12292
  20.4 14.1 %collective-permute-start.6 = (bf16[16,512]{1,0:T(8,128)(2,1)S(1)}, bf16[16,512]{1,0:T(8,128)(2,1)S(1)}, u32[]{:S(2)}, u32[]{:S(2)}) collective-permute-start(bf16[16,512]{1,0:T(8,128)(2,1)S(1)} %get-tuple-element.30), channel_id=1, source_target_pairs={{0,1},{1,2},{2,3},{3,4},{4,5},{5,6},{6,7},{7,8},{8,9},{9,10},{10,1... | collective-permute-start | bytes 49160 | tf_op jit(solution)/shard_map/ppermute | solution.py:619
  23.7 10.8 %collective-permute-start.7 = (bf16[16,512]{1,0:T(8,128)(2,1)S(1)}, bf16[16,512]{1,0:T(8,128)(2,1)S(1)}, u32[]{:S(2)}, u32[]{:S(2)}) collective-permute-start(bf16[16,512]{1,0:T(8,128)(2,1)S(1)} %get-tuple-element.31), channel_id=1, source_target_pairs={{1,0},{2,1},{3,2},{4,3},{5,4},{6,5},{7,6},{8,7},{9,8},{10,9},{11,1... | collective-permute-start | bytes 49160 | tf_op jit(solution)/shard_map/ppermute | solution.py:624
  25.8 8.7 %collective-permute-start.4 = (bf16[128,512]{1,0:T(8,128)(2,1)S(1)}, bf16[128,512]{1,0:T(8,128)(2,1)S(1)}, u32[]{:S(2)}, u32[]{:S(2)}) collective-permute-start(bf16[128,512]{1,0:T(8,128)(2,1)S(1)} %get-tuple-element.28), channel_id=1, source_target_pairs={{0,16},{16,32},{32,48},{48,64},{64,80},{80,96},{96,112},{112,0},{1... | collective-permute-start | bytes 393224 | tf_op jit(solution)/shard_map/ppermute | solution.py:609
  25.8 8.7 %collective-permute-start.5 = (bf16[128,512]{1,0:T(8,128)(2,1)S(1)}, bf16[128,512]{1,0:T(8,128)(2,1)S(1)}, u32[]{:S(2)}, u32[]{:S(2)}) collective-permute-start(bf16[128,512]{1,0:T(8,128)(2,1)S(1)} %get-tuple-element.29), channel_id=1, source_target_pairs={{16,0},{32,16},{48,32},{64,48},{80,64},{96,80},{112,96},{0,112},{1... | collective-permute-start | bytes 393224 | tf_op jit(solution)/shard_map/ppermute | solution.py:614
  49.3 42.0 %all-to-all-start = ((bf16[128,8,1152]{2,1,0:T(8,128)(2,1)}), bf16[128,8,1152]{2,1,0:T(8,128)(2,1)S(1)}, u32[]{:S(2)}, u32[]{:S(2)}) async-start(bf16[128,8,1152]{2,1,0:T(8,128)(2,1)} %bitcast.24), calls=%async_computation | async-start | bytes 4718592 | tf_op jit(solution)/shard_map/all_to_all | solution.py:645
  58.9 32.5 %copy-start.5 = (bf16[1,1,16,128,128]{4,3,2,1,0:T(8,128)(2,1)S(1)}, bf16[1,1,16,128,128]{4,3,2,1,0:T(8,128)(2,1)}, u32[]{:S(2)}) copy-start(bf16[1,1,16,128,128]{4,3,2,1,0:T(8,128)(2,1)} %param.22) | copy-start | bytes 1572868
  58.9 32.5 %copy-start.6 = (bf16[256,1024]{1,0:T(8,128)(2,1)S(1)}, bf16[256,1024]{1,0:T(8,128)(2,1)}, u32[]{:S(2)}) copy-start(bf16[256,1024]{1,0:T(8,128)(2,1)} %w1_ref.5) | copy-start | bytes 1572868
  58.9 32.5 %copy-start.9 = (f32[1024]{0:T(1024)S(1)}, f32[1024]{0:T(1024)}, u32[]{:S(2)}) copy-start(f32[1024]{0:T(1024)} %param.24) | copy-start | bytes 12292

commit v6 on v5

--- a/solution.py
+++ b/solution.py
@@ -189,7 +189,7 @@
             vmem_out((SEGS, LANES), BF16),
         ],
         compiler_params=params(10),
-        cost_estimate=cost(3_000_000_000, 1 << 20),
+        cost_estimate=cost(300_000_000, 1 << 20),
         name="plan",
     )(sun_columns.reshape(1, CELLS), segment_route)
 

time: 99.2 us -> 99 us (level)
  no operation moved by 1% of the time
where the time goes in v6:
time: 99 us; the launch traced here: 98.8 us
  Pallas kernels  44 us (44%)
  waiting for transfers between devices  28.5 us (29%)
  starting transfers between devices  25.1 us (25%)
  between operations  1.06 us (1%)
    all_to_all x1, waiting for transfers between devices, local(): lax.all_to_all(packed, ('gx', 'gy'), split_axis=0, concat_axis=0, tiled=T...  28.5 us
    pallas_call x1, Pallas kernels, final(): pl.pallas_call(final_kernel, in_specs=[VMEM] * len(near), out_specs=[VMEM...  14.8 us
    all_to_all x1, starting transfers between devices, local(): lax.all_to_all(packed, ('gx', 'gy'), split_axis=0, concat_axis=0, tiled=T...  9.53 us
    pallas_call x2, Pallas kernels, piece(): pl.pallas_call(lambda *refs: piece_kernel(number, *refs), in_specs=[VMEM]...  9.01 us
    pallas_call x1, Pallas kernels, chem(): pl.pallas_call(chem_kernel, in_specs=[VMEM] * 4 + [HBM], out_specs=HBM, o...  7.37 us
    ppermute x2, starting transfers between devices, columns_right(): return lax.ppermute(x, 'gy', [(i, (i + 1) % count) for i in range(count)])  6.77 us
    ppermute x2, starting transfers between devices, rows_down(): return lax.ppermute(x, 'gx', [((i + 1) % count, i) for i in range(count)])  5.85 us
    pallas_call x1, Pallas kernels, unturn(): pl.pallas_call(unturn_kernel, in_specs=[HBM], out_specs=HBM, out_shape=hb...  3.97 us
  transfers between devices with their start and end apart: 9, of which 1 were waited for; matrix products, arithmetic and copies ran while one was open for 0% of the time, Pallas kernels for 15%

profile of v6, /device:TPU:1, one launch (start us, length us, event | category | flops | bytes accessed | tf_op | source)
XLA Modules:
  0.0 98.8 jit_solution(3305243282836008234)
XLA Ops:
  0.6 0.0 copy-start.7
  0.6 0.0 copy-start.8
  0.7 0.0 copy-start
  0.7 0.0 copy-start.1
  0.7 0.0 copy-start.2
  0.7 0.0 copy-start.3
  0.7 0.0 copy-start.4
  0.7 3.7 %turn.1 = (f32[4,18,144,128]{3,2,1,0:T(8,128)S(1)}, f32[2,18,144,128]{3,2,1,0:T(8,128)S(1)}, bf16[128,640]{1,0:T(8,128)(2,1)S(1)}, bf16[128,640]{1,0:T(8,128)(2,...) custom-call(f32[8192,128]{1,0:T(8,128)} %bitcast.25, f32[4096,128]{1,0:T(8,128)} %bitcast.26), custom_call_target="tpu_custom_call" | custom-call | flops 4000000000 | bytes 12582912 | tf_op jit(solution)/shard_map/turn/pallas_call | solution.py:120
  4.5 3.1 %collective-permute-start.2 = (bf16[16,640]{1,0:T(8,128)(2,1)S(1)}, bf16[16,640]{1,0:T(8,128)(2,1)S(1)}, u32[]{:S(2)}, u32[]{:S(2)}) collective-permute-start(bf16[16,640]{1,0:T(8,128)(2,1)S(1)} %get-tuple-element.23), channel_id=1, source_target_pairs={{0,1},{1,2},{2,3},{3,4},{4,5},{5,6},{6,7},{7,8},{8,9},{9,10},{10,1... | collective-permute-start | bytes 61448 | tf_op jit(solution)/shard_map/ppermute | solution.py:619
  7.6 0.0 collective-permute-start.3
  7.6 1.3 %collective-permute-start = (bf16[128,640]{1,0:T(8,128)(2,1)S(1)}, bf16[128,640]{1,0:T(8,128)(2,1)S(1)}, u32[]{:S(2)}, u32[]{:S(2)}) collective-permute-start(bf16[128,640]{1,0:T(8,128)(2,1)S(1)} %get-tuple-element.21), channel_id=1, source_target_pairs={{0,16},{16,32},{32,48},{48,64},{64,80},{80,96},{96,112},{112,0},{1... | collective-permute-start | bytes 491528 | tf_op jit(solution)/shard_map/ppermute | solution.py:609
  8.9 2.3 %collective-permute-start.1 = (bf16[128,640]{1,0:T(8,128)(2,1)S(1)}, bf16[128,640]{1,0:T(8,128)(2,1)S(1)}, u32[]{:S(2)}, u32[]{:S(2)}) collective-permute-start(bf16[128,640]{1,0:T(8,128)(2,1)S(1)} %get-tuple-element.22), channel_id=1, source_target_pairs={{16,0},{32,16},{48,32},{64,48},{80,64},{96,80},{112,96},{0,112},{1... | collective-permute-start | bytes 491528 | tf_op jit(solution)/shard_map/ppermute | solution.py:614
  11.1 0.0 copy-done.7
  11.1 0.0 copy-done.8
  11.1 1.8 %plan.1 = (f32[16,128,128]{2,1,0:T(8,128)S(1)}, bf16[2,1024,1024]{2,1,0:T(8,128)(2,1)S(1)}, bf16[1024,128]{1,0:T(8,128)(2,1)S(1)}) custom-call(s32[1,2048]{1,0:T(1,128)S(1)} %bitcast.21, s32[2,1,1,1024]{3,2,1,0:T(1,128)S(1)} %copy-done.8), custom_call_target="tpu_custom_call" | custom-call | flops 300000000 | bytes 1048576 | tf_op jit(solution)/shard_map/plan/pallas_call | solution.py:182
  12.9 0.0 copy-done
  12.9 0.0 copy-done.1
  12.9 0.0 copy-done.2
  12.9 0.0 copy-done.3
  12.9 0.0 copy-done.4
  12.9 3.9 %piece_0.1._out = f32[4,18,144,128]{3,2,1,0:T(8,128)S(1)} custom-call(f32[4,18,144,128]{3,2,1,0:T(8,128)S(1)} %get-tuple-element.25.refs_0_._v, f32[2,18,144,128]{3,2,1,0:T(8,128)S(1)} %get-tuple-element.26.refs_1_._c, f32[16,128,128]{2,1,0:T(8,128)S(1)} %get-tuple-element.20.refs_2_.mask_ref, bf16[512,1024]{1,0:T(8,128)(2,1)S(1)} %copy-done.1, ...), custom_call_target="tpu_custom_call" | custom-call | flops 2000000000 | bytes 1048576 | tf_op jit(solution)/shard_map/piece_0/pallas_call | solution.py:396
  16.8 0.0 collective-permute-done.2.col_lo_ref
  16.9 0.0 collective-permute-done.3.col_hi_ref
  16.9 0.0 collective-permute-done.row_lo_ref
  16.9 0.0 collective-permute-done.1.row_hi_ref
  16.9 3.3 %rim.1 = (f32[4,18,144,128]{3,2,1,0:T(8,128)S(1)}, f32[2,18,144,128]{3,2,1,0:T(8,128)S(1)}, f32[4,18,144,128]{3,2,1,0:T(8,128)S(1)}, bf16[128,512]{1,0:T(8,128)(...) custom-call(f32[16,128,128]{2,1,0:T(8,128)S(1)} %get-tuple-element.2, ...), custom_call_target="tpu_custom_call", output_to_operand_aliasing={{0}: (10, {}), {1}: (11, {}), {2}: (12, {})} | custom-call | flops 3000000000 | bytes 4194304 | tf_op jit(solution)/shard_map/rim/pallas_call | solution.py:351
  20.2 3.7 %collective-permute-start.6 = (bf16[16,512]{1,0:T(8,128)(2,1)S(1)}, bf16[16,512]{1,0:T(8,128)(2,1)S(1)}, u32[]{:S(2)}, u32[]{:S(2)}) collective-permute-start(bf16[16,512]{1,0:T(8,128)(2,1)S(1)} %get-tuple-element.30), channel_id=1, source_target_pairs={{0,1},{1,2},{2,3},{3,4},{4,5},{5,6},{6,7},{7,8},{8,9},{9,10},{10,1... | collective-permute-start | bytes 49160 | tf_op jit(solution)/shard_map/ppermute | solution.py:619
  23.9 1.7 %collective-permute-start.7 = (bf16[16,512]{1,0:T(8,128)(2,1)S(1)}, bf16[16,512]{1,0:T(8,128)(2,1)S(1)}, u32[]{:S(2)}, u32[]{:S(2)}) collective-permute-start(bf16[16,512]{1,0:T(8,128)(2,1)S(1)} %get-tuple-element.31), channel_id=1, source_target_pairs={{1,0},{2,1},{3,2},{4,3},{5,4},{6,5},{7,6},{8,7},{9,8},{10,9},{11,1... | collective-permute-start | bytes 49160 | tf_op jit(solution)/shard_map/ppermute | solution.py:624
  25.6 0.0 collective-permute-start.4
  25.6 3.6 %collective-permute-start.5 = (bf16[128,512]{1,0:T(8,128)(2,1)S(1)}, bf16[128,512]{1,0:T(8,128)(2,1)S(1)}, u32[]{:S(2)}, u32[]{:S(2)}) collective-permute-start(bf16[128,512]{1,0:T(8,128)(2,1)S(1)} %get-tuple-element.29), channel_id=1, source_target_pairs={{16,0},{32,16},{48,32},{64,48},{80,64},{96,80},{112,96},{0,112},{1... | collective-permute-start | bytes 393224 | tf_op jit(solution)/shard_map/ppermute | solution.py:614
  29.2 5.1 %piece_1.1._ = f32[4,18,144,128]{3,2,1,0:T(8,128)S(1)} custom-call(f32[4,18,144,128]{3,2,1,0:T(8,128)S(1)} %get-tuple-element.34.refs_0_, f32[2,18,144,128]{3,2,1,0:T(8,128)S(1)} %get-tuple-element.27.refs_1_.c_ref, f32[16,128,128]{2,1,0:T(8,128)S(1)} %get-tuple-element.20.refs_2_.mask_ref, ...), custom_call_target="tpu_custom_call", output_to_operand_aliasing={{}: (8, {})} | custom-call | flops 6000000000 | bytes 1048576 | tf_op jit(solution)/shard_map/piece_1/pallas_call | solution.py:396
  34.3 0.0 collective-permute-done.6.col_lo_ref
  34.3 0.0 collective-permute-done.7.col_hi_ref
  34.3 0.0 collective-permute-done.4.row_lo_ref
  34.3 0.0 collective-permute-done.5.row_hi_ref
  34.3 14.8 %final.1 = (f32[4,18,144,128]{3,2,1,0:T(8,128)S(1)}, f32[4,16,128,128]{3,2,1,0:T(8,128)}, bf16[1024,1152]{1,0:T(8,128)(2,1)}) custom-call(f32[2,18,144,128]{3,2,1,0:T(8,128)S(1)} %get-tuple-element.27.refs_1_.c_ref, f32[16,128,128]{2,1,0:T(8,128)S(1)} %get-tuple-element.20.refs_2_.mask_ref, ...), custom_call_target="tpu_custom_call", output_to_operand_aliasing={{0}: (13, {})} | custom-call | flops 12000000000 | bytes 4194304 | tf_op jit(solution)/shard_map/final/pallas_call | solution.py:468
  49.2 9.5 %all-to-all-start = ((bf16[128,8,1152]{2,1,0:T(8,128)(2,1)}), bf16[128,8,1152]{2,1,0:T(8,128)(2,1)S(1)}, u32[]{:S(2)}, u32[]{:S(2)}) async-start(bf16[128,8,1152]{2,1,0:T(8,128)(2,1)} %bitcast.24), calls=%async_computation | async-start | bytes 4718592 | tf_op jit(solution)/shard_map/all_to_all | solution.py:645
  58.7 0.0 copy-start.5
  58.7 0.0 copy-start.6
  58.7 0.0 copy-start.9
  58.7 4.0 %unturn.1 = f32[8192,128]{1,0:T(8,128)} custom-call(f32[4,16,128,128]{3,2,1,0:T(8,128)} %get-tuple-element.36.t_hbm), custom_call_target="tpu_custom_call" | custom-call | flops 1000000000 | bytes 8388608 | tf_op jit(solution)/shard_map/unturn/pallas_call | solution.py:511
  62.7 28.5 %all-to-all-done = bf16[128,8,1152]{2,1,0:T(8,128)(2,1)S(1)} async-done(((bf16[128,8,1152]{2,1,0:T(8,128)(2,1)}), bf16[128,8,1152]{2,1,0:T(8,128)(2,1)S(1)}, u32[]{:S(2)}, u32[]{:S(2)}) %all-to-all-start) | async-done | bytes 2359328 | tf_op jit(solution)/shard_map/all_to_all | solution.py:645
  91.2 0.0 copy-done.5
  91.2 0.0 copy-done.6
  91.2 0.0 copy-done.9
  91.2 7.4 %chem.1 = bf16[2048,256]{1,0:T(8,128)(2,1)} custom-call(bf16[1024,1152]{1,0:T(8,128)(2,1)S(1)} %bitcast.11, bf16[2048,128]{1,0:T(8,128)(2,1)S(1)} %bitcast.20, bf16[256,1024]{1,0:T(8,128)(2,1)S(1)} %copy-done.6, f32[1,1024]{1,0:T(1,128)S(1)} %bitcast.22, bf16[1024,256]{1,0:T(8,128)(2,1)} %w2_hbm.1), custom_call_target="tpu_custom_call" | custom-call | flops 4400000000 | bytes 4194304 | tf_op jit(solution)/shard_map/chem/pallas_call | solution.py:580
Async XLA Ops:
  0.6 10.5 %copy-start.7 = (s32[1,1,2048]{2,1,0:T(1,128)S(1)}, s32[1,1,2048]{2,1,0:T(1,128)}, u32[]{:S(2)}) copy-start(s32[1,1,2048]{2,1,0:T(1,128)} %param.15) | copy-start | bytes 24580
  0.6 10.5 %copy-start.8 = (s32[2,1,1,1024]{3,2,1,0:T(1,128)S(1)}, s32[2,1,1,1024]{3,2,1,0:T(1,128)}, u32[]{:S(2)}) copy-start(s32[2,1,1,1024]{3,2,1,0:T(1,128)} %route_ref.1) | copy-start | bytes 24580
  0.7 12.2 %copy-start = (bf16[1024,1024]{1,0:T(8,128)(2,1)S(1)}, bf16[1024,1024]{1,0:T(8,128)(2,1)}, u32[]{:S(2)}) copy-start(bf16[1024,1024]{1,0:T(8,128)(2,1)} %w2_ref.3) | copy-start | bytes 6291460
  0.7 12.2 %copy-start.1 = (bf16[512,1024]{1,0:T(8,128)(2,1)S(1)}, bf16[512,1024]{1,0:T(8,128)(2,1)}, u32[]{:S(2)}) copy-start(bf16[512,1024]{1,0:T(8,128)(2,1)} %w1_ref.4) | copy-start | bytes 3145732
  0.7 12.2 %copy-start.2 = (bf16[1024,512]{1,0:T(8,128)(2,1)S(1)}, bf16[1024,512]{1,0:T(8,128)(2,1)}, u32[]{:S(2)}) copy-start(bf16[1024,512]{1,0:T(8,128)(2,1)} %w3_ref.3) | copy-start | bytes 3145732
  0.7 12.2 %copy-start.3 = (f32[1024]{0:T(1024)S(1)}, f32[1024]{0:T(1024)}, u32[]{:S(2)}) copy-start(f32[1024]{0:T(1024)} %param.17) | copy-start | bytes 12292
  0.7 12.2 %copy-start.4 = (f32[1024]{0:T(1024)S(1)}, f32[1024]{0:T(1024)}, u32[]{:S(2)}) copy-start(f32[1024]{0:T(1024)} %param.19) | copy-start | bytes 12292
  4.5 12.4 %collective-permute-start.2 = (bf16[16,640]{1,0:T(8,128)(2,1)S(1)}, bf16[16,640]{1,0:T(8,128)(2,1)S(1)}, u32[]{:S(2)}, u32[]{:S(2)}) collective-permute-start(bf16[16,640]{1,0:T(8,128)(2,1)S(1)} %get-tuple-element.23), channel_id=1, source_target_pairs={{0,1},{1,2},{2,3},{3,4},{4,5},{5,6},{6,7},{7,8},{8,9},{9,10},{10,1... | collective-permute-start | bytes 61448 | tf_op jit(solution)/shard_map/ppermute | solution.py:619
  7.6 9.3 %collective-permute-start.3 = (bf16[16,640]{1,0:T(8,128)(2,1)S(1)}, bf16[16,640]{1,0:T(8,128)(2,1)S(1)}, u32[]{:S(2)}, u32[]{:S(2)}) collective-permute-start(bf16[16,640]{1,0:T(8,128)(2,1)S(1)} %get-tuple-element.24), channel_id=1, source_target_pairs={{1,0},{2,1},{3,2},{4,3},{5,4},{6,5},{7,6},{8,7},{9,8},{10,9},{11,1... | collective-permute-start | bytes 61448 | tf_op jit(solution)/shard_map/ppermute | solution.py:624
  7.6 9.3 %collective-permute-start = (bf16[128,640]{1,0:T(8,128)(2,1)S(1)}, bf16[128,640]{1,0:T(8,128)(2,1)S(1)}, u32[]{:S(2)}, u32[]{:S(2)}) collective-permute-start(bf16[128,640]{1,0:T(8,128)(2,1)S(1)} %get-tuple-element.21), channel_id=1, source_target_pairs={{0,16},{16,32},{32,48},{48,64},{64,80},{80,96},{96,112},{112,0},{1... | collective-permute-start | bytes 491528 | tf_op jit(solution)/shard_map/ppermute | solution.py:609
  8.9 8.0 %collective-permute-start.1 = (bf16[128,640]{1,0:T(8,128)(2,1)S(1)}, bf16[128,640]{1,0:T(8,128)(2,1)S(1)}, u32[]{:S(2)}, u32[]{:S(2)}) collective-permute-start(bf16[128,640]{1,0:T(8,128)(2,1)S(1)} %get-tuple-element.22), channel_id=1, source_target_pairs={{16,0},{32,16},{48,32},{64,48},{80,64},{96,80},{112,96},{0,112},{1... | collective-permute-start | bytes 491528 | tf_op jit(solution)/shard_map/ppermute | solution.py:614
  20.2 14.1 %collective-permute-start.6 = (bf16[16,512]{1,0:T(8,128)(2,1)S(1)}, bf16[16,512]{1,0:T(8,128)(2,1)S(1)}, u32[]{:S(2)}, u32[]{:S(2)}) collective-permute-start(bf16[16,512]{1,0:T(8,128)(2,1)S(1)} %get-tuple-element.30), channel_id=1, source_target_pairs={{0,1},{1,2},{2,3},{3,4},{4,5},{5,6},{6,7},{7,8},{8,9},{9,10},{10,1... | collective-permute-start | bytes 49160 | tf_op jit(solution)/shard_map/ppermute | solution.py:619
  23.9 10.4 %collective-permute-start.7 = (bf16[16,512]{1,0:T(8,128)(2,1)S(1)}, bf16[16,512]{1,0:T(8,128)(2,1)S(1)}, u32[]{:S(2)}, u32[]{:S(2)}) collective-permute-start(bf16[16,512]{1,0:T(8,128)(2,1)S(1)} %get-tuple-element.31), channel_id=1, source_target_pairs={{1,0},{2,1},{3,2},{4,3},{5,4},{6,5},{7,6},{8,7},{9,8},{10,9},{11,1... | collective-permute-start | bytes 49160 | tf_op jit(solution)/shard_map/ppermute | solution.py:624
  25.6 8.7 %collective-permute-start.4 = (bf16[128,512]{1,0:T(8,128)(2,1)S(1)}, bf16[128,512]{1,0:T(8,128)(2,1)S(1)}, u32[]{:S(2)}, u32[]{:S(2)}) collective-permute-start(bf16[128,512]{1,0:T(8,128)(2,1)S(1)} %get-tuple-element.28), channel_id=1, source_target_pairs={{0,16},{16,32},{32,48},{48,64},{64,80},{80,96},{96,112},{112,0},{1... | collective-permute-start | bytes 393224 | tf_op jit(solution)/shard_map/ppermute | solution.py:609
  25.6 8.7 %collective-permute-start.5 = (bf16[128,512]{1,0:T(8,128)(2,1)S(1)}, bf16[128,512]{1,0:T(8,128)(2,1)S(1)}, u32[]{:S(2)}, u32[]{:S(2)}) collective-permute-start(bf16[128,512]{1,0:T(8,128)(2,1)S(1)} %get-tuple-element.29), channel_id=1, source_target_pairs={{16,0},{32,16},{48,32},{64,48},{80,64},{96,80},{112,96},{0,112},{1... | collective-permute-start | bytes 393224 | tf_op jit(solution)/shard_map/ppermute | solution.py:614
  49.2 42.1 %all-to-all-start = ((bf16[128,8,1152]{2,1,0:T(8,128)(2,1)}), bf16[128,8,1152]{2,1,0:T(8,128)(2,1)S(1)}, u32[]{:S(2)}, u32[]{:S(2)}) async-start(bf16[128,8,1152]{2,1,0:T(8,128)(2,1)} %bitcast.24), calls=%async_computation | async-start | bytes 4718592 | tf_op jit(solution)/shard_map/all_to_all | solution.py:645
  58.7 32.5 %copy-start.5 = (bf16[1,1,16,128,128]{4,3,2,1,0:T(8,128)(2,1)S(1)}, bf16[1,1,16,128,128]{4,3,2,1,0:T(8,128)(2,1)}, u32[]{:S(2)}) copy-start(bf16[1,1,16,128,128]{4,3,2,1,0:T(8,128)(2,1)} %param.22) | copy-start | bytes 1572868
  58.7 32.5 %copy-start.6 = (bf16[256,1024]{1,0:T(8,128)(2,1)S(1)}, bf16[256,1024]{1,0:T(8,128)(2,1)}, u32[]{:S(2)}) copy-start(bf16[256,1024]{1,0:T(8,128)(2,1)} %w1_ref.5) | copy-start | bytes 1572868
  58.7 32.5 %copy-start.9 = (f32[1024]{0:T(1024)S(1)}, f32[1024]{0:T(1024)}, u32[]{:S(2)}) copy-start(f32[1024]{0:T(1024)} %param.24) | copy-start | bytes 12292
